TPU v7x, 32 devices: a whole 2x2x4 slice. The times are simulated.
32 devices in a mesh: member: 4 (over y, core), dx: 4 (over z), dy: 2 (over x).
Axes of the slice: x: 2, y: 2, z: 4, core: 2. Of those that a mesh axis runs over, the one named last changes fastest.
Arguments:
- perturbed_states: float32 [4, 4, 8, 64, 256], P('member', None, None, 'dx', 'dy'), may hold values from -6 to 6
- control: float32 [4, 4, 8, 64, 256], P('member', None, None, 'dx', 'dy'), may hold values from -6 to 6
- owner: int32 [4], replicated, may hold values from 0 to 3, each once
- map_factor: float32 [64, 256], P('dx', 'dy'), may hold values from 0.5 to 2
- terrain: int32 [64, 256], P('dx', 'dy'), may hold values from 0 to 3
Outputs:
- forecast: float32 [4, 4, 8, 64, 256], P('member', None, None, 'dx', 'dy')
Inputs may be any that keep to these rules, and one draw needn't show every extreme that they name: `owner`: a permutation of the member indices.
All inputs are finite; a program needn't handle non-finite values.
Results may differ from a plain program's by a relative error of at most 0.0003.
Values sent between devices are 32-bit elements; how exact they have to be, the bound alone decides.
No kernel may reach another device: no remote copies, remote signals or barrier semaphores. Data moves between devices by JAX's collectives and lax.ppermute only.
A program may use at most 64 MiB of HBM per device.

v0:
```python
import jax
import jax.numpy as jnp
from jax import lax
from jax.sharding import PartitionSpec as P

STEPS = 4


integration_step = 0.2
diffusion = 0.1


def extended(value, sides, width):
    for axis, dim in sides:
        peers, length = (lax.axis_size(axis), value.shape[dim])
        up = [(i, (i + 1) % peers) for i in range(peers - 1)]
        down = [(j, i) for i, j in up]
        last = lax.slice_in_dim(value, length - width, length, axis=dim)
        first = lax.slice_in_dim(value, 0, width, axis=dim)
        before = lax.ppermute(last, axis, up)
        after = lax.ppermute(first, axis, down)
        value = jnp.concatenate([before, value, after], axis=dim)
    return value


def advance(padded, metric, vertical_level_mask):
    middle_point = padded[:, :, 1:-1, 1:-1]
    east = padded[:, :, 2:, 1:-1]
    west = padded[:, :, :-2, 1:-1]
    north = padded[:, :, 1:-1, 2:]
    south = padded[:, :, 1:-1, :-2]
    gradient_along_x = (east - west) * 0.5
    grad_y = (north - south) * 0.5
    stacked = jnp.pad(middle_point, ((0, 0), (1, 1), (0, 0), (0, 0)))
    laplace = east + west + north + south + stacked[:, 2:] + stacked[:, :-2] - 6.0 * middle_point
    wind_x = middle_point[0]
    meridional_velocity = middle_point[1]
    trend = (
        -metric * (wind_x * gradient_along_x + meridional_velocity * grad_y) + diffusion * laplace
    )
    extra = jnp.stack(
        [
            -metric * gradient_along_x[2],
            -metric * grad_y[2],
            -metric * (gradient_along_x[0] + grad_y[1]),
            jnp.zeros_like(wind_x),
        ]
    )
    return vertical_level_mask * (middle_point + integration_step * (trend + extra))


def own_weight(owner, members, here):
    ranks = lax.broadcasted_iota(jnp.int32, (members,), 0)
    per_rank = 2.0 * (members - ranks.astype(jnp.float32)) / (members * (members + 1.0))
    return jnp.sum(jnp.where(owner == here, per_rank, jnp.zeros_like(per_rank)))


def on_device(perturbed_states, control, owner, map_factor, terrain):
    levels_here = perturbed_states.shape[2]
    cols_x = perturbed_states.shape[3]
    column_count_y = perturbed_states.shape[4]
    members = lax.axis_size("member")
    levels = lax.broadcasted_iota(jnp.int32, (levels_here, cols_x, column_count_y), 0)
    vertical_level_mask = (levels >= terrain[None]).astype(jnp.float32)
    weighted = own_weight(owner, members, lax.axis_index("member")) * control[0]
    total, chosen = lax.psum((perturbed_states[0], weighted), "member")
    mean = total / members
    state = chosen + perturbed_states[0] - mean
    padded = extended(state, (("dx", 2), ("dy", 3)), STEPS)
    metric_all = jnp.concatenate([vertical_level_mask, map_factor[None]], axis=0)
    metric_extended = extended(metric_all, (("dx", 1), ("dy", 2)), STEPS)
    for number in range(STEPS):
        offset = number + 1
        width_x = cols_x + 2 * STEPS - 2 * offset
        meridional_extent = column_count_y + 2 * STEPS - 2 * offset
        window = metric_extended[:, offset : offset + width_x, offset : offset + meridional_extent]
        padded = advance(padded, window[levels_here], window[:levels_here])
    state = padded
    return state[None]


def solution(mesh):
    placed = (
        P("member", None, None, "dx", "dy"),
        P("member", None, None, "dx", "dy"),
        P(),
        P("dx", "dy"),
        P("dx", "dy"),
    )
    return jax.shard_map(
        on_device,
        mesh=mesh,
        in_specs=placed,
        out_specs=P("member", None, None, "dx", "dy"),
        check_vma=False,
    )
```

profile of v0, /device:TPU:0, one launch (start us, length us, event | category | flops | bytes accessed | tf_op | source)
XLA Modules:
  0.0 87.4 jit_solution(11314432513633406776)
XLA Ops:
  6.5 0.7 fusion.49
  7.3 1.3 %collective-permute-start.1 = (f32[9,4,128]{2,1,0:T(4,128)S(1)}, f32[9,4,128]{2,1,0:T(4,128)S(1)}, u32[]{:S(2)}, u32[]{:S(2)}) collective-permute-start(f32[9,4,128]{2,1,0:T(4,128)S(1)} %get-tuple-element.46), channel_id=1, source_target_pairs={{2,0},{4,2},{6,4},{3,1},{5,3},{7,5},{10,8},{12,10},{14,12},{11,9},... | collective-permute-start | bytes 55304 | tf_op jit(solution)/shard_map/ppermute | solution.py:21
  8.6 5.6 %collective-permute-start = (f32[9,4,128]{2,1,0:T(4,128)S(1)}, f32[9,4,128]{2,1,0:T(4,128)S(1)}, u32[]{:S(2)}, u32[]{:S(2)}) collective-permute-start(f32[9,4,128]{2,1,0:T(4,128)S(1)} %get-tuple-element.45), channel_id=1, source_target_pairs={{0,2},{2,4},{4,6},{1,3},{3,5},{5,7},{8,10},{10,12},{12,14},{9,11},... | collective-permute-start | bytes 55304 | tf_op jit(solution)/shard_map/ppermute | solution.py:20
  14.1 0.6 copy-done.2
  14.8 0.6 fusion.53
  15.4 2.2 %multiply_bitcast_fusion = f32[4,8,16,128]{3,2,1,0:T(8,128)} fusion(f32[1,4,8,16,128]{4,3,2,1,0:T(8,128)} %param.6, f32[]{:T(128)} %fusion.53), kind=kLoop, calls=%fused_computation.60 | loop fusion | flops 65536 | bytes 524292 | tf_op jit(solution)/shard_map/mul | solution.py:65
  17.8 1.3 %collective-permute-start.3 = (f32[9,24,4]{2,1,0:T(8,128)S(1)}, f32[9,24,4]{2,1,0:T(8,128)S(1)}, u32[]{:S(2)}, u32[]{:S(2)}) collective-permute-start(f32[9,24,4]{2,1,0:T(8,128)S(1)} %get-tuple-element.44), channel_id=1, source_target_pairs={{1,0},{3,2},{5,4},{7,6},{9,8},{11,10},{13,12},{15,14},{17,16},{19,... | collective-permute-start | bytes 10376 | tf_op jit(solution)/shard_map/ppermute | solution.py:21
  19.1 4.6 %collective-permute-start.2 = (f32[9,24,4]{2,1,0:T(8,128)S(1)}, f32[9,24,4]{2,1,0:T(8,128)S(1)}, u32[]{:S(2)}, u32[]{:S(2)}) collective-permute-start(f32[9,24,4]{2,1,0:T(8,128)S(1)} %get-tuple-element.43), channel_id=1, source_target_pairs={{0,1},{2,3},{4,5},{6,7},{8,9},{10,11},{12,13},{14,15},{16,17},{18,... | collective-permute-start | bytes 10376 | tf_op jit(solution)/shard_map/ppermute | solution.py:20
  23.8 0.7 collective-permute-done.3
  24.5 1.5 %collective-permute-done.2 = f32[9,24,4]{2,1,0:T(8,128)S(1)} collective-permute-done((f32[9,24,4]{2,1,0:T(8,128)S(1)}, f32[9,24,4]{2,1,0:T(8,128)S(1)}, u32[]{:S(2)}, u32[]{:S(2)}) %collective-permute-start.2) | collective-permute-done | bytes 3488 | tf_op jit(solution)/shard_map/ppermute | solution.py:20
  26.1 0.2 pad_maximum_fusion.2
  26.3 25.4 %all-reduce.7.cloned.1.call-done = (f32[4,8,16,128]{3,2,1,0:T(8,128)}, f32[4,8,16,128]{3,2,1,0:T(8,128)}) async-done(((f32[4,8,16,128]{3,2,1,0:T(8,128)}, f32[4,8,16,128]{3,2,1,0:T(8,128)}), (f32[4,8,16,128]{3,2,1,0:T(8,128)}, f32[4,8,16,128]{3,2,1,0:T(8,128)})) %all-reduce.7.cloned.1.call-update) | async-done | bytes 524304 | tf_op jit(solution)/shard_map/psum | solution.py:66
  51.7 1.1 %multiply_subtract_fusion = f32[4,8,16,128]{3,2,1,0:T(8,128)S(1)} fusion(f32[4,8,16,128]{3,2,1,0:T(8,128)} %get-tuple-element.5, f32[4,8,16,128]{3,2,1,0:T(8,128)} %get-tuple-element.6, f32[1,4,8,16,128]{4,3,2,1,0:T(8,128)S(1)} %copy-done), kind=kLoop, calls=%fused_computation.59 | loop fusion | flops 196608 | bytes 1048576 | tf_op jit(solution)/shard_map/sub | solution.py:68
  52.8 1.3 %collective-permute-start.5 = (f32[4,8,4,128]{3,2,1,0:T(4,128)S(1)}, f32[4,8,4,128]{3,2,1,0:T(4,128)S(1)}, u32[]{:S(2)}, u32[]{:S(2)}) collective-permute-start(f32[4,8,4,128]{3,2,1,0:T(4,128)S(1)} %get-tuple-element.42), channel_id=1, source_target_pairs={{2,0},{4,2},{6,4},{3,1},{5,3},{7,5},{10,8},{12,10},{14,12},{11,9},... | collective-permute-start | bytes 196616 | tf_op jit(solution)/shard_map/ppermute | solution.py:21
  54.1 4.5 %collective-permute-start.4 = (f32[4,8,4,128]{3,2,1,0:T(4,128)S(1)}, f32[4,8,4,128]{3,2,1,0:T(4,128)S(1)}, u32[]{:S(2)}, u32[]{:S(2)}) collective-permute-start(f32[4,8,4,128]{3,2,1,0:T(4,128)S(1)} %get-tuple-element.41), channel_id=1, source_target_pairs={{0,2},{2,4},{4,6},{1,3},{3,5},{5,7},{8,10},{10,12},{12,14},{9,11},... | collective-permute-start | bytes 196616 | tf_op jit(solution)/shard_map/ppermute | solution.py:20
  58.8 0.2 collective-permute-done.5
  59.0 1.6 %collective-permute-done.4 = f32[4,8,4,128]{3,2,1,0:T(4,128)S(1)} collective-permute-done((f32[4,8,4,128]{3,2,1,0:T(4,128)S(1)}, f32[4,8,4,128]{3,2,1,0:T(4,128)S(1)}, u32[]{:S(2)}, u32[]{:S(2)}) %collective-permute-start.4) | collective-permute-done | bytes 65568 | tf_op jit(solution)/shard_map/ppermute | solution.py:20
  60.6 0.2 fusion.54
  60.8 1.3 %collective-permute-start.7 = (f32[4,8,24,4]{3,2,1,0:T(8,128)S(1)}, f32[4,8,24,4]{3,2,1,0:T(8,128)S(1)}, u32[]{:S(2)}, u32[]{:S(2)}) collective-permute-start(f32[4,8,24,4]{3,2,1,0:T(8,128)S(1)} %get-tuple-element.37), channel_id=1, source_target_pairs={{1,0},{3,2},{5,4},{7,6},{9,8},{11,10},{13,12},{15,14},{17,16},{19,... | collective-permute-start | bytes 36872 | tf_op jit(solution)/shard_map/ppermute | solution.py:21
  62.1 4.6 %collective-permute-start.6 = (f32[4,8,24,4]{3,2,1,0:T(8,128)S(1)}, f32[4,8,24,4]{3,2,1,0:T(8,128)S(1)}, u32[]{:S(2)}, u32[]{:S(2)}) collective-permute-start(f32[4,8,24,4]{3,2,1,0:T(8,128)S(1)} %get-tuple-element.36), channel_id=1, source_target_pairs={{0,1},{2,3},{4,5},{6,7},{8,9},{10,11},{12,13},{14,15},{16,17},{18,... | collective-permute-start | bytes 36872 | tf_op jit(solution)/shard_map/ppermute | solution.py:20
  67.2 4.1 %collective-permute-done.7 = f32[4,8,24,4]{3,2,1,0:T(8,128)S(1)} collective-permute-done((f32[4,8,24,4]{3,2,1,0:T(8,128)S(1)}, f32[4,8,24,4]{3,2,1,0:T(8,128)S(1)}, u32[]{:S(2)}, u32[]{:S(2)}) %collective-permute-start.7) | collective-permute-done | bytes 12320 | tf_op jit(solution)/shard_map/ppermute | solution.py:21
  71.3 1.2 %collective-permute-done.6 = f32[4,8,24,4]{3,2,1,0:T(8,128)S(1)} collective-permute-done((f32[4,8,24,4]{3,2,1,0:T(8,128)S(1)}, f32[4,8,24,4]{3,2,1,0:T(8,128)S(1)}, u32[]{:S(2)}, u32[]{:S(2)}) %collective-permute-start.6) | collective-permute-done | bytes 12320 | tf_op jit(solution)/shard_map/ppermute | solution.py:20
  72.5 0.5 pad_maximum_fusion
  73.0 0.9 %broadcast_multiply_fusion.5 = (f32[4,8,22,134]{3,2,1,0:T(8,128)S(1)}, f32[4,8,22,134]{3,2,1,0:T(8,128)S(1)}, f32[4,8,22,134]{3,2,1,0:T(8,128)S(1)}) fusion(f32[4,8,24,136]{3,2,1,0:T(8,128)S(1)} %pad_maximum_fusion), kind=kLoop, calls=%fused_computation.46 | loop fusion | flops 377344 | bytes 3018752 | tf_op jit(solution)/shard_map/mul | solution.py:32
  73.9 0.2 fusion.45
  74.1 0.9 %fusion.8 = f32[4,8,22,134]{3,2,1,0:T(8,128)S(1)} fusion(f32[4,8,22,134]{3,2,1,0:T(8,128)S(1)} %get-tuple-element.35, f32[1,8,22,134]{3,2,1,0:T(8,128)S(1)} %get-tuple-element.14, f32[1,8,22,134]{3,2,1,0:T(8,128)S(1)} %get-tuple-element.15, f32[1,8,22,134]{3,2,1,0:T(8,128)S(1)} %get-tuple-element.13, f32[4,8,24,136]{3,2,1,0:T(8,128)S(1)} %pad_maximum_fusion, ...), kind=kLoop, calls=%fused_computation.14 | loop fusion | flops 2075392 | bytes 2841888 | tf_op jit(solution)/shard_map/mul | solution.py:49
  75.0 0.9 %broadcast_multiply_fusion.3 = (f32[4,8,20,132]{3,2,1,0:T(8,128)S(1)}, f32[4,8,20,132]{3,2,1,0:T(8,128)S(1)}, f32[4,8,20,132]{3,2,1,0:T(8,128)S(1)}) fusion(f32[4,8,22,134]{3,2,1,0:T(8,128)S(1)} %fusion.8), kind=kLoop, calls=%fused_computation.44 | loop fusion | flops 337920 | bytes 2703360 | tf_op jit(solution)/shard_map/mul | solution.py:32
  76.1 0.9 %fusion.17 = f32[4,8,20,132]{3,2,1,0:T(8,128)S(1)} fusion(f32[4,8,20,132]{3,2,1,0:T(8,128)S(1)} %get-tuple-element.30, f32[1,8,20,132]{3,2,1,0:T(8,128)S(1)} %get-tuple-element.11, f32[1,8,20,132]{3,2,1,0:T(8,128)S(1)} %get-tuple-element.12, f32[1,8,20,132]{3,2,1,0:T(8,128)S(1)} %get-tuple-element.10, f32[4,8,22,134]{3,2,1,0:T(8,128)S(1)} %fusion.8, ...), kind=kLoop, calls=%fused_computation.23 | loop fusion | flops 1858560 | bytes 2544976 | tf_op jit(solution)/shard_map/mul | solution.py:49
  77.0 0.9 %broadcast_multiply_fusion.1 = (f32[4,8,18,130]{3,2,1,0:T(8,128)S(1)}, f32[4,8,18,130]{3,2,1,0:T(8,128)S(1)}, f32[4,8,18,130]{3,2,1,0:T(8,128)S(1)}) fusion(f32[4,8,20,132]{3,2,1,0:T(8,128)S(1)} %fusion.17), kind=kLoop, calls=%fused_computation.42 | loop fusion | flops 299520 | bytes 2396160 | tf_op jit(solution)/shard_map/mul | solution.py:32
  78.1 0.9 %fusion.26 = f32[4,8,18,130]{3,2,1,0:T(8,128)S(1)} fusion(f32[4,8,18,130]{3,2,1,0:T(8,128)S(1)} %get-tuple-element.25, f32[1,8,18,130]{3,2,1,0:T(8,128)S(1)} %get-tuple-element.8, f32[1,8,18,130]{3,2,1,0:T(8,128)S(1)} %get-tuple-element.9, f32[1,8,18,130]{3,2,1,0:T(8,128)S(1)} %get-tuple-element.7, f32[4,8,20,132]{3,2,1,0:T(8,128)S(1)} %fusion.17, ...), kind=kLoop, calls=%fused_computation.32 | loop fusion | flops 1647360 | bytes 2255776 | tf_op jit(solution)/shard_map/mul | solution.py:49
  79.0 0.3 broadcast_multiply_fusion.7
  79.5 1.1 %fusion.36 = f32[1,4,8,16,128]{4,3,2,1,0:T(8,128)} fusion(f32[4,8,16,128]{3,2,1,0:T(8,128)S(1)} %get-tuple-element.20, f32[1,8,16,128]{3,2,1,0:T(8,128)S(1)} %get-tuple-element.39, f32[1,8,16,128]{3,2,1,0:T(8,128)S(1)} %get-tuple-element.40, f32[1,8,16,128]{3,2,1,0:T(8,128)S(1)} %get-tuple-element.38, f32[4,8,18,130]{3,2,1,0:T(8,128)S(1)} %fusion.26, ...), kind=kLoop, calls=%fused_computation.58 | loop fusion | flops 1441792 | bytes 1974288 | tf_op jit(solution)/shard_map/broadcast_in_dim | solution.py:79
  (29 shorter events, 1.5 us)
Async XLA Ops:
  6.5 0.7 copy-start.1
  6.5 45.2 %all-reduce.7.cloned.1.call-start = ((), (), s32[]{:S(2)}) async-start(), calls=%async_computation | async-start | bytes 1048576 | tf_op jit(solution)/shard_map/psum | solution.py:66
  7.3 10.4 %collective-permute-start.1 = (f32[9,4,128]{2,1,0:T(4,128)S(1)}, f32[9,4,128]{2,1,0:T(4,128)S(1)}, u32[]{:S(2)}, u32[]{:S(2)}) collective-permute-start(f32[9,4,128]{2,1,0:T(4,128)S(1)} %get-tuple-element.46), channel_id=1, source_target_pairs={{2,0},{4,2},{6,4},{3,1},{5,3},{7,5},{10,8},{12,10},{14,12},{11,9},... | collective-permute-start | bytes 55304 | tf_op jit(solution)/shard_map/ppermute | solution.py:21
  8.6 9.1 %collective-permute-start = (f32[9,4,128]{2,1,0:T(4,128)S(1)}, f32[9,4,128]{2,1,0:T(4,128)S(1)}, u32[]{:S(2)}, u32[]{:S(2)}) collective-permute-start(f32[9,4,128]{2,1,0:T(4,128)S(1)} %get-tuple-element.45), channel_id=1, source_target_pairs={{0,2},{2,4},{4,6},{1,3},{3,5},{5,7},{8,10},{10,12},{12,14},{9,11},... | collective-permute-start | bytes 55304 | tf_op jit(solution)/shard_map/ppermute | solution.py:20
  14.1 0.7 copy-start.2
  17.8 6.6 %collective-permute-start.3 = (f32[9,24,4]{2,1,0:T(8,128)S(1)}, f32[9,24,4]{2,1,0:T(8,128)S(1)}, u32[]{:S(2)}, u32[]{:S(2)}) collective-permute-start(f32[9,24,4]{2,1,0:T(8,128)S(1)} %get-tuple-element.44), channel_id=1, source_target_pairs={{1,0},{3,2},{5,4},{7,6},{9,8},{11,10},{13,12},{15,14},{17,16},{19,... | collective-permute-start | bytes 10376 | tf_op jit(solution)/shard_map/ppermute | solution.py:21
  19.1 6.9 %collective-permute-start.2 = (f32[9,24,4]{2,1,0:T(8,128)S(1)}, f32[9,24,4]{2,1,0:T(8,128)S(1)}, u32[]{:S(2)}, u32[]{:S(2)}) collective-permute-start(f32[9,24,4]{2,1,0:T(8,128)S(1)} %get-tuple-element.43), channel_id=1, source_target_pairs={{0,1},{2,3},{4,5},{6,7},{8,9},{10,11},{12,13},{14,15},{16,17},{18,... | collective-permute-start | bytes 10376 | tf_op jit(solution)/shard_map/ppermute | solution.py:20
  26.1 25.6 %copy-start = (f32[1,4,8,16,128]{4,3,2,1,0:T(8,128)S(1)}, f32[1,4,8,16,128]{4,3,2,1,0:T(8,128)}, u32[]{:S(2)}) copy-start(f32[1,4,8,16,128]{4,3,2,1,0:T(8,128)} %param.5) | copy-start | bytes 786436
  52.8 6.2 %collective-permute-start.5 = (f32[4,8,4,128]{3,2,1,0:T(4,128)S(1)}, f32[4,8,4,128]{3,2,1,0:T(4,128)S(1)}, u32[]{:S(2)}, u32[]{:S(2)}) collective-permute-start(f32[4,8,4,128]{3,2,1,0:T(4,128)S(1)} %get-tuple-element.42), channel_id=1, source_target_pairs={{2,0},{4,2},{6,4},{3,1},{5,3},{7,5},{10,8},{12,10},{14,12},{11,9},... | collective-permute-start | bytes 196616 | tf_op jit(solution)/shard_map/ppermute | solution.py:21
  54.1 6.4 %collective-permute-start.4 = (f32[4,8,4,128]{3,2,1,0:T(4,128)S(1)}, f32[4,8,4,128]{3,2,1,0:T(4,128)S(1)}, u32[]{:S(2)}, u32[]{:S(2)}) collective-permute-start(f32[4,8,4,128]{3,2,1,0:T(4,128)S(1)} %get-tuple-element.41), channel_id=1, source_target_pairs={{0,2},{2,4},{4,6},{1,3},{3,5},{5,7},{8,10},{10,12},{12,14},{9,11},... | collective-permute-start | bytes 196616 | tf_op jit(solution)/shard_map/ppermute | solution.py:20
  60.8 10.5 %collective-permute-start.7 = (f32[4,8,24,4]{3,2,1,0:T(8,128)S(1)}, f32[4,8,24,4]{3,2,1,0:T(8,128)S(1)}, u32[]{:S(2)}, u32[]{:S(2)}) collective-permute-start(f32[4,8,24,4]{3,2,1,0:T(8,128)S(1)} %get-tuple-element.37), channel_id=1, source_target_pairs={{1,0},{3,2},{5,4},{7,6},{9,8},{11,10},{13,12},{15,14},{17,16},{19,... | collective-permute-start | bytes 36872 | tf_op jit(solution)/shard_map/ppermute | solution.py:21
  62.1 10.4 %collective-permute-start.6 = (f32[4,8,24,4]{3,2,1,0:T(8,128)S(1)}, f32[4,8,24,4]{3,2,1,0:T(8,128)S(1)}, u32[]{:S(2)}, u32[]{:S(2)}) collective-permute-start(f32[4,8,24,4]{3,2,1,0:T(8,128)S(1)} %get-tuple-element.36), channel_id=1, source_target_pairs={{0,1},{2,3},{4,5},{6,7},{8,9},{10,11},{12,13},{14,15},{16,17},{18,... | collective-permute-start | bytes 36872 | tf_op jit(solution)/shard_map/ppermute | solution.py:20
Sparse Core Ops, SparseCore 0:
  17.8 33.8 all-reduce.6
where the time goes:
time: 88.1 us; the launch traced here: 87.4 us
  waiting for transfers between devices  34.7 us (39%)
  starting transfers between devices  24.4 us (28%)
  between operations  13.7 us (16%)
  other arithmetic  13.2 us (15%)
  local copies, waits for them, and re-layouts  1.37 us (2%)
    psum x1, waiting for transfers between devices, on_device(): total, chosen = lax.psum((perturbed_states[0], weighted), 'member')  25.4 us
    ppermute x4, starting transfers between devices, extended(): before = lax.ppermute(last, axis, up)  19.3 us
    ppermute x4, starting transfers between devices, extended(): after = lax.ppermute(first, axis, down)  5.17 us
    ppermute x4, waiting for transfers between devices, extended(): after = lax.ppermute(first, axis, down)  5 us
    ppermute x4, waiting for transfers between devices, extended(): before = lax.ppermute(last, axis, up)  4.31 us
    mul x4, other arithmetic, advance(): gradient_along_x = (east - west) * 0.5  2.98 us
    mul x3, other arithmetic, advance(): vertical_level_mask * (middle_point + integration_step * (trend + extra))  2.65 us
    mul x1, other arithmetic, on_device(): weighted = own_weight(owner, members, lax.axis_index('member')) * control[0]  2.24 us
  transfers between devices with their start and end apart: 9, of which 7 were waited for; matrix products, arithmetic and copies ran while one was open for 4% of the time, Pallas kernels for 0%

commit v1 on v0

v1 whole, which is shorter than its diff:
```python
import functools

import jax
import jax.numpy as jnp
from jax import lax
from jax.experimental import pallas as pl
from jax.experimental.pallas import tpu as pltpu
from jax.sharding import PartitionSpec as P

STEPS = 4

integration_step = 0.2
diffusion = 0.1

OUTSIDE = 1.0e6
AXES = ("member", "dx", "dy")
VMEM = pl.BlockSpec(memory_space=pltpu.VMEM)
SMEM = pl.BlockSpec(memory_space=pltpu.SMEM)


def send(value, target):
    sizes = [lax.axis_size(axis) for axis in AXES]
    pairs = []
    for member in range(sizes[0]):
        for i in range(sizes[1]):
            for j in range(sizes[2]):
                k, l, m = target(member, i, j)
                pairs.append(
                    (
                        (member * sizes[1] + i) * sizes[2] + j,
                        (k * sizes[1] + l) * sizes[2] + m,
                    )
                )
    return lax.ppermute(value, AXES, pairs)


def loop_target(rows, forward):
    def target(member, i, j):
        step = 1 if (member % 2 == 0) == forward else -1
        if 0 <= i + step < rows:
            return member, i + step, j
        return member ^ 1, i, j

    return target


def lanes_of(shape):
    return lax.broadcasted_iota(jnp.int32, shape, len(shape) - 1)


def turn(tile, by, axis=1):
    return pltpu.roll(tile, by % tile.shape[axis], axis)


def edges_of(tiles, width):
    lane = lanes_of(tiles[0].shape)
    total = None
    for x, tile in enumerate(tiles):
        moved = turn(tile, 2 * width * x + width)
        total = moved if total is None else jnp.where(lane < 2 * width * x, total, moved)
    return total


def split_kernel(p_ref, c_ref, owner_ref, m_ref, t_ref, pt_ref, keep_ref, send_ref, more_ref):
    fields, _, cols = p_ref.shape
    rows = m_ref.shape[0]
    levels = p_ref.shape[1] // rows
    half = rows // 2
    member = lax.axis_index("member")
    members = owner_ref.shape[0]
    first = lax.rem(member, 2) == 0
    weight = jnp.float32(0.0)
    for rank in range(members):
        per_rank = 2.0 * (members - rank) / (members * (members + 1.0))
        weight = weight + jnp.where(owner_ref[rank] == member, per_rank, 0.0)
    for f in range(fields):
        states, parts = [], []
        for x in range(rows):
            state = p_ref[f, pl.ds(x, levels, stride=rows), :]
            analysis = c_ref[f, pl.ds(x, levels, stride=rows), :]
            pt_ref[x * fields + f] = state
            states.append(state)
            parts.append(weight * analysis - state * (1.0 / members))
        for x in range(half):
            keep_ref[x * fields + f] = jnp.where(first, parts[x], parts[x + half])
            send_ref[x * fields + f] = jnp.where(first, parts[x + half], parts[x])
        send_ref[half * fields + f] = edges_of(parts, STEPS)
        more_ref[f] = edges_of(states, STEPS)
    level = lax.broadcasted_iota(jnp.int32, (levels, cols), 0)
    columns = []
    for x in range(rows):
        scale = jnp.broadcast_to(m_ref[pl.ds(x, 1), :], (levels, cols))
        ground = jnp.broadcast_to(t_ref[pl.ds(x, 1), :].astype(jnp.float32), (levels, cols))
        columns.append(jnp.where(level == 0, scale, ground))
    more_ref[fields] = edges_of(columns, STEPS)


def join_kernel(
    sizes, n_left, pt_ref, mine_ref, other_ref, m_ref, t_ref, more_ref, *refs
):
    left, rest = refs[:n_left], refs[n_left:]
    right, rest = rest[:n_left], rest[n_left:]
    start_ref, strip_ref, first_ref, second_ref = rest
    rows, cols = m_ref.shape
    levels = pt_ref.shape[1]
    fields = pt_ref.shape[0] // rows
    half, wide = rows // 2, STEPS
    parity = lax.rem(lax.axis_index("member"), 2)
    place = lax.axis_index("dy")
    has_left, has_right = place > 0, place < sizes[2] - 1
    for r in range(half):
        for f in range(fields):
            near = (parity * half + r) * fields + f
            far = ((1 - parity) * half + r) * fields + f
            start_ref[near] = pt_ref[near] + mine_ref[r * fields + f]
            start_ref[far] = pt_ref[far] + other_ref[r * fields + f]
    lane = lanes_of((levels, cols))
    early = lax.rem(lane, 2 * wide) < wide
    quarter = 2 * wide * wide

    def strips(own, before, after):
        a = jnp.where(early, before, own)
        b = jnp.where(early, own, after)
        ends = jnp.where(
            lane < quarter,
            a,
            jnp.where(
                lane < 2 * quarter,
                turn(b, quarter),
                jnp.where(lane < cols - quarter, turn(b, -quarter), a),
            ),
        )
        return a, b, ends

    def beside(parts, f):
        total = parts[0][fields + f] + parts[0][f]
        for part in parts[1:]:
            total = total + part[f]
        return total

    ends = []
    for f in range(fields):
        own = edges_of([start_ref[x * fields + f] for x in range(rows)], wide)
        before = jnp.where(has_left, beside(left, f), 0.0)
        after = jnp.where(has_right, beside(right, f), 0.0)
        a, b, end = strips(own, before, after)
        strip_ref[f] = a
        strip_ref[fields + 1 + f] = b
        ends.append(end)
    a, b, end = strips(
        more_ref[fields],
        jnp.where(has_left, left[0][2 * fields], OUTSIDE),
        jnp.where(has_right, right[0][2 * fields], OUTSIDE),
    )
    strip_ref[fields] = a
    strip_ref[2 * fields + 1] = b
    ends.append(end)
    scale, ground = m_ref[...], t_ref[...].astype(jnp.float32)
    tops = jnp.concatenate([scale[rows - wide :], ground[rows - wide :]], axis=0)
    bottoms = jnp.concatenate([scale[:wide], ground[:wide]], axis=0)
    for message, up in ((first_ref, parity == 0), (second_ref, parity == 1)):
        base = jnp.where(up, rows - wide, 0) * fields
        for k in range(wide * fields):
            message[k] = start_ref[base + k]
        for k, end in enumerate(ends):
            message[wide * fields + k] = end
        message[wide * fields + fields + 1] = jnp.where(up, tops, bottoms)


def forecast_kernel(
    sizes, start_ref, strip_ref, m_ref, t_ref, first_ref, second_ref, out_ref, a_ref, b_ref, coef_ref
):
    rows, cols = m_ref.shape
    levels = start_ref.shape[1]
    fields = start_ref.shape[0] // rows
    wide = STEPS
    group = 2 * wide
    tall = rows + 2 * wide
    parity = lax.rem(lax.axis_index("member"), 2)
    place = lax.axis_index("dx")
    has_low, has_high = place > 0, place < sizes[1] - 1
    lane = lanes_of((levels, cols))
    level = lax.broadcasted_iota(jnp.int32, (levels, cols), 0)
    quarter = group * wide
    even = parity == 0

    def low(k):
        return jnp.where(even, first_ref[k], second_ref[k])

    def high(k):
        return jnp.where(even, second_ref[k], first_ref[k])

    def coefficients(scale, ground):
        mask = (level.astype(jnp.float32) >= ground).astype(jnp.float32)
        return (
            mask * (1.0 - 6.0 * integration_step * diffusion),
            mask * (integration_step * diffusion),
            mask * (scale * (0.5 * integration_step)),
        )

    def wide_row(row):
        return jnp.broadcast_to(row, (levels, cols))

    for k in range(wide * fields):
        a_ref[k] = jnp.where(has_low, low(k), 0.0)
        a_ref[(rows + wide) * fields + k] = jnp.where(has_high, high(k), 0.0)
    for k in range(rows * fields):
        a_ref[wide * fields + k] = start_ref[k]
    metric = wide * fields + fields + 1
    below, above = low(metric), high(metric)
    below = jnp.where(has_low, below, OUTSIDE)
    above = jnp.where(has_high, above, OUTSIDE)
    for x in range(tall):
        if x < wide:
            scale, ground = below[x : x + 1], below[wide + x : wide + x + 1]
        elif x < wide + rows:
            scale = m_ref[pl.ds(x - wide, 1), :]
            ground = t_ref[pl.ds(x - wide, 1), :].astype(jnp.float32)
        else:
            r = x - wide - rows
            scale, ground = above[r : r + 1], above[wide + r : wide + r + 1]
        for k, value in enumerate(coefficients(wide_row(scale), wide_row(ground))):
            coef_ref[3 * x + k] = value

    def stretched(k, empty):
        mine_a = turn(strip_ref[k], quarter)
        mine_b = turn(strip_ref[fields + 1 + k], quarter)
        under, over = low(wide * fields + k), high(wide * fields + k)
        under = jnp.where(has_low, under, empty)
        over = jnp.where(has_high, over, empty)
        blank = jnp.full((levels, cols), empty, jnp.float32)

        def end(own, other):
            return jnp.where(
                lane < quarter, own, jnp.where(lane < 2 * quarter, other, blank)
            )

        return (
            (
                jnp.where(lane < quarter, turn(under, quarter), mine_a),
                end(mine_a, turn(over, quarter)),
            ),
            (
                jnp.where(lane < quarter, turn(under, 2 * quarter), mine_b),
                end(mine_b, over),
            ),
        )

    strips = [stretched(f, 0.0) for f in range(fields)]
    strip_coefs = [
        [coefficients(wide_row(tile[0:1]), wide_row(tile[1:2])) for tile in side]
        for side in stretched(fields, OUTSIDE)
    ]

    def updated(coefs, cur, dx, sx, dy, sy):
        new = []
        for f in range(fields):
            advected = cur[0] * dx[f] + cur[1] * dy[f]
            if f == 0:
                advected = advected + dx[2]
            elif f == 1:
                advected = advected + dy[2]
            elif f == 2:
                advected = advected + (dx[0] + dy[1])
            upper = jnp.where(level < levels - 1, turn(cur[f], -1, 0), 0.0)
            lower = jnp.where(level > 0, turn(cur[f], 1, 0), 0.0)
            total = (sx[f] + sy[f]) + (upper + lower)
            new.append(coefs[0] * cur[f] + coefs[1] * total - coefs[2] * advected)
        return new

    def strip_step(tiles):
        new = [[[None, None], [None, None]] for _ in range(fields)]
        for side in range(2):
            for v in range(2):
                cur, dx, sx, dy, sy = [], [], [], [], []
                for f in range(fields):
                    one, two = tiles[f][side]
                    if v == 0:
                        east = jnp.where(lane < cols - group, turn(one, -group), turn(two, -group))
                        west = turn(one, group)
                    else:
                        east = turn(two, -group)
                        west = jnp.where(lane < group, turn(one, group), turn(two, group))
                    here = (one, two)[v]
                    north, south = turn(here, -1), turn(here, 1)
                    cur.append(here)
                    dx.append(east - west)
                    sx.append(east + west)
                    dy.append(north - south)
                    sy.append(north + south)
                result = updated(strip_coefs[side][v], cur, dx, sx, dy, sy)
                for f in range(fields):
                    new[f][side][v] = result[f]
        return new

    for number in range(STEPS):
        source = a_ref if number % 2 == 0 else b_ref
        sink = b_ref if number % 2 == 0 else a_ref
        beyond = [
            [
                jnp.where(lax.rem(lane, group) == wide - 1, a, turn(b, -2))
                for a, b in zip(strips[f][0], strips[f][1])
            ]
            for f in range(fields)
        ]
        bottom, top = number + 1, tall - number - 1
        rows_at = lambda x: [source[x * fields + f] for f in range(fields)]
        before, cur = rows_at(bottom - 1), rows_at(bottom)
        for x in range(bottom, top):
            after = rows_at(x + 1)
            dx, sx, dy, sy = [], [], [], []
            for f in range(fields):
                spot = group * x + wide - 1
                outer = turn(beyond[f][spot // cols], -(spot % cols))
                north = jnp.where(lane == cols - 1, outer, turn(cur[f], -1))
                south = jnp.where(lane == 0, outer, turn(cur[f], 1))
                dx.append(after[f] - before[f])
                sx.append(after[f] + before[f])
                dy.append(north - south)
                sy.append(north + south)
            coefs = [coef_ref[3 * x + k] for k in range(3)]
            new = updated(coefs, cur, dx, sx, dy, sy)
            for f in range(fields):
                if number == STEPS - 1:
                    out_ref[f, pl.ds(x - wide, levels, stride=rows), :] = new[f]
                else:
                    sink[x * fields + f] = new[f]
            before, cur = cur, after
        if number < STEPS - 1:
            strips = strip_step(strips)


def on_device(perturbed_states, control, owner, map_factor, terrain):
    _, fields, levels, rows, cols = perturbed_states.shape
    sizes = tuple(lax.axis_size(axis) for axis in AXES)
    members = sizes[0]
    half = rows // 2
    tile = (levels, cols)

    def tiles(count):
        return jax.ShapeDtypeStruct((count, *tile), jnp.float32)

    flat = (fields, levels * rows, cols)
    states, keep, give, more = pl.pallas_call(
        split_kernel,
        out_shape=(
            tiles(rows * fields),
            tiles(half * fields),
            tiles(half * fields + fields),
            tiles(fields + 1),
        ),
        in_specs=[VMEM, VMEM, SMEM, VMEM, VMEM],
        out_specs=(VMEM,) * 4,
        name="split",
    )(perturbed_states.reshape(flat), control.reshape(flat), owner, map_factor, terrain)

    given = send(give, lambda k, i, j: (k ^ 1, i, j))
    total = keep + given[: half * fields]
    edges = give[half * fields :] + given[half * fields :]

    chips = [b for b in range(2, members, 2)]
    bit = 2
    got = []
    while bit < members:
        got.append(send(total, lambda k, i, j, bit=bit: (k ^ bit, i, j)))
        total = total + got[-1]
        bit *= 2
    along = sizes[2]

    def from_side(step):
        there = lambda b: lambda k, i, j: (k ^ b, i, (j + step) % along)
        near = send(jnp.concatenate([edges, more], axis=0), there(0))
        return [near] + [send(edges, there(b)) for b in chips]

    left = from_side(1)
    right = left if along == 2 else from_side(-1)

    other = send(total, lambda k, i, j: (k ^ 1, i, j))
    count = STEPS * fields + fields + 2
    start, strips, first, second = pl.pallas_call(
        functools.partial(join_kernel, sizes, len(left)),
        out_shape=(tiles(rows * fields), tiles(2 * (fields + 1)), tiles(count), tiles(count)),
        in_specs=[VMEM] * (6 + 2 * len(left)),
        out_specs=(VMEM,) * 4,
        name="join",
    )(states, total, other, map_factor, terrain, more, *left, *right)
    first = send(first, loop_target(sizes[1], True))
    second = send(second, loop_target(sizes[1], False))
    out = pl.pallas_call(
        functools.partial(forecast_kernel, sizes),
        out_shape=jax.ShapeDtypeStruct(flat, jnp.float32),
        in_specs=[VMEM] * 6,
        out_specs=VMEM,
        scratch_shapes=[
            pltpu.VMEM(((rows + 2 * STEPS) * fields, *tile), jnp.float32),
            pltpu.VMEM(((rows + 2 * STEPS) * fields, *tile), jnp.float32),
            pltpu.VMEM(((rows + 2 * STEPS) * 3, *tile), jnp.float32),
        ],
        name="forecast",
    )(start, strips, map_factor, terrain, first, second)
    return out.reshape(perturbed_states.shape)


def solution(mesh):
    placed = (
        P("member", None, None, "dx", "dy"),
        P("member", None, None, "dx", "dy"),
        P(),
        P("dx", "dy"),
        P("dx", "dy"),
    )
    return jax.shard_map(
        on_device,
        mesh=mesh,
        in_specs=placed,
        out_specs=P("member", None, None, "dx", "dy"),
        check_vma=False,
    )
```

time: 88.1 us -> 31.4 us (0.36)
  waiting for transfers between devices: 34.7 us -> 12.2 us
  starting transfers between devices: 24.4 us -> 8.31 us
  between operations: 13.7 us -> 0.07 us
  other arithmetic: 13.2 us -> 1.66 us
  Pallas kernels: 0 us -> 7.62 us
    psum x1 -> x0, waiting for transfers between devices: 25.4 us -> none  [on_device(): total, chosen = lax.psum((perturbed_states[0], weighted), 'member')]
    ppermute x8 -> x7, starting transfers between devices: 24.4 us -> 8.31 us  [send(): return lax.ppermute(value, AXES, pairs)]
    mul x16 -> x0, other arithmetic: 8.68 us -> none  [the longest x4 2.98 us: advance(): gradient_along_x = (east - west) * 0.5]
    pallas_call x0 -> x3, Pallas kernels: none -> 7.62 us  [the longest x1 3.56 us: on_device(): pl.pallas_call(functools.partial(forecast_kernel, sizes), out_shape=jax.S...]
    ppermute x8 -> x7, waiting for transfers between devices: 9.31 us -> 12.2 us  [send(): return lax.ppermute(value, AXES, pairs)]
    add x0 -> x3, other arithmetic: none -> 1.66 us  [the longest x1 0.92 us: on_device(): total = keep + given[:half * fields]]
    sub x1 -> x0, other arithmetic: 1.08 us -> none  [on_device(): state = chosen + perturbed_states[0] - mean]
    broadcast_in_dim x1 -> x0, other arithmetic: 1.06 us -> none  [on_device(): return state[None]]
  transfers between devices with their start and end apart: 9 -> 7, of which waited for: 7 -> 5; matrix products, arithmetic and copies ran while one was open for 4% -> 2% of each run, Pallas kernels for 0% -> 0%
where the time goes in v1:
time: 31.4 us; the launch traced here: 31.2 us
  waiting for transfers between devices  12.2 us (39%)
  starting transfers between devices  8.31 us (26%)
  Pallas kernels  7.62 us (24%)
  other arithmetic  1.66 us (5%)
  local copies, waits for them, and re-layouts  1.3 us (4%)
    ppermute x7, waiting for transfers between devices, send(): return lax.ppermute(value, AXES, pairs)  12.2 us
    ppermute x7, starting transfers between devices, send(): return lax.ppermute(value, AXES, pairs)  8.31 us
    pallas_call x1, Pallas kernels, on_device(): pl.pallas_call(functools.partial(forecast_kernel, sizes), out_shape=jax.S...  3.56 us
    pallas_call x1, Pallas kernels, on_device(): pl.pallas_call(functools.partial(join_kernel, sizes, len(left)), out_shap...  2.06 us
    pallas_call x1, Pallas kernels, on_device(): pl.pallas_call(split_kernel, out_shape=(tiles(rows * fields), tiles(half...  2 us
    unnamed x14, local copies, waits for them, and re-layouts  1.3 us
    add x1, other arithmetic, on_device(): total = keep + given[:half * fields]  0.92 us
    add x1, other arithmetic, on_device(): edges = give[half * fields:] + given[half * fields:]  0.72 us
  transfers between devices with their start and end apart: 7, of which 5 were waited for; matrix products, arithmetic and copies ran while one was open for 2% of the time, Pallas kernels for 0%

profile of v1, /device:TPU:0, one launch (start us, length us, event | category | flops | bytes accessed | tf_op | source)
XLA Modules:
  0.0 31.2 jit_solution(9786520014270640404)
XLA Ops:
  0.0 2.0 %split.1 = (f32[64,8,128]{2,1,0:T(8,128)}, f32[32,8,128]{2,1,0:T(8,128)}, f32[36,8,128]{2,1,0:T(8,128)}, f32[5,8,128]{2,1,0:T(8,128)}) custom-call(f32[4,128,128]{2,1,0:T(8,128)} %bitcast.3, f32[4,128,128]{2,1,0:T(8,128)} %bitcast.4, s32[4]{0:T(128)} %owner_ref.1, f32[16,128]{1,0:T(8,128)} %m_ref.5, s32[16,128]{1,0:T(8,128)} %t_ref.5), custom_call_target="tpu_custom_call" | custom-call | tf_op jit(solution)/shard_map/split/pallas_call | solution.py:344
  2.0 0.5 %collective-permute-start = (f32[36,8,128]{2,1,0:T(8,128)}, f32[36,8,128]{2,1,0:T(8,128)S(1)}, u32[]{:S(2)}, u32[]{:S(2)}) collective-permute-start(f32[36,8,128]{2,1,0:T(8,128)} %get-tuple-element.15), channel_id=1, source_target_pairs={{0,8},{1,9},{2,10},{3,11},{4,12},{5,13},{6,14},{7,15},{8,0},{9,1},... | collective-permute-start | bytes 442376 | tf_op jit(solution)/shard_map/ppermute | solution.py:34
  2.5 1.2 %collective-permute-done = f32[36,8,128]{2,1,0:T(8,128)S(1)} collective-permute-done((f32[36,8,128]{2,1,0:T(8,128)}, f32[36,8,128]{2,1,0:T(8,128)S(1)}, u32[]{:S(2)}, u32[]{:S(2)}) %collective-permute-start) | collective-permute-done | bytes 147488 | tf_op jit(solution)/shard_map/ppermute | solution.py:34
  3.7 0.9 %slice_add_fusion = f32[32,8,128]{2,1,0:T(8,128)S(1)} fusion(f32[32,8,128]{2,1,0:T(8,128)} %get-tuple-element.14, f32[36,8,128]{2,1,0:T(8,128)S(1)} %collective-permute-done), kind=kLoop, calls=%fused_computation | loop fusion | flops 32768 | bytes 393216 | tf_op jit(solution)/shard_map/add | solution.py:358
  4.6 2.9 %collective-permute-start.1 = (f32[32,8,128]{2,1,0:T(8,128)S(1)}, f32[32,8,128]{2,1,0:T(8,128)S(1)}, u32[]{:S(2)}, u32[]{:S(2)}) collective-permute-start(f32[32,8,128]{2,1,0:T(8,128)S(1)} %slice_add_fusion), channel_id=1, source_target_pairs={{0,16},{1,17},{2,18},{3,19},{4,20},{5,21},{6,22},{7,23},{8,24},{9,... | collective-permute-start | bytes 393224 | tf_op jit(solution)/shard_map/ppermute | solution.py:34
  7.5 0.7 %slice_add_fusion.1 = f32[4,8,128]{2,1,0:T(8,128)S(1)} fusion(f32[36,8,128]{2,1,0:T(8,128)S(1)} %collective-permute-done, f32[36,8,128]{2,1,0:T(8,128)} %get-tuple-element.15), kind=kLoop, calls=%fused_computation.2 | loop fusion | flops 4096 | bytes 49152 | tf_op jit(solution)/shard_map/add | solution.py:359
  8.3 0.0 copy-start.5
  8.3 3.1 %collective-permute-done.1 = f32[32,8,128]{2,1,0:T(8,128)S(1)} collective-permute-done((f32[32,8,128]{2,1,0:T(8,128)S(1)}, f32[32,8,128]{2,1,0:T(8,128)S(1)}, u32[]{:S(2)}, u32[]{:S(2)}) %collective-permute-start.1) | collective-permute-done | bytes 131104 | tf_op jit(solution)/shard_map/ppermute | solution.py:34
  11.4 0.0 copy-start
  11.4 0.1 collective-permute-start.2
  11.5 0.0 copy-done.5
  11.5 1.8 %collective-permute-start.3 = (f32[9,8,128]{2,1,0:T(8,128)S(1)}, f32[9,8,128]{2,1,0:T(8,128)S(1)}, u32[]{:S(2)}, u32[]{:S(2)}) collective-permute-start(f32[9,8,128]{2,1,0:T(8,128)S(1)} %pad_maximum_fusion), channel_id=1, source_target_pairs={{0,1},{1,0},{2,3},{3,2},{4,5},{5,4},{6,7},{7,6},{8,9},{9,8},{10,11... | collective-permute-start | bytes 110600 | tf_op jit(solution)/shard_map/ppermute | solution.py:34
  13.3 1.5 %collective-permute-start.4 = (f32[4,8,128]{2,1,0:T(8,128)S(1)}, f32[4,8,128]{2,1,0:T(8,128)S(1)}, u32[]{:S(2)}, u32[]{:S(2)}) collective-permute-start(f32[4,8,128]{2,1,0:T(8,128)S(1)} %slice_add_fusion.1), channel_id=1, source_target_pairs={{0,17},{1,16},{2,19},{3,18},{4,21},{5,20},{6,23},{7,22},{8,25},{9,... | collective-permute-start | bytes 49160 | tf_op jit(solution)/shard_map/ppermute | solution.py:34
  14.8 3.1 %collective-permute-done.4.refs_1_.refs_3_ = f32[4,8,128]{2,1,0:T(8,128)S(1)} collective-permute-done((f32[4,8,128]{2,1,0:T(8,128)S(1)}, f32[4,8,128]{2,1,0:T(8,128)S(1)}, u32[]{:S(2)}, u32[]{:S(2)}) %collective-permute-start.4) | collective-permute-done | bytes 16416 | tf_op jit(solution)/shard_map/ppermute | solution.py:34
  17.9 0.0 copy-start.6
  17.9 0.0 collective-permute-done.3.refs_0_.refs_2_
  17.9 0.0 copy-start.1
  17.9 0.0 collective-permute-done.2.other_ref
  17.9 0.0 copy-start.2
  17.9 0.0 copy-done
  17.9 0.6 %copy-done.6 = f32[4,8,128]{2,1,0:T(8,128)} copy-done((f32[4,8,128]{2,1,0:T(8,128)}, f32[4,8,128]{2,1,0:T(8,128)S(1)}, u32[]{:S(2)}) %copy-start.6) | copy-done | bytes 16408
  18.5 0.0 copy-done.1
  18.5 0.1 copy-done.2
  18.6 2.1 %join.1 = (f32[64,8,128]{2,1,0:T(8,128)}, f32[10,8,128]{2,1,0:T(8,128)}, f32[22,8,128]{2,1,0:T(8,128)}, f32[22,8,128]{2,1,0:T(8,128)}) custom-call(f32[64,8,128]{2,1,0:T(8,128)} %get-tuple-element.13.pt_ref, f32[32,8,128]{2,1,0:T(8,128)} %copy-done, f32[32,8,128]{2,1,0:T(8,128)} %copy-done.2, f32[16,128]{1,0:T(8,128)} %m_ref.5, s32[16,128]{1,0:T(8,128)} %t_ref.5, ...), custom_call_target="tpu_custom_call" | custom-call | tf_op jit(solution)/shard_map/join/pallas_call | solution.py:380
  20.6 1.6 %collective-permute-start.5 = (f32[22,8,128]{2,1,0:T(8,128)}, f32[22,8,128]{2,1,0:T(8,128)S(1)}, u32[]{:S(2)}, u32[]{:S(2)}) collective-permute-start(f32[22,8,128]{2,1,0:T(8,128)} %get-tuple-element.19), channel_id=1, source_target_pairs={{0,2},{1,3},{2,4},{3,5},{4,6},{5,7},{6,14},{7,15},{8,0},{9,1},{10,... | collective-permute-start | bytes 270344 | tf_op jit(solution)/shard_map/ppermute | solution.py:34
  22.2 0.0 collective-permute-start.6
  22.2 2.4 %collective-permute-done.5.first_ref = f32[22,8,128]{2,1,0:T(8,128)S(1)} collective-permute-done((f32[22,8,128]{2,1,0:T(8,128)}, f32[22,8,128]{2,1,0:T(8,128)S(1)}, u32[]{:S(2)}, u32[]{:S(2)}) %collective-permute-start.5) | collective-permute-done | bytes 90144 | tf_op jit(solution)/shard_map/ppermute | solution.py:34
  24.7 0.0 copy-start.3
  24.7 2.3 %collective-permute-done.6.second_ref = f32[22,8,128]{2,1,0:T(8,128)S(1)} collective-permute-done((f32[22,8,128]{2,1,0:T(8,128)}, f32[22,8,128]{2,1,0:T(8,128)S(1)}, u32[]{:S(2)}, u32[]{:S(2)}) %collective-permute-start.6) | collective-permute-done | bytes 90144 | tf_op jit(solution)/shard_map/ppermute | solution.py:34
  27.0 0.0 copy-done.3
  27.0 0.6 %copy-done.4 = f32[22,8,128]{2,1,0:T(8,128)} copy-done((f32[22,8,128]{2,1,0:T(8,128)}, f32[22,8,128]{2,1,0:T(8,128)S(1)}, u32[]{:S(2)}) %copy-start.4) | copy-done | bytes 90136
  27.6 3.6 %forecast.1 = f32[4,128,128]{2,1,0:T(8,128)} custom-call(f32[64,8,128]{2,1,0:T(8,128)} %get-tuple-element.17.start_ref, f32[10,8,128]{2,1,0:T(8,128)} %get-tuple-element.18.strip_ref, f32[16,128]{1,0:T(8,128)} %m_ref.5, s32[16,128]{1,0:T(8,128)} %t_ref.5, f32[22,8,128]{2,1,0:T(8,128)} %copy-done.3, f32[22,8,128]{2,1,0:T(8,128)} %copy-done.4), custom_call_target="tpu_custom_call" | custom-call | tf_op jit(solution)/shard_map/forecast/pallas_call | solution.py:389
  (3 shorter events, 0.0 us)
Async XLA Ops:
  2.0 1.7 %collective-permute-start = (f32[36,8,128]{2,1,0:T(8,128)}, f32[36,8,128]{2,1,0:T(8,128)S(1)}, u32[]{:S(2)}, u32[]{:S(2)}) collective-permute-start(f32[36,8,128]{2,1,0:T(8,128)} %get-tuple-element.15), channel_id=1, source_target_pairs={{0,8},{1,9},{2,10},{3,11},{4,12},{5,13},{6,14},{7,15},{8,0},{9,1},... | collective-permute-start | bytes 442376 | tf_op jit(solution)/shard_map/ppermute | solution.py:34
  4.6 6.8 %collective-permute-start.1 = (f32[32,8,128]{2,1,0:T(8,128)S(1)}, f32[32,8,128]{2,1,0:T(8,128)S(1)}, u32[]{:S(2)}, u32[]{:S(2)}) collective-permute-start(f32[32,8,128]{2,1,0:T(8,128)S(1)} %slice_add_fusion), channel_id=1, source_target_pairs={{0,16},{1,17},{2,18},{3,19},{4,20},{5,21},{6,22},{7,23},{8,24},{9,... | collective-permute-start | bytes 393224 | tf_op jit(solution)/shard_map/ppermute | solution.py:34
  8.3 3.2 %copy-start.5 = (f32[5,8,128]{2,1,0:T(8,128)S(1)}, f32[5,8,128]{2,1,0:T(8,128)}, u32[]{:S(2)}) copy-start(f32[5,8,128]{2,1,0:T(8,128)} %get-tuple-element.16.more_ref) | copy-start | bytes 61444
  11.4 6.6 %copy-start = (f32[32,8,128]{2,1,0:T(8,128)}, f32[32,8,128]{2,1,0:T(8,128)S(1)}, u32[]{:S(2)}) copy-start(f32[32,8,128]{2,1,0:T(8,128)S(1)} %add.10.mine_ref) | copy-start | bytes 393220
  11.4 6.5 %collective-permute-start.2 = (f32[32,8,128]{2,1,0:T(8,128)S(1)}, f32[32,8,128]{2,1,0:T(8,128)S(1)}, u32[]{:S(2)}, u32[]{:S(2)}) collective-permute-start(f32[32,8,128]{2,1,0:T(8,128)S(1)} %add.10.mine_ref), channel_id=1, source_target_pairs={{0,8},{1,9},{2,10},{3,11},{4,12},{5,13},{6,14},{7,15},{8,0},{9,1},... | collective-permute-start | bytes 393224 | tf_op jit(solution)/shard_map/ppermute | solution.py:34
  11.5 6.4 %collective-permute-start.3 = (f32[9,8,128]{2,1,0:T(8,128)S(1)}, f32[9,8,128]{2,1,0:T(8,128)S(1)}, u32[]{:S(2)}, u32[]{:S(2)}) collective-permute-start(f32[9,8,128]{2,1,0:T(8,128)S(1)} %pad_maximum_fusion), channel_id=1, source_target_pairs={{0,1},{1,0},{2,3},{3,2},{4,5},{5,4},{6,7},{7,6},{8,9},{9,8},{10,11... | collective-permute-start | bytes 110600 | tf_op jit(solution)/shard_map/ppermute | solution.py:34
  13.3 4.6 %collective-permute-start.4 = (f32[4,8,128]{2,1,0:T(8,128)S(1)}, f32[4,8,128]{2,1,0:T(8,128)S(1)}, u32[]{:S(2)}, u32[]{:S(2)}) collective-permute-start(f32[4,8,128]{2,1,0:T(8,128)S(1)} %slice_add_fusion.1), channel_id=1, source_target_pairs={{0,17},{1,16},{2,19},{3,18},{4,21},{5,20},{6,23},{7,22},{8,25},{9,... | collective-permute-start | bytes 49160 | tf_op jit(solution)/shard_map/ppermute | solution.py:34
  17.9 0.6 %copy-start.6 = (f32[4,8,128]{2,1,0:T(8,128)}, f32[4,8,128]{2,1,0:T(8,128)S(1)}, u32[]{:S(2)}) copy-start(f32[4,8,128]{2,1,0:T(8,128)S(1)} %collective-permute-done.4.refs_1_.refs_3_) | copy-start | bytes 49156
  17.9 0.6 %copy-start.1 = (f32[9,8,128]{2,1,0:T(8,128)}, f32[9,8,128]{2,1,0:T(8,128)S(1)}, u32[]{:S(2)}) copy-start(f32[9,8,128]{2,1,0:T(8,128)S(1)} %collective-permute-done.3.refs_0_.refs_2_) | copy-start | bytes 110596
  17.9 0.7 %copy-start.2 = (f32[32,8,128]{2,1,0:T(8,128)}, f32[32,8,128]{2,1,0:T(8,128)S(1)}, u32[]{:S(2)}) copy-start(f32[32,8,128]{2,1,0:T(8,128)S(1)} %collective-permute-done.2.other_ref) | copy-start | bytes 393220
  20.6 4.0 %collective-permute-start.5 = (f32[22,8,128]{2,1,0:T(8,128)}, f32[22,8,128]{2,1,0:T(8,128)S(1)}, u32[]{:S(2)}, u32[]{:S(2)}) collective-permute-start(f32[22,8,128]{2,1,0:T(8,128)} %get-tuple-element.19), channel_id=1, source_target_pairs={{0,2},{1,3},{2,4},{3,5},{4,6},{5,7},{6,14},{7,15},{8,0},{9,1},{10,... | collective-permute-start | bytes 270344 | tf_op jit(solution)/shard_map/ppermute | solution.py:34
  22.2 4.7 %collective-permute-start.6 = (f32[22,8,128]{2,1,0:T(8,128)}, f32[22,8,128]{2,1,0:T(8,128)S(1)}, u32[]{:S(2)}, u32[]{:S(2)}) collective-permute-start(f32[22,8,128]{2,1,0:T(8,128)} %get-tuple-element.20), channel_id=1, source_target_pairs={{0,8},{1,9},{2,0},{3,1},{4,2},{5,3},{6,4},{7,5},{8,10},{9,11},{10,... | collective-permute-start | bytes 270344 | tf_op jit(solution)/shard_map/ppermute | solution.py:34
  24.7 2.3 %copy-start.3 = (f32[22,8,128]{2,1,0:T(8,128)}, f32[22,8,128]{2,1,0:T(8,128)S(1)}, u32[]{:S(2)}) copy-start(f32[22,8,128]{2,1,0:T(8,128)S(1)} %collective-permute-done.5.first_ref) | copy-start | bytes 270340
  27.0 0.6 %copy-start.4 = (f32[22,8,128]{2,1,0:T(8,128)}, f32[22,8,128]{2,1,0:T(8,128)S(1)}, u32[]{:S(2)}) copy-start(f32[22,8,128]{2,1,0:T(8,128)S(1)} %collective-permute-done.6.second_ref) | copy-start | bytes 270340

commit v2 on v1

--- a/solution.py
+++ b/solution.py
@@ -15,7 +15,8 @@
 OUTSIDE = 1.0e6
 AXES = ("member", "dx", "dy")
 VMEM = pl.BlockSpec(memory_space=pltpu.VMEM)
-SMEM = pl.BlockSpec(memory_space=pltpu.SMEM)
+HBM = pl.BlockSpec(memory_space=pltpu.HBM)
+MODEST = pltpu.CompilerParams(vmem_limit_bytes=8 * 2**20)
 
 
 def send(value, target):
@@ -61,19 +62,36 @@
     return total
 
 
-def split_kernel(p_ref, c_ref, owner_ref, m_ref, t_ref, pt_ref, keep_ref, send_ref, more_ref):
+def split_kernel(
+    p_hbm, c_hbm, owner_hbm, m_hbm, t_hbm,
+    pt_ref, keep_ref, send_ref, more_ref, metric_ref,
+    p_ref, c_ref, owner_ref, t_ref, sems,
+):
     fields, _, cols = p_ref.shape
-    rows = m_ref.shape[0]
+    rows = t_ref.shape[0]
     levels = p_ref.shape[1] // rows
     half = rows // 2
     member = lax.axis_index("member")
     members = owner_ref.shape[0]
     first = lax.rem(member, 2) == 0
+    copies = [pltpu.make_async_copy(owner_hbm, owner_ref, sems.at[0])]
+    for f in range(fields):
+        copies.append(pltpu.make_async_copy(p_hbm.at[f], p_ref.at[f], sems.at[1 + 2 * f]))
+        copies.append(pltpu.make_async_copy(c_hbm.at[f], c_ref.at[f], sems.at[2 + 2 * f]))
+    copies.append(
+        pltpu.make_async_copy(m_hbm, metric_ref.at[pl.ds(0, rows), :], sems.at[1 + 2 * fields])
+    )
+    copies.append(pltpu.make_async_copy(t_hbm, t_ref, sems.at[2 + 2 * fields]))
+    for copy in copies:
+        copy.start()
+    copies[0].wait()
     weight = jnp.float32(0.0)
     for rank in range(members):
         per_rank = 2.0 * (members - rank) / (members * (members + 1.0))
         weight = weight + jnp.where(owner_ref[rank] == member, per_rank, 0.0)
     for f in range(fields):
+        copies[1 + 2 * f].wait()
+        copies[2 + 2 * f].wait()
         states, parts = [], []
         for x in range(rows):
             state = p_ref[f, pl.ds(x, levels, stride=rows), :]
@@ -86,22 +104,25 @@
             send_ref[x * fields + f] = jnp.where(first, parts[x + half], parts[x])
         send_ref[half * fields + f] = edges_of(parts, STEPS)
         more_ref[f] = edges_of(states, STEPS)
+    copies[-2].wait()
+    copies[-1].wait()
+    metric_ref[pl.ds(rows, rows), :] = t_ref[...].astype(jnp.float32)
     level = lax.broadcasted_iota(jnp.int32, (levels, cols), 0)
     columns = []
     for x in range(rows):
-        scale = jnp.broadcast_to(m_ref[pl.ds(x, 1), :], (levels, cols))
-        ground = jnp.broadcast_to(t_ref[pl.ds(x, 1), :].astype(jnp.float32), (levels, cols))
+        scale = jnp.broadcast_to(metric_ref[pl.ds(x, 1), :], (levels, cols))
+        ground = jnp.broadcast_to(metric_ref[pl.ds(rows + x, 1), :], (levels, cols))
         columns.append(jnp.where(level == 0, scale, ground))
     more_ref[fields] = edges_of(columns, STEPS)
 
 
 def join_kernel(
-    sizes, n_left, pt_ref, mine_ref, other_ref, m_ref, t_ref, more_ref, *refs
+    sizes, n_left, pt_ref, mine_ref, other_ref, metric_ref, more_ref, *refs
 ):
     left, rest = refs[:n_left], refs[n_left:]
     right, rest = rest[:n_left], rest[n_left:]
     start_ref, strip_ref, first_ref, second_ref = rest
-    rows, cols = m_ref.shape
+    rows, cols = metric_ref.shape[0] // 2, metric_ref.shape[1]
     levels = pt_ref.shape[1]
     fields = pt_ref.shape[0] // rows
     half, wide = rows // 2, STEPS
@@ -155,7 +176,7 @@
     strip_ref[fields] = a
     strip_ref[2 * fields + 1] = b
     ends.append(end)
-    scale, ground = m_ref[...], t_ref[...].astype(jnp.float32)
+    scale, ground = metric_ref[pl.ds(0, rows), :], metric_ref[pl.ds(rows, rows), :]
     tops = jnp.concatenate([scale[rows - wide :], ground[rows - wide :]], axis=0)
     bottoms = jnp.concatenate([scale[:wide], ground[:wide]], axis=0)
     for message, up in ((first_ref, parity == 0), (second_ref, parity == 1)):
@@ -168,9 +189,9 @@
 
 
 def forecast_kernel(
-    sizes, start_ref, strip_ref, m_ref, t_ref, first_ref, second_ref, out_ref, a_ref, b_ref, coef_ref
+    sizes, start_ref, strip_ref, metric_ref, first_ref, second_ref, out_ref, a_ref, b_ref, coef_ref
 ):
-    rows, cols = m_ref.shape
+    rows, cols = metric_ref.shape[0] // 2, metric_ref.shape[1]
     levels = start_ref.shape[1]
     fields = start_ref.shape[0] // rows
     wide = STEPS
@@ -214,8 +235,8 @@
         if x < wide:
             scale, ground = below[x : x + 1], below[wide + x : wide + x + 1]
         elif x < wide + rows:
-            scale = m_ref[pl.ds(x - wide, 1), :]
-            ground = t_ref[pl.ds(x - wide, 1), :].astype(jnp.float32)
+            scale = metric_ref[pl.ds(x - wide, 1), :]
+            ground = metric_ref[pl.ds(rows + x - wide, 1), :]
         else:
             r = x - wide - rows
             scale, ground = above[r : r + 1], above[wide + r : wide + r + 1]
@@ -341,18 +362,34 @@
         return jax.ShapeDtypeStruct((count, *tile), jnp.float32)
 
     flat = (fields, levels * rows, cols)
-    states, keep, give, more = pl.pallas_call(
+    states, keep, give, more, metric = pl.pallas_call(
         split_kernel,
         out_shape=(
             tiles(rows * fields),
             tiles(half * fields),
             tiles(half * fields + fields),
             tiles(fields + 1),
+            jax.ShapeDtypeStruct((2 * rows, cols), jnp.float32),
         ),
-        in_specs=[VMEM, VMEM, SMEM, VMEM, VMEM],
-        out_specs=(VMEM,) * 4,
+        in_specs=[HBM] * 5,
+        out_specs=(VMEM,) * 5,
+        scratch_shapes=[
+            pltpu.VMEM(flat, jnp.float32),
+            pltpu.VMEM(flat, jnp.float32),
+            pltpu.SMEM(owner.shape, jnp.int32),
+            pltpu.VMEM((rows, cols), jnp.int32),
+            pltpu.SemaphoreType.DMA((2 * fields + 3,)),
+        ],
+        compiler_params=MODEST,
         name="split",
-    )(perturbed_states.reshape(flat), control.reshape(flat), owner, map_factor, terrain)
+    )(
+        *(
+            pltpu.with_memory_space_constraint(value, pltpu.HBM)
+            for value in (
+                perturbed_states.reshape(flat), control.reshape(flat), owner, map_factor, terrain
+            )
+        )
+    )
 
     given = send(give, lambda k, i, j: (k ^ 1, i, j))
     total = keep + given[: half * fields]
@@ -373,31 +410,35 @@
         return [near] + [send(edges, there(b)) for b in chips]
 
     left = from_side(1)
-    right = left if along == 2 else from_side(-1)
-
+    right = from_side(-1) if along > 2 else []
+
+    total, left, right = lax.optimization_barrier((total, left, right))
     other = send(total, lambda k, i, j: (k ^ 1, i, j))
+    right = right or left
     count = STEPS * fields + fields + 2
     start, strips, first, second = pl.pallas_call(
         functools.partial(join_kernel, sizes, len(left)),
         out_shape=(tiles(rows * fields), tiles(2 * (fields + 1)), tiles(count), tiles(count)),
-        in_specs=[VMEM] * (6 + 2 * len(left)),
+        in_specs=[VMEM] * (5 + 2 * len(left)),
         out_specs=(VMEM,) * 4,
+        compiler_params=MODEST,
         name="join",
-    )(states, total, other, map_factor, terrain, more, *left, *right)
+    )(states, total, other, metric, more, *left, *right)
     first = send(first, loop_target(sizes[1], True))
     second = send(second, loop_target(sizes[1], False))
     out = pl.pallas_call(
         functools.partial(forecast_kernel, sizes),
         out_shape=jax.ShapeDtypeStruct(flat, jnp.float32),
-        in_specs=[VMEM] * 6,
+        in_specs=[VMEM] * 5,
         out_specs=VMEM,
         scratch_shapes=[
             pltpu.VMEM(((rows + 2 * STEPS) * fields, *tile), jnp.float32),
             pltpu.VMEM(((rows + 2 * STEPS) * fields, *tile), jnp.float32),
             pltpu.VMEM(((rows + 2 * STEPS) * 3, *tile), jnp.float32),
         ],
+        compiler_params=MODEST,
         name="forecast",
-    )(start, strips, map_factor, terrain, first, second)
+    )(start, strips, metric, first, second)
     return out.reshape(perturbed_states.shape)
 
 

time: 31.4 us -> 22.6 us (0.72)
  Pallas kernels: 7.62 us -> 4.3 us
  starting transfers between devices: 8.31 us -> 6.64 us
  other arithmetic: 1.66 us -> 0.05 us
  local copies, waits for them, and re-layouts: 1.3 us -> 0 us
  waiting for transfers between devices: 12.2 us -> 11.5 us
    pallas_call x1, Pallas kernels: 2.06 us -> 0.28 us  [on_device(): pl.pallas_call(functools.partial(join_kernel, sizes, len(left)), out_shap...]
    ppermute x7, starting transfers between devices: 8.31 us -> 6.64 us  [send(): return lax.ppermute(value, AXES, pairs)]
    unnamed x14 -> x0, local copies, waits for them, and re-layouts: 1.3 us -> none
    pallas_call x1, Pallas kernels: 3.56 us -> 2.5 us  [on_device(): pl.pallas_call(functools.partial(forecast_kernel, sizes), out_shape=jax.S...]
    add x1, other arithmetic: 0.92 us -> 0.02 us  [on_device(): total = keep + given[:half * fields]]
    add x1, other arithmetic: 0.72 us -> 0.01 us  [on_device(): edges = give[half * fields:] + given[half * fields:]]
    ppermute x7, waiting for transfers between devices: 12.2 us -> 11.5 us  [send(): return lax.ppermute(value, AXES, pairs)]
    pallas_call x1, Pallas kernels: 2 us -> 1.52 us  [on_device(): pl.pallas_call(split_kernel, out_shape=(tiles(rows * fields), tiles(half...]
  transfers between devices with their start and end apart: 7 -> 7, of which waited for: 5 -> 6; matrix products, arithmetic and copies ran while one was open for 2% -> 0% of each run, Pallas kernels for 0% -> 0%
where the time goes in v2:
time: 22.6 us; the launch traced here: 22.5 us
  waiting for transfers between devices  11.5 us (51%)
  starting transfers between devices  6.64 us (29%)
  Pallas kernels  4.3 us (19%)
    ppermute x7, waiting for transfers between devices, send(): return lax.ppermute(value, AXES, pairs)  11.5 us
    ppermute x7, starting transfers between devices, send(): return lax.ppermute(value, AXES, pairs)  6.64 us
    pallas_call x1, Pallas kernels, on_device(): pl.pallas_call(functools.partial(forecast_kernel, sizes), out_shape=jax.S...  2.5 us
    pallas_call x1, Pallas kernels, on_device(): pl.pallas_call(split_kernel, out_shape=(tiles(rows * fields), tiles(half...  1.52 us
  transfers between devices with their start and end apart: 7, of which 6 were waited for; matrix products, arithmetic and copies ran while one was open for 0% of the time, Pallas kernels for 0%

profile of v2, /device:TPU:0, one launch (start us, length us, event | category | flops | bytes accessed | tf_op | source)
XLA Modules:
  0.0 22.5 jit_solution(1399315835588248849)
XLA Ops:
  0.0 1.5 %split.1 = (f32[64,8,128]{2,1,0:T(8,128)S(1)}, f32[32,8,128]{2,1,0:T(8,128)S(1)}, f32[36,8,128]{2,1,0:T(8,128)S(1)}, f32[5,8,128]{2,1,0:T(8,128)S(1)}, f32[32,128]{1,0:T(8,128)S(1)}) custom-call(f32[4,128,128]{2,1,0:T(8,128)} %bitcast.3, f32[4,128,128]{2,1,0:T(8,128)} %bitcast.4, s32[4]{0:T(128)} %owner_hbm.1, f32[16,128]{1,0:T(8,128)} %m_hbm.1, s32[16,128]{1,0:T(8,128)} %t_hbm.1), custom_call_target="tpu_custom_call" | custom-call | tf_op jit(solution)/shard_map/split/pallas_call | solution.py:365
  1.5 0.5 %collective-permute-start = (f32[36,8,128]{2,1,0:T(8,128)S(1)}, f32[36,8,128]{2,1,0:T(8,128)S(1)}, u32[]{:S(2)}, u32[]{:S(2)}) collective-permute-start(f32[36,8,128]{2,1,0:T(8,128)S(1)} %get-tuple-element.19), channel_id=1, source_target_pairs={{0,8},{1,9},{2,10},{3,11},{4,12},{5,13},{6,14},{7,15},{8,0},{9,1},... | collective-permute-start | bytes 442376 | tf_op jit(solution)/shard_map/ppermute | solution.py:35
  2.0 1.0 %collective-permute-done = f32[36,8,128]{2,1,0:T(8,128)S(1)} collective-permute-done((f32[36,8,128]{2,1,0:T(8,128)S(1)}, f32[36,8,128]{2,1,0:T(8,128)S(1)}, u32[]{:S(2)}, u32[]{:S(2)}) %collective-permute-start) | collective-permute-done | bytes 147488 | tf_op jit(solution)/shard_map/ppermute | solution.py:35
  3.1 2.9 %collective-permute-start.1 = (f32[32,8,128]{2,1,0:T(8,128)S(1)}, f32[32,8,128]{2,1,0:T(8,128)S(1)}, u32[]{:S(2)}, u32[]{:S(2)}) collective-permute-start(f32[32,8,128]{2,1,0:T(8,128)S(1)} %slice_add_fusion), channel_id=1, source_target_pairs={{0,16},{1,17},{2,18},{3,19},{4,20},{5,21},{6,22},{7,23},{8,24},{9,... | collective-permute-start | bytes 393224 | tf_op jit(solution)/shard_map/ppermute | solution.py:35
  6.0 1.6 %collective-permute-start.2 = (f32[9,8,128]{2,1,0:T(8,128)S(1)}, f32[9,8,128]{2,1,0:T(8,128)S(1)}, u32[]{:S(2)}, u32[]{:S(2)}) collective-permute-start(f32[9,8,128]{2,1,0:T(8,128)S(1)} %pad_maximum_fusion), channel_id=1, source_target_pairs={{0,1},{1,0},{2,3},{3,2},{4,5},{5,4},{6,7},{7,6},{8,9},{9,8},{10,11... | collective-permute-start | bytes 110600 | tf_op jit(solution)/shard_map/ppermute | solution.py:35
  7.6 0.0 collective-permute-start.3
  7.6 2.2 %collective-permute-done.1 = f32[32,8,128]{2,1,0:T(8,128)S(1)} collective-permute-done((f32[32,8,128]{2,1,0:T(8,128)S(1)}, f32[32,8,128]{2,1,0:T(8,128)S(1)}, u32[]{:S(2)}, u32[]{:S(2)}) %collective-permute-start.1) | collective-permute-done | bytes 131104 | tf_op jit(solution)/shard_map/ppermute | solution.py:35
  9.8 2.4 %collective-permute-done.3.refs_1_.refs_3_ = f32[4,8,128]{2,1,0:T(8,128)S(1)} collective-permute-done((f32[4,8,128]{2,1,0:T(8,128)S(1)}, f32[4,8,128]{2,1,0:T(8,128)S(1)}, u32[]{:S(2)}, u32[]{:S(2)}) %collective-permute-start.3) | collective-permute-done | bytes 16416 | tf_op jit(solution)/shard_map/ppermute | solution.py:35
  12.2 0.0 collective-permute-done.2.refs_0_.refs_2_
  12.2 0.0 collective-permute-start.4
  12.2 1.3 %collective-permute-done.4.other_ref = f32[32,8,128]{2,1,0:T(8,128)S(1)} collective-permute-done((f32[32,8,128]{2,1,0:T(8,128)S(1)}, f32[32,8,128]{2,1,0:T(8,128)S(1)}, u32[]{:S(2)}, u32[]{:S(2)}) %collective-permute-start.4) | collective-permute-done | bytes 131104 | tf_op jit(solution)/shard_map/ppermute | solution.py:35
  13.6 0.3 %join.1 = (f32[64,8,128]{2,1,0:T(8,128)S(1)}, f32[10,8,128]{2,1,0:T(8,128)S(1)}, f32[22,8,128]{2,1,0:T(8,128)S(1)}, f32[22,8,128]{2,1,0:T(8,128)S(1)}) custom-call(f32[64,8,128]{2,1,0:T(8,128)S(1)} %get-tuple-element.17.pt_ref, f32[32,8,128]{2,1,0:T(8,128)S(1)} %add.10.mine_ref, f32[32,8,128]{2,1,0:T(8,128)S(1)} %collective-permute-done.4.other_ref, ...), custom_call_target="tpu_custom_call" | custom-call | tf_op jit(solution)/shard_map/join/pallas_call | solution.py:419
  13.9 1.6 %collective-permute-start.5 = (f32[22,8,128]{2,1,0:T(8,128)S(1)}, f32[22,8,128]{2,1,0:T(8,128)S(1)}, u32[]{:S(2)}, u32[]{:S(2)}) collective-permute-start(f32[22,8,128]{2,1,0:T(8,128)S(1)} %get-tuple-element.27), channel_id=1, source_target_pairs={{0,2},{1,3},{2,4},{3,5},{4,6},{5,7},{6,14},{7,15},{8,0},{9,1},{10,... | collective-permute-start | bytes 270344 | tf_op jit(solution)/shard_map/ppermute | solution.py:35
  15.5 0.0 collective-permute-start.6
  15.5 2.4 %collective-permute-done.5.first_ref = f32[22,8,128]{2,1,0:T(8,128)S(1)} collective-permute-done((f32[22,8,128]{2,1,0:T(8,128)S(1)}, f32[22,8,128]{2,1,0:T(8,128)S(1)}, u32[]{:S(2)}, u32[]{:S(2)}) %collective-permute-start.5) | collective-permute-done | bytes 90144 | tf_op jit(solution)/shard_map/ppermute | solution.py:35
  17.8 2.2 %collective-permute-done.6.second_ref = f32[22,8,128]{2,1,0:T(8,128)S(1)} collective-permute-done((f32[22,8,128]{2,1,0:T(8,128)S(1)}, f32[22,8,128]{2,1,0:T(8,128)S(1)}, u32[]{:S(2)}, u32[]{:S(2)}) %collective-permute-start.6) | collective-permute-done | bytes 90144 | tf_op jit(solution)/shard_map/ppermute | solution.py:35
  20.0 2.5 %forecast.1 = f32[4,128,128]{2,1,0:T(8,128)} custom-call(f32[64,8,128]{2,1,0:T(8,128)S(1)} %get-tuple-element.25.start_ref, f32[10,8,128]{2,1,0:T(8,128)S(1)} %get-tuple-element.26.strip_ref, f32[32,128]{1,0:T(8,128)S(1)} %get-tuple-element.22.metric_ref, f32[22,8,128]{2,1,0:T(8,128)S(1)} %collective-permute-done.5.first_ref, ...), custom_call_target="tpu_custom_call" | custom-call | tf_op jit(solution)/shard_map/forecast/pallas_call | solution.py:429
  (4 shorter events, 0.0 us)
Async XLA Ops:
  1.5 1.5 %collective-permute-start = (f32[36,8,128]{2,1,0:T(8,128)S(1)}, f32[36,8,128]{2,1,0:T(8,128)S(1)}, u32[]{:S(2)}, u32[]{:S(2)}) collective-permute-start(f32[36,8,128]{2,1,0:T(8,128)S(1)} %get-tuple-element.19), channel_id=1, source_target_pairs={{0,8},{1,9},{2,10},{3,11},{4,12},{5,13},{6,14},{7,15},{8,0},{9,1},... | collective-permute-start | bytes 442376 | tf_op jit(solution)/shard_map/ppermute | solution.py:35
  3.1 6.8 %collective-permute-start.1 = (f32[32,8,128]{2,1,0:T(8,128)S(1)}, f32[32,8,128]{2,1,0:T(8,128)S(1)}, u32[]{:S(2)}, u32[]{:S(2)}) collective-permute-start(f32[32,8,128]{2,1,0:T(8,128)S(1)} %slice_add_fusion), channel_id=1, source_target_pairs={{0,16},{1,17},{2,18},{3,19},{4,20},{5,21},{6,22},{7,23},{8,24},{9,... | collective-permute-start | bytes 393224 | tf_op jit(solution)/shard_map/ppermute | solution.py:35
  6.0 6.2 %collective-permute-start.2 = (f32[9,8,128]{2,1,0:T(8,128)S(1)}, f32[9,8,128]{2,1,0:T(8,128)S(1)}, u32[]{:S(2)}, u32[]{:S(2)}) collective-permute-start(f32[9,8,128]{2,1,0:T(8,128)S(1)} %pad_maximum_fusion), channel_id=1, source_target_pairs={{0,1},{1,0},{2,3},{3,2},{4,5},{5,4},{6,7},{7,6},{8,9},{9,8},{10,11... | collective-permute-start | bytes 110600 | tf_op jit(solution)/shard_map/ppermute | solution.py:35
  7.6 4.6 %collective-permute-start.3 = (f32[4,8,128]{2,1,0:T(8,128)S(1)}, f32[4,8,128]{2,1,0:T(8,128)S(1)}, u32[]{:S(2)}, u32[]{:S(2)}) collective-permute-start(f32[4,8,128]{2,1,0:T(8,128)S(1)} %slice_add_fusion.1), channel_id=1, source_target_pairs={{0,17},{1,16},{2,19},{3,18},{4,21},{5,20},{6,23},{7,22},{8,25},{9,... | collective-permute-start | bytes 49160 | tf_op jit(solution)/shard_map/ppermute | solution.py:35
  12.2 1.3 %collective-permute-start.4 = (f32[32,8,128]{2,1,0:T(8,128)S(1)}, f32[32,8,128]{2,1,0:T(8,128)S(1)}, u32[]{:S(2)}, u32[]{:S(2)}) collective-permute-start(f32[32,8,128]{2,1,0:T(8,128)S(1)} %add.10.mine_ref), channel_id=1, source_target_pairs={{0,8},{1,9},{2,10},{3,11},{4,12},{5,13},{6,14},{7,15},{8,0},{9,1},... | collective-permute-start | bytes 393224 | tf_op jit(solution)/shard_map/ppermute | solution.py:35
  13.9 4.0 %collective-permute-start.5 = (f32[22,8,128]{2,1,0:T(8,128)S(1)}, f32[22,8,128]{2,1,0:T(8,128)S(1)}, u32[]{:S(2)}, u32[]{:S(2)}) collective-permute-start(f32[22,8,128]{2,1,0:T(8,128)S(1)} %get-tuple-element.27), channel_id=1, source_target_pairs={{0,2},{1,3},{2,4},{3,5},{4,6},{5,7},{6,14},{7,15},{8,0},{9,1},{10,... | collective-permute-start | bytes 270344 | tf_op jit(solution)/shard_map/ppermute | solution.py:35
  15.5 4.5 %collective-permute-start.6 = (f32[22,8,128]{2,1,0:T(8,128)S(1)}, f32[22,8,128]{2,1,0:T(8,128)S(1)}, u32[]{:S(2)}, u32[]{:S(2)}) collective-permute-start(f32[22,8,128]{2,1,0:T(8,128)S(1)} %get-tuple-element.28), channel_id=1, source_target_pairs={{0,8},{1,9},{2,0},{3,1},{4,2},{5,3},{6,4},{7,5},{8,10},{9,11},{10,... | collective-permute-start | bytes 270344 | tf_op jit(solution)/shard_map/ppermute | solution.py:35

commit v3 on v2

v3 whole, which is shorter than its diff:
```python
import functools

import jax
import jax.numpy as jnp
from jax import lax
from jax.experimental import pallas as pl
from jax.experimental.pallas import tpu as pltpu
from jax.sharding import PartitionSpec as P

STEPS = 4

integration_step = 0.2
diffusion = 0.1

OUTSIDE = 1.0e6
AXES = ("member", "dx", "dy")
VMEM = pl.BlockSpec(memory_space=pltpu.VMEM)
HBM = pl.BlockSpec(memory_space=pltpu.HBM)
MODEST = pltpu.CompilerParams(vmem_limit_bytes=8 * 2**20)


def send(value, target):
    sizes = [lax.axis_size(axis) for axis in AXES]
    pairs = []
    for member in range(sizes[0]):
        for i in range(sizes[1]):
            for j in range(sizes[2]):
                k, l, m = target(member, i, j)
                pairs.append(
                    (
                        (member * sizes[1] + i) * sizes[2] + j,
                        (k * sizes[1] + l) * sizes[2] + m,
                    )
                )
    return lax.ppermute(value, AXES, pairs)


def loop_target(rows, forward):
    def target(member, i, j):
        step = 1 if (member % 2 == 0) == forward else -1
        if 0 <= i + step < rows:
            return member, i + step, j
        return member ^ 1, i, j

    return target


def lanes_of(shape):
    return lax.broadcasted_iota(jnp.int32, shape, len(shape) - 1)


def turn(tile, by, axis=1):
    return pltpu.roll(tile, by % tile.shape[axis], axis)


def edges_of(tiles, width):
    lane = lanes_of(tiles[0].shape)
    total = None
    for x, tile in enumerate(tiles):
        moved = turn(tile, 2 * width * x + width)
        total = moved if total is None else jnp.where(lane < 2 * width * x, total, moved)
    return total


def split_kernel(
    p_hbm, c_hbm, owner_hbm, m_hbm, t_hbm,
    pt_ref, keep_ref, send_ref, edge_ref, side_ref, metric_ref,
    p_ref, c_ref, owner_ref, t_ref, sems,
):
    fields, _, cols = p_ref.shape
    rows = t_ref.shape[0]
    levels = p_ref.shape[1] // rows
    half = rows // 2
    member = lax.axis_index("member")
    members = owner_ref.shape[0]
    first = lax.rem(member, 2) == 0
    copies = [pltpu.make_async_copy(owner_hbm, owner_ref, sems.at[0])]
    for f in range(fields):
        copies.append(pltpu.make_async_copy(p_hbm.at[f], p_ref.at[f], sems.at[1 + 2 * f]))
        copies.append(pltpu.make_async_copy(c_hbm.at[f], c_ref.at[f], sems.at[2 + 2 * f]))
    copies.append(
        pltpu.make_async_copy(m_hbm, metric_ref.at[pl.ds(0, rows), :], sems.at[1 + 2 * fields])
    )
    copies.append(pltpu.make_async_copy(t_hbm, t_ref, sems.at[2 + 2 * fields]))
    for copy in copies:
        copy.start()
    copies[0].wait()
    weight = jnp.float32(0.0)
    for rank in range(members):
        per_rank = 2.0 * (members - rank) / (members * (members + 1.0))
        weight = weight + jnp.where(owner_ref[rank] == member, per_rank, 0.0)
    for f in range(fields):
        copies[1 + 2 * f].wait()
        copies[2 + 2 * f].wait()
        states, parts = [], []
        for x in range(rows):
            state = p_ref[f, pl.ds(x, levels, stride=rows), :]
            analysis = c_ref[f, pl.ds(x, levels, stride=rows), :]
            pt_ref[x * fields + f] = state
            states.append(state)
            parts.append(weight * analysis - state * (1.0 / members))
        for r in range(half):
            keep_ref[r * fields + f] = jnp.where(first, parts[r], parts[rows - 1 - r])
            send_ref[r * fields + f] = jnp.where(first, parts[rows - 1 - r], parts[r])
        edge_ref[f] = edges_of(parts, STEPS)
        side_ref[f] = edge_ref[f]
        side_ref[fields + f] = edges_of(states, STEPS)
    copies[-2].wait()
    copies[-1].wait()
    metric_ref[pl.ds(rows, rows), :] = t_ref[...].astype(jnp.float32)
    level = lax.broadcasted_iota(jnp.int32, (levels, cols), 0)
    columns = []
    for x in range(rows):
        scale = jnp.broadcast_to(metric_ref[pl.ds(x, 1), :], (levels, cols))
        ground = jnp.broadcast_to(metric_ref[pl.ds(rows + x, 1), :], (levels, cols))
        columns.append(jnp.where(level == 0, scale, ground))
    side_ref[2 * fields] = edges_of(columns, STEPS)


def has_neighbours(axis, size):
    place = lax.axis_index(axis)
    return place > 0, place < size - 1


def coefficients(level, scale, ground):
    scale = jnp.broadcast_to(scale, level.shape)
    ground = jnp.broadcast_to(ground, level.shape)
    mask = (level.astype(jnp.float32) >= ground).astype(jnp.float32)
    return (
        mask * (1.0 - 6.0 * integration_step * diffusion),
        mask * (integration_step * diffusion),
        mask * (scale * (0.5 * integration_step)),
    )


def updated(level, coefs, cur, dx, sx, dy, sy):
    levels = level.shape[0]
    new = []
    for f, here in enumerate(cur):
        advected = cur[0] * dx[f] + cur[1] * dy[f]
        if f == 0:
            advected = advected + dx[2]
        elif f == 1:
            advected = advected + dy[2]
        elif f == 2:
            advected = advected + (dx[0] + dy[1])
        upper = jnp.where(level < levels - 1, turn(here, -1, 0), 0.0)
        lower = jnp.where(level > 0, turn(here, 1, 0), 0.0)
        total = (sx[f] + sy[f]) + (upper + lower)
        new.append(coefs[0] * here + coefs[1] * total - coefs[2] * advected)
    return new


def row_step(level, lane, coefs, before, cur, after, beyond, spot):
    cols = lane.shape[1]
    dx, sx, dy, sy = [], [], [], []
    for f, here in enumerate(cur):
        outer = turn(beyond[f], -spot)
        north = jnp.where(lane == cols - 1, outer, turn(here, -1))
        south = jnp.where(lane == 0, outer, turn(here, 1))
        dx.append(after[f] - before[f])
        sx.append(after[f] + before[f])
        dy.append(north - south)
        sy.append(north + south)
    return updated(level, coefs, cur, dx, sx, dy, sy)


def strip_step(level, coefs, here, east, west):
    dx, sx, dy, sy = [], [], [], []
    for f, tile in enumerate(here):
        north, south = turn(tile, -1), turn(tile, 1)
        dx.append(east[f] - west[f])
        sx.append(east[f] + west[f])
        dy.append(north - south)
        sy.append(north + south)
    return updated(level, coefs, here, dx, sx, dy, sy)


def outside_columns(lane, width, left, right):
    return [
        jnp.where(lax.rem(lane, 2 * width) == width - 1, a, turn(b, -2))
        for a, b in zip(left, right)
    ]


def join_kernel(
    sizes, n_sides, pt_ref, mine_ref, edge_ref, other_ref, metric_ref, side_ref, *refs
):
    near, (start_ref, beside_ref, first_ref, second_ref) = refs[:n_sides], refs[n_sides:]
    rows, cols = metric_ref.shape[0] // 2, metric_ref.shape[1]
    levels = pt_ref.shape[1]
    fields = pt_ref.shape[0] // rows
    wide = STEPS
    parity = lax.rem(lax.axis_index("member"), 2)
    has_left, has_right = has_neighbours("dy", sizes[2])
    lane = lanes_of((levels, cols))
    early = lax.rem(lane, 2 * wide) < wide
    quarter = 2 * wide * wide

    for r in range(wide):
        for f in range(fields):
            mine, other = mine_ref[r * fields + f], other_ref[r * fields + f]
            low, high = jnp.where(parity == 0, mine, other), jnp.where(parity == 0, other, mine)
            start_ref[r * fields + f] = pt_ref[r * fields + f] + low
            end = 2 * wide - 1 - r
            start_ref[end * fields + f] = pt_ref[(rows - 1 - r) * fields + f] + high

    def ends_of(a, b):
        return jnp.where(
            lane < quarter,
            a,
            jnp.where(
                lane < 2 * quarter,
                turn(b, quarter),
                jnp.where(lane < cols - quarter, turn(b, -quarter), a),
            ),
        )

    ends = []
    far = 0 if n_sides == 1 else 1
    for f in range(fields + 1):
        if f < fields:
            own_rows = {}
            for r in range(wide):
                own_rows[r] = start_ref[r * fields + f]
                own_rows[rows - 1 - r] = start_ref[(2 * wide - 1 - r) * fields + f]
            own = None
            for x in sorted(own_rows):
                moved = turn(own_rows[x], 2 * wide * x + wide)
                own = moved if own is None else jnp.where(lane < 2 * wide * x, own, moved)
            sums = []
            for side in (0, far):
                k = side * fields + f
                total = edge_ref[k] + other_ref[wide * fields + k]
                sums.append(near[side][fields + f] + total)
            before = jnp.where(has_left, sums[0], 0.0)
            after = jnp.where(has_right, sums[1], 0.0)
        else:
            own = side_ref[2 * fields]
            before = jnp.where(has_left, near[0][2 * fields], OUTSIDE)
            after = jnp.where(has_right, near[far][2 * fields], OUTSIDE)
        beside_ref[f] = before
        beside_ref[fields + 1 + f] = after
        ends.append(ends_of(jnp.where(early, before, own), jnp.where(early, own, after)))
    scale, ground = metric_ref[pl.ds(0, rows), :], metric_ref[pl.ds(rows, rows), :]
    tops = jnp.concatenate([scale[rows - wide :], ground[rows - wide :]], axis=0)
    bottoms = jnp.concatenate([scale[:wide], ground[:wide]], axis=0)
    for message, up in ((first_ref, parity == 0), (second_ref, parity == 1)):
        base = jnp.where(up, wide, 0) * fields
        for k in range(wide * fields):
            message[k] = start_ref[base + k]
        for k, end in enumerate(ends):
            message[wide * fields + k] = end
        message[wide * fields + fields + 1] = jnp.where(up, tops, bottoms)


def middle_kernel(
    pt_ref, outer_ref, mine_ref, other_ref, metric_ref, side_ref, beside_ref,
    strip_ref, saved_ref, done_ref, a_ref, b_ref,
):
    rows, cols = metric_ref.shape[0] // 2, metric_ref.shape[1]
    levels = pt_ref.shape[1]
    fields = pt_ref.shape[0] // rows
    wide = STEPS
    group = 2 * wide
    half = rows // 2
    parity = lax.rem(lax.axis_index("member"), 2)
    lane = lanes_of((levels, cols))
    level = lax.broadcasted_iota(jnp.int32, (levels, cols), 0)
    early = lax.rem(lane, group) < wide
    for r in range(wide):
        for f in range(fields):
            a_ref[r * fields + f] = outer_ref[r * fields + f]
            a_ref[(rows - 1 - r) * fields + f] = outer_ref[(group - 1 - r) * fields + f]
    for r in range(wide, half):
        for f in range(fields):
            k = (r - wide) * fields + f
            mine, other = mine_ref[k], other_ref[k]
            low, high = jnp.where(parity == 0, mine, other), jnp.where(parity == 0, other, mine)
            a_ref[r * fields + f] = pt_ref[r * fields + f] + low
            mirrored = (rows - 1 - r) * fields + f
            a_ref[mirrored] = pt_ref[mirrored] + high
    left, right = [], []
    for f in range(fields + 1):
        if f < fields:
            own = edges_of([a_ref[x * fields + f] for x in range(rows)], wide)
        else:
            own = side_ref[2 * fields]
        left.append(jnp.where(early, beside_ref[f], own))
        right.append(jnp.where(early, own, beside_ref[fields + 1 + f]))
        strip_ref[f] = left[f]
        strip_ref[fields + 1 + f] = right[f]
    strip_coefs = [coefficients(level, side[fields][0:1], side[fields][1:2]) for side in (left, right)]
    left, right = left[:fields], right[:fields]
    coefs = [
        coefficients(level, metric_ref[pl.ds(x, 1), :], metric_ref[pl.ds(rows + x, 1), :])
        for x in range(rows)
    ]
    for number in range(STEPS):
        source, sink = (a_ref, b_ref) if number % 2 == 0 else (b_ref, a_ref)
        beyond = outside_columns(lane, wide, left, right)
        bottom, top = number + 1, rows - 1 - number
        row = lambda x: [source[x * fields + f] for f in range(fields)]
        before, cur = row(bottom - 1), row(bottom)
        for x in range(bottom, top):
            after = row(x + 1)
            new = row_step(
                level, lane, coefs[x], before, cur, after, beyond, group * x + wide - 1
            )
            edge = {bottom: 0, bottom + 1: 1, top - 2: 2, top - 1: 3}.get(x)
            for f in range(fields):
                if number == STEPS - 1:
                    done_ref[(x - wide) * fields + f] = new[f]
                else:
                    sink[x * fields + f] = new[f]
                    if edge is not None:
                        saved_ref[(4 * number + edge) * fields + f] = new[f]
            before, cur = cur, after
        if number < STEPS - 1:
            left, right = [
                strip_step(
                    level,
                    strip_coefs[side],
                    tiles,
                    [turn(tile, -group) for tile in tiles],
                    [turn(tile, group) for tile in tiles],
                )
                for side, tiles in enumerate((left, right))
            ]


def outer_kernel(
    sizes, outer_ref, strip_ref, saved_ref, done_ref, metric_ref, first_ref, second_ref,
    out_hbm, out_ref, sems,
):
    rows, cols = metric_ref.shape[0] // 2, metric_ref.shape[1]
    levels = outer_ref.shape[1]
    wide = STEPS
    group = 2 * wide
    fields = outer_ref.shape[0] // group
    half = rows // 2
    even = lax.rem(lax.axis_index("member"), 2) == 0
    has_low, has_high = has_neighbours("dx", sizes[1])
    lane = lanes_of((levels, cols))
    level = lax.broadcasted_iota(jnp.int32, (levels, cols), 0)
    quarter = group * wide

    def low(k, empty=0.0):
        return jnp.where(has_low, jnp.where(even, first_ref[k], second_ref[k]), empty)

    def high(k, empty=0.0):
        return jnp.where(has_high, jnp.where(even, second_ref[k], first_ref[k]), empty)

    def stretched(k, empty):
        mine_a = turn(strip_ref[k], quarter)
        mine_b = turn(strip_ref[fields + 1 + k], quarter)
        under, over = low(wide * fields + k, empty), high(wide * fields + k, empty)

        def end(own, other):
            return jnp.where(lane < quarter, own, jnp.where(lane < 2 * quarter, other, empty))

        return (
            (
                jnp.where(lane < quarter, turn(under, quarter), mine_a),
                end(mine_a, turn(over, quarter)),
            ),
            (
                jnp.where(lane < quarter, turn(under, 2 * quarter), mine_b),
                end(mine_b, over),
            ),
        )

    by_field = [stretched(f, 0.0) for f in range(fields)]
    strips = [[[by_field[f][side][v] for f in range(fields)] for v in range(2)] for side in range(2)]
    strip_coefs = [
        [coefficients(level, tile[0:1], tile[1:2]) for tile in side]
        for side in stretched(fields, OUTSIDE)
    ]
    beyond = []
    for number in range(STEPS):
        beyond.append(
            [outside_columns(lane, wide, strips[0][v], strips[1][v]) for v in range(2)]
        )
        if number == STEPS - 1:
            break
        new = []
        for side, (one, two) in enumerate(strips):
            ahead = [
                [jnp.where(lane < cols - group, turn(p, -group), turn(q, -group)) for p, q in zip(one, two)],
                [turn(q, -group) for q in two],
            ]
            behind = [
                [turn(p, group) for p in one],
                [jnp.where(lane < group, turn(p, group), turn(q, group)) for p, q in zip(one, two)],
            ]
            new.append(
                [
                    strip_step(level, strip_coefs[side][v], (one, two)[v], ahead[v], behind[v])
                    for v in range(2)
                ]
            )
        strips = new

    for x in range(wide, rows - wide):
        for f in range(fields):
            out_ref[f, pl.ds(x, levels, stride=rows), :] = done_ref[(x - wide) * fields + f]

    def saved(number, edge):
        return [saved_ref[(4 * (number - 1) + edge) * fields + f] for f in range(fields)]

    def finish(is_low):
        metric = wide * fields + fields + 1
        halo = low(metric, OUTSIDE) if is_low else high(metric, OUTSIDE)
        coefs, state = {}, {}
        for r in range(wide):
            message = [(low if is_low else high)(r * fields + f) for f in range(fields)]
            state[r - wide if is_low else rows + r] = message
            coefs[r - wide if is_low else rows + r] = coefficients(
                level, halo[r : r + 1], halo[wide + r : wide + r + 1]
            )
            x = r if is_low else rows - wide + r
            k = r if is_low else wide + r
            state[x] = [outer_ref[k * fields + f] for f in range(fields)]
            coefs[x] = coefficients(
                level, metric_ref[pl.ds(x, 1), :], metric_ref[pl.ds(rows + x, 1), :]
            )
        for number in range(STEPS):
            if number > 0:
                if is_low:
                    state[number], state[number + 1] = saved(number, 0), saved(number, 1)
                else:
                    state[rows - 2 - number], state[rows - 1 - number] = saved(number, 2), saved(number, 3)
            bottom = number + 1 - wide if is_low else rows - 1 - number
            new = {}
            for x in range(bottom, bottom + wide):
                spot = group * (x + wide) + wide - 1
                outside = beyond[number][spot // cols]
                new[x] = row_step(
                    level, lane, coefs[x], state[x - 1], state[x], state[x + 1], outside, spot % cols
                )
            state = new
        for x, tiles in state.items():
            for f in range(fields):
                out_ref[f, pl.ds(x, levels, stride=rows), :] = tiles[f]

    copies = []
    for n, is_low in enumerate((True, False)):
        finish(is_low)
        part = pl.ds(n * half, half)
        source = out_ref.reshape(fields * levels, rows, cols)
        copies.append(
            pltpu.make_async_copy(source.at[:, part, :], out_hbm.at[:, part, :], sems.at[n])
        )
        copies[-1].start()
    for copy in copies:
        copy.wait()


def on_device(perturbed_states, control, owner, map_factor, terrain):
    _, fields, levels, rows, cols = perturbed_states.shape
    sizes = tuple(lax.axis_size(axis) for axis in AXES)
    members, along = sizes[0], sizes[2]
    half = rows // 2
    tile = (levels, cols)

    def tiles(count):
        return jax.ShapeDtypeStruct((count, *tile), jnp.float32)

    def room(count):
        return pltpu.VMEM((count, *tile), jnp.float32)

    flat = (fields, levels * rows, cols)
    states, keep, give, edge, side, metric = pl.pallas_call(
        split_kernel,
        out_shape=(
            tiles(rows * fields),
            tiles(half * fields),
            tiles(half * fields),
            tiles(fields),
            tiles(2 * fields + 1),
            jax.ShapeDtypeStruct((2 * rows, cols), jnp.float32),
        ),
        in_specs=[HBM] * 5,
        out_specs=(VMEM,) * 6,
        scratch_shapes=[
            pltpu.VMEM(flat, jnp.float32),
            pltpu.VMEM(flat, jnp.float32),
            pltpu.SMEM(owner.shape, jnp.int32),
            pltpu.VMEM((rows, cols), jnp.int32),
            pltpu.SemaphoreType.DMA((2 * fields + 3,)),
        ],
        compiler_params=MODEST,
        name="split",
    )(
        *(
            pltpu.with_memory_space_constraint(value, pltpu.HBM)
            for value in (
                perturbed_states.reshape(flat), control.reshape(flat), owner, map_factor, terrain
            )
        )
    )

    def over_members(value, bit):
        return send(value, lambda k, i, j: (k ^ bit, i, j))

    def over_chips(value):
        bit = 2
        while bit < members:
            value = value + over_members(value, bit)
            bit *= 2
        return value

    given = over_members(give, 1)
    def from_beside(value, step, bit):
        return send(value, lambda k, i, j: (k ^ bit, i, (j + step) % along))

    steps = (1, -1) if along > 2 else (1,)
    near = [from_beside(side, step, 0) for step in steps]
    edges = []
    for step, n in zip(steps, near):
        total = n[:fields]
        for bit in range(2, members, 2):
            total = total + from_beside(edge, step, bit)
        edges.append(total)
    edges = jnp.concatenate(edges, axis=0)
    cut = STEPS * fields
    outer = over_chips(keep[:cut] + given[:cut])
    inner = over_chips(keep[cut:] + given[cut:])

    other = over_members(jnp.concatenate([outer, edges], axis=0), 1)
    count = cut + fields + 2
    start, beside, first, second = pl.pallas_call(
        functools.partial(join_kernel, sizes, len(near)),
        out_shape=(tiles(2 * cut), tiles(2 * (fields + 1)), tiles(count), tiles(count)),
        in_specs=[VMEM] * (6 + len(near)),
        out_specs=(VMEM,) * 4,
        compiler_params=MODEST,
        name="join",
    )(states, outer, edges, other, metric, side, *near)
    first_in = send(first, loop_target(sizes[1], True))
    second_in = send(second, loop_target(sizes[1], False))
    inner, _ = lax.optimization_barrier((inner, first))
    other = over_members(inner, 1)
    strips, saved, done = pl.pallas_call(
        middle_kernel,
        out_shape=(
            tiles(2 * (fields + 1)),
            tiles(4 * (STEPS - 1) * fields),
            tiles((rows - 2 * STEPS) * fields),
        ),
        in_specs=[VMEM] * 7,
        out_specs=(VMEM,) * 3,
        scratch_shapes=[room(rows * fields), room(rows * fields)],
        compiler_params=MODEST,
        cost_estimate=pl.CostEstimate(
            flops=30 * rows * fields * levels * cols * STEPS, bytes_accessed=2**20, transcendentals=0
        ),
        name="middle",
    )(states, start, inner, other, metric, side, beside)
    out = pl.pallas_call(
        functools.partial(outer_kernel, sizes),
        out_shape=jax.ShapeDtypeStruct((fields * levels, rows, cols), jnp.float32),
        in_specs=[VMEM] * 7,
        out_specs=HBM,
        scratch_shapes=[pltpu.VMEM(flat, jnp.float32), pltpu.SemaphoreType.DMA((2,))],
        compiler_params=MODEST,
        name="outer",
    )(start, strips, saved, done, metric, first_in, second_in)
    return out.reshape(perturbed_states.shape)


def solution(mesh):
    placed = (
        P("member", None, None, "dx", "dy"),
        P("member", None, None, "dx", "dy"),
        P(),
        P("dx", "dy"),
        P("dx", "dy"),
    )
    return jax.shard_map(
        on_device,
        mesh=mesh,
        in_specs=placed,
        out_specs=P("member", None, None, "dx", "dy"),
        check_vma=False,
    )
```

time: 22.6 us -> 19.8 us (0.88)
  waiting for transfers between devices: 11.5 us -> 7.5 us
  Pallas kernels: 4.3 us -> 4.88 us
  starting transfers between devices: 6.64 us -> 7.1 us
    ppermute x7 -> x9, waiting for transfers between devices: 11.5 us -> 7.5 us  [send(): return lax.ppermute(value, AXES, pairs)]
    pallas_call x2 -> x3, Pallas kernels: 2.78 us -> 3.32 us  [the longest x1 1.83 us: on_device(): pl.pallas_call(functools.partial(outer_kernel, sizes), out_shape=jax.Shap...]
    ppermute x7 -> x9, starting transfers between devices: 6.64 us -> 7.1 us  [send(): return lax.ppermute(value, AXES, pairs)]
  transfers between devices with their start and end apart: 7 -> 9, of which waited for: 6 -> 6; matrix products, arithmetic and copies ran while one was open for 0% -> 0% of each run, Pallas kernels for 0% -> 8%
where the time goes in v3:
time: 19.8 us; the launch traced here: 19.6 us
  waiting for transfers between devices  7.5 us (38%)
  starting transfers between devices  7.1 us (36%)
  Pallas kernels  4.88 us (25%)
    ppermute x9, waiting for transfers between devices, send(): return lax.ppermute(value, AXES, pairs)  7.5 us
    ppermute x9, starting transfers between devices, send(): return lax.ppermute(value, AXES, pairs)  7.1 us
    pallas_call x1, Pallas kernels, on_device(): pl.pallas_call(functools.partial(outer_kernel, sizes), out_shape=jax.Shap...  1.83 us
    pallas_call x1, Pallas kernels, on_device(): pl.pallas_call(split_kernel, out_shape=(tiles(rows * fields), tiles(half...  1.56 us
    pallas_call x1, Pallas kernels, on_device(): pl.pallas_call(middle_kernel, out_shape=(tiles(2 * (fields + 1)), tiles(4...  1.29 us
  transfers between devices with their start and end apart: 9, of which 6 were waited for; matrix products, arithmetic and copies ran while one was open for 0% of the time, Pallas kernels for 8%

profile of v3, /device:TPU:0, one launch (start us, length us, event | category | flops | bytes accessed | tf_op | source)
XLA Modules:
  0.0 19.6 jit_solution(18071061134644020741)
XLA Ops:
  0.0 1.6 %split.1 = (f32[64,8,128]{2,1,0:T(8,128)S(1)}, f32[32,8,128]{2,1,0:T(8,128)S(1)}, f32[32,8,128]{2,1,0:T(8,128)S(1)}, f32[4,8,128]{2,1,0:T(8,128)S(1)}, f32[9,8,128]{2,1,0:T(8,128)S(1)}, /*index=5*/f32[32,128]{1,0:T(8,128)S(1)}) custom-call(f32[4,128,128]{2,1,0:T(8,128)} %bitcast.3, f32[4,128,128]{2,1,0:T(8,128)} %bitcast.4, s32[4]{0:T(128)} %owner_hbm.1, ...), custom_call_target="tpu_custom_call" | custom-call | tf_op jit(solution)/shard_map/split/pallas_call | solution.py:473
  1.6 0.5 %collective-permute-start = (f32[32,8,128]{2,1,0:T(8,128)S(1)}, f32[32,8,128]{2,1,0:T(8,128)S(1)}, u32[]{:S(2)}, u32[]{:S(2)}) collective-permute-start(f32[32,8,128]{2,1,0:T(8,128)S(1)} %get-tuple-element.21), channel_id=1, source_target_pairs={{0,8},{1,9},{2,10},{3,11},{4,12},{5,13},{6,14},{7,15},{8,0},{9,1},... | collective-permute-start | bytes 393224 | tf_op jit(solution)/shard_map/ppermute | solution.py:35
  2.1 3.5 %collective-permute-start.3 = (f32[4,8,128]{2,1,0:T(8,128)S(1)}, f32[4,8,128]{2,1,0:T(8,128)S(1)}, u32[]{:S(2)}, u32[]{:S(2)}) collective-permute-start(f32[4,8,128]{2,1,0:T(8,128)S(1)} %get-tuple-element.23), channel_id=1, source_target_pairs={{0,17},{1,16},{2,19},{3,18},{4,21},{5,20},{6,23},{7,22},{8,25},{9,... | collective-permute-start | bytes 49160 | tf_op jit(solution)/shard_map/ppermute | solution.py:35
  5.6 0.5 %collective-permute-start.2 = (f32[9,8,128]{2,1,0:T(8,128)S(1)}, f32[9,8,128]{2,1,0:T(8,128)S(1)}, u32[]{:S(2)}, u32[]{:S(2)}) collective-permute-start(f32[9,8,128]{2,1,0:T(8,128)S(1)} %get-tuple-element.22.side_ref), channel_id=1, source_target_pairs={{0,1},{1,0},{2,3},{3,2},{4,5},{5,4},{6,7},{7,6},{8,9},{9,8},{10,11... | collective-permute-start | bytes 110600 | tf_op jit(solution)/shard_map/ppermute | solution.py:35
  6.1 0.0 collective-permute-done
  6.2 0.2 collective-permute-start.1
  6.3 1.0 %collective-permute-done.3 = f32[4,8,128]{2,1,0:T(8,128)S(1)} collective-permute-done((f32[4,8,128]{2,1,0:T(8,128)S(1)}, f32[4,8,128]{2,1,0:T(8,128)S(1)}, u32[]{:S(2)}, u32[]{:S(2)}) %collective-permute-start.3) | collective-permute-done | bytes 16416 | tf_op jit(solution)/shard_map/ppermute | solution.py:35
  7.3 2.2 %collective-permute-done.2.refs_0_ = f32[9,8,128]{2,1,0:T(8,128)S(1)} collective-permute-done((f32[9,8,128]{2,1,0:T(8,128)S(1)}, f32[9,8,128]{2,1,0:T(8,128)S(1)}, u32[]{:S(2)}, u32[]{:S(2)}) %collective-permute-start.2) | collective-permute-done | bytes 36896 | tf_op jit(solution)/shard_map/ppermute | solution.py:35
  9.6 0.9 %collective-permute-done.1 = f32[16,8,128]{2,1,0:T(8,128)S(1)} collective-permute-done((f32[16,8,128]{2,1,0:T(8,128)S(1)}, f32[16,8,128]{2,1,0:T(8,128)S(1)}, u32[]{:S(2)}, u32[]{:S(2)}) %collective-permute-start.1) | collective-permute-done | bytes 65568 | tf_op jit(solution)/shard_map/ppermute | solution.py:35
  10.5 0.1 collective-permute-start.4
  10.6 0.2 collective-permute-start.5
  10.8 1.1 %collective-permute-done.4.other_ref = f32[20,8,128]{2,1,0:T(8,128)S(1)} collective-permute-done((f32[20,8,128]{2,1,0:T(8,128)S(1)}, f32[20,8,128]{2,1,0:T(8,128)S(1)}, u32[]{:S(2)}, u32[]{:S(2)}) %collective-permute-start.4) | collective-permute-done | bytes 81952 | tf_op jit(solution)/shard_map/ppermute | solution.py:35
  11.9 0.2 join.1
  12.1 0.2 collective-permute-start.8
  12.2 1.9 %collective-permute-start.7 = (f32[22,8,128]{2,1,0:T(8,128)S(1)}, f32[22,8,128]{2,1,0:T(8,128)S(1)}, u32[]{:S(2)}, u32[]{:S(2)}) collective-permute-start(f32[22,8,128]{2,1,0:T(8,128)S(1)} %get-tuple-element.26), channel_id=1, source_target_pairs={{0,2},{1,3},{2,4},{3,5},{4,6},{5,7},{6,14},{7,15},{8,0},{9,1},{10,... | collective-permute-start | bytes 270344 | tf_op jit(solution)/shard_map/ppermute | solution.py:35
  14.1 1.0 %collective-permute-done.5 = f32[16,8,128]{2,1,0:T(8,128)S(1)} collective-permute-done((f32[16,8,128]{2,1,0:T(8,128)S(1)}, f32[16,8,128]{2,1,0:T(8,128)S(1)}, u32[]{:S(2)}, u32[]{:S(2)}) %collective-permute-start.5) | collective-permute-done | bytes 65568 | tf_op jit(solution)/shard_map/ppermute | solution.py:35
  15.1 0.1 collective-permute-start.6
  15.2 1.2 %collective-permute-done.6.other_ref = f32[16,8,128]{2,1,0:T(8,128)S(1)} collective-permute-done((f32[16,8,128]{2,1,0:T(8,128)S(1)}, f32[16,8,128]{2,1,0:T(8,128)S(1)}, u32[]{:S(2)}, u32[]{:S(2)}) %collective-permute-start.6) | collective-permute-done | bytes 65568 | tf_op jit(solution)/shard_map/ppermute | solution.py:35
  16.4 1.3 %middle.1 = (f32[10,8,128]{2,1,0:T(8,128)S(1)}, f32[48,8,128]{2,1,0:T(8,128)S(1)}, f32[32,8,128]{2,1,0:T(8,128)S(1)}) custom-call(f32[64,8,128]{2,1,0:T(8,128)S(1)} %get-tuple-element.19.pt_ref, f32[32,8,128]{2,1,0:T(8,128)S(1)} %get-tuple-element.25.outer_ref, f32[16,8,128]{2,1,0:T(8,128)S(1)} %add.19.mine_ref, ...), custom_call_target="tpu_custom_call" | custom-call | flops 7864320 | bytes 1048576 | tf_op jit(solution)/shard_map/middle/pallas_call | solution.py:544
  17.7 0.0 collective-permute-done.8.second_ref
  17.8 0.0 collective-permute-done.7.first_ref
  17.8 1.8 %outer.1 = f32[32,16,128]{2,1,0:T(8,128)} custom-call(f32[32,8,128]{2,1,0:T(8,128)S(1)} %get-tuple-element.25.outer_ref, f32[10,8,128]{2,1,0:T(8,128)S(1)} %get-tuple-element.29.strip_ref, f32[48,8,128]{2,1,0:T(8,128)S(1)} %get-tuple-element.30.saved_ref, f32[32,8,128]{2,1,0:T(8,128)S(1)} %get-tuple-element.31.done_ref, ...), custom_call_target="tpu_custom_call" | custom-call | tf_op jit(solution)/shard_map/outer/pallas_call | solution.py:560
  (5 shorter events, 0.0 us)
Async XLA Ops:
  1.6 4.6 %collective-permute-start = (f32[32,8,128]{2,1,0:T(8,128)S(1)}, f32[32,8,128]{2,1,0:T(8,128)S(1)}, u32[]{:S(2)}, u32[]{:S(2)}) collective-permute-start(f32[32,8,128]{2,1,0:T(8,128)S(1)} %get-tuple-element.21), channel_id=1, source_target_pairs={{0,8},{1,9},{2,10},{3,11},{4,12},{5,13},{6,14},{7,15},{8,0},{9,1},... | collective-permute-start | bytes 393224 | tf_op jit(solution)/shard_map/ppermute | solution.py:35
  2.1 5.2 %collective-permute-start.3 = (f32[4,8,128]{2,1,0:T(8,128)S(1)}, f32[4,8,128]{2,1,0:T(8,128)S(1)}, u32[]{:S(2)}, u32[]{:S(2)}) collective-permute-start(f32[4,8,128]{2,1,0:T(8,128)S(1)} %get-tuple-element.23), channel_id=1, source_target_pairs={{0,17},{1,16},{2,19},{3,18},{4,21},{5,20},{6,23},{7,22},{8,25},{9,... | collective-permute-start | bytes 49160 | tf_op jit(solution)/shard_map/ppermute | solution.py:35
  5.6 4.0 %collective-permute-start.2 = (f32[9,8,128]{2,1,0:T(8,128)S(1)}, f32[9,8,128]{2,1,0:T(8,128)S(1)}, u32[]{:S(2)}, u32[]{:S(2)}) collective-permute-start(f32[9,8,128]{2,1,0:T(8,128)S(1)} %get-tuple-element.22.side_ref), channel_id=1, source_target_pairs={{0,1},{1,0},{2,3},{3,2},{4,5},{5,4},{6,7},{7,6},{8,9},{9,8},{10,11... | collective-permute-start | bytes 110600 | tf_op jit(solution)/shard_map/ppermute | solution.py:35
  6.2 4.3 %collective-permute-start.1 = (f32[16,8,128]{2,1,0:T(8,128)S(1)}, f32[16,8,128]{2,1,0:T(8,128)S(1)}, u32[]{:S(2)}, u32[]{:S(2)}) collective-permute-start(f32[16,8,128]{2,1,0:T(8,128)S(1)} %get-tuple-element.34), channel_id=1, source_target_pairs={{0,16},{1,17},{2,18},{3,19},{4,20},{5,21},{6,22},{7,23},{8,24},{9,... | collective-permute-start | bytes 196616 | tf_op jit(solution)/shard_map/ppermute | solution.py:35
  10.5 1.3 %collective-permute-start.4 = (f32[20,8,128]{2,1,0:T(8,128)S(1)}, f32[20,8,128]{2,1,0:T(8,128)S(1)}, u32[]{:S(2)}, u32[]{:S(2)}) collective-permute-start(f32[20,8,128]{2,1,0:T(8,128)S(1)} %pad_maximum_fusion), channel_id=1, source_target_pairs={{0,8},{1,9},{2,10},{3,11},{4,12},{5,13},{6,14},{7,15},{8,0},{9,1},... | collective-permute-start | bytes 245768 | tf_op jit(solution)/shard_map/ppermute | solution.py:35
  10.6 4.5 %collective-permute-start.5 = (f32[16,8,128]{2,1,0:T(8,128)S(1)}, f32[16,8,128]{2,1,0:T(8,128)S(1)}, u32[]{:S(2)}, u32[]{:S(2)}) collective-permute-start(f32[16,8,128]{2,1,0:T(8,128)S(1)} %get-tuple-element.33), channel_id=1, source_target_pairs={{0,16},{1,17},{2,18},{3,19},{4,20},{5,21},{6,22},{7,23},{8,24},{9,... | collective-permute-start | bytes 196616 | tf_op jit(solution)/shard_map/ppermute | solution.py:35
  12.1 5.7 %collective-permute-start.8 = (f32[22,8,128]{2,1,0:T(8,128)S(1)}, f32[22,8,128]{2,1,0:T(8,128)S(1)}, u32[]{:S(2)}, u32[]{:S(2)}) collective-permute-start(f32[22,8,128]{2,1,0:T(8,128)S(1)} %get-tuple-element.32), channel_id=1, source_target_pairs={{0,8},{1,9},{2,0},{3,1},{4,2},{5,3},{6,4},{7,5},{8,10},{9,11},{10,... | collective-permute-start | bytes 270344 | tf_op jit(solution)/shard_map/ppermute | solution.py:35
  12.2 5.5 %collective-permute-start.7 = (f32[22,8,128]{2,1,0:T(8,128)S(1)}, f32[22,8,128]{2,1,0:T(8,128)S(1)}, u32[]{:S(2)}, u32[]{:S(2)}) collective-permute-start(f32[22,8,128]{2,1,0:T(8,128)S(1)} %get-tuple-element.26), channel_id=1, source_target_pairs={{0,2},{1,3},{2,4},{3,5},{4,6},{5,7},{6,14},{7,15},{8,0},{9,1},{10,... | collective-permute-start | bytes 270344 | tf_op jit(solution)/shard_map/ppermute | solution.py:35
  15.1 1.3 %collective-permute-start.6 = (f32[16,8,128]{2,1,0:T(8,128)S(1)}, f32[16,8,128]{2,1,0:T(8,128)S(1)}, u32[]{:S(2)}, u32[]{:S(2)}) collective-permute-start(f32[16,8,128]{2,1,0:T(8,128)S(1)} %add.19.mine_ref), channel_id=1, source_target_pairs={{0,8},{1,9},{2,10},{3,11},{4,12},{5,13},{6,14},{7,15},{8,0},{9,1},... | collective-permute-start | bytes 196616 | tf_op jit(solution)/shard_map/ppermute | solution.py:35

commit v4 on v3

--- a/solution.py
+++ b/solution.py
@@ -50,7 +50,8 @@
 
 
 def turn(tile, by, axis=1):
-    return pltpu.roll(tile, by % tile.shape[axis], axis)
+    size = tile.shape[axis]
+    return pltpu.roll(tile, by % size if isinstance(by, int) else lax.rem(by, size), axis)
 
 
 def edges_of(tiles, width):
@@ -74,24 +75,33 @@
     member = lax.axis_index("member")
     members = owner_ref.shape[0]
     first = lax.rem(member, 2) == 0
-    copies = [pltpu.make_async_copy(owner_hbm, owner_ref, sems.at[0])]
+    copies = [
+        pltpu.make_async_copy(owner_hbm, owner_ref, sems.at[0]),
+        pltpu.make_async_copy(m_hbm, metric_ref.at[pl.ds(0, rows), :], sems.at[1]),
+        pltpu.make_async_copy(t_hbm, t_ref, sems.at[2]),
+    ]
     for f in range(fields):
-        copies.append(pltpu.make_async_copy(p_hbm.at[f], p_ref.at[f], sems.at[1 + 2 * f]))
-        copies.append(pltpu.make_async_copy(c_hbm.at[f], c_ref.at[f], sems.at[2 + 2 * f]))
-    copies.append(
-        pltpu.make_async_copy(m_hbm, metric_ref.at[pl.ds(0, rows), :], sems.at[1 + 2 * fields])
-    )
-    copies.append(pltpu.make_async_copy(t_hbm, t_ref, sems.at[2 + 2 * fields]))
+        copies.append(pltpu.make_async_copy(p_hbm.at[f], p_ref.at[f], sems.at[3 + 2 * f]))
+        copies.append(pltpu.make_async_copy(c_hbm.at[f], c_ref.at[f], sems.at[4 + 2 * f]))
     for copy in copies:
         copy.start()
-    copies[0].wait()
+    for copy in copies[:3]:
+        copy.wait()
+    metric_ref[pl.ds(rows, rows), :] = t_ref[...].astype(jnp.float32)
+    level = lax.broadcasted_iota(jnp.int32, (levels, cols), 0)
+    columns = []
+    for x in range(rows):
+        scale = jnp.broadcast_to(metric_ref[pl.ds(x, 1), :], (levels, cols))
+        ground = jnp.broadcast_to(metric_ref[pl.ds(rows + x, 1), :], (levels, cols))
+        columns.append(jnp.where(level == 0, scale, ground))
+    side_ref[2 * fields] = edges_of(columns, STEPS)
     weight = jnp.float32(0.0)
     for rank in range(members):
         per_rank = 2.0 * (members - rank) / (members * (members + 1.0))
         weight = weight + jnp.where(owner_ref[rank] == member, per_rank, 0.0)
     for f in range(fields):
-        copies[1 + 2 * f].wait()
-        copies[2 + 2 * f].wait()
+        copies[3 + 2 * f].wait()
+        copies[4 + 2 * f].wait()
         states, parts = [], []
         for x in range(rows):
             state = p_ref[f, pl.ds(x, levels, stride=rows), :]
@@ -105,16 +115,6 @@
         edge_ref[f] = edges_of(parts, STEPS)
         side_ref[f] = edge_ref[f]
         side_ref[fields + f] = edges_of(states, STEPS)
-    copies[-2].wait()
-    copies[-1].wait()
-    metric_ref[pl.ds(rows, rows), :] = t_ref[...].astype(jnp.float32)
-    level = lax.broadcasted_iota(jnp.int32, (levels, cols), 0)
-    columns = []
-    for x in range(rows):
-        scale = jnp.broadcast_to(metric_ref[pl.ds(x, 1), :], (levels, cols))
-        ground = jnp.broadcast_to(metric_ref[pl.ds(rows + x, 1), :], (levels, cols))
-        columns.append(jnp.where(level == 0, scale, ground))
-    side_ref[2 * fields] = edges_of(columns, STEPS)
 
 
 def has_neighbours(axis, size):
@@ -165,22 +165,31 @@
     return updated(level, coefs, cur, dx, sx, dy, sy)
 
 
-def strip_step(level, coefs, here, east, west):
+def strip_step(level, coefs, here, group):
     dx, sx, dy, sy = [], [], [], []
-    for f, tile in enumerate(here):
+    for tile in here:
+        east, west = turn(tile, -group), turn(tile, group)
         north, south = turn(tile, -1), turn(tile, 1)
-        dx.append(east[f] - west[f])
-        sx.append(east[f] + west[f])
+        dx.append(east - west)
+        sx.append(east + west)
         dy.append(north - south)
         sy.append(north + south)
     return updated(level, coefs, here, dx, sx, dy, sy)
 
 
-def outside_columns(lane, width, left, right):
-    return [
-        jnp.where(lax.rem(lane, 2 * width) == width - 1, a, turn(b, -2))
-        for a, b in zip(left, right)
-    ]
+def outside_columns(lane, width, strips, has_left):
+    place = lax.rem(lane, 2 * width)
+    if len(strips) == 2:
+        return [jnp.where(place == width - 1, a, turn(b, -2)) for a, b in zip(*strips)]
+    before = jnp.logical_and(place == width - 1, has_left)
+    after = jnp.logical_and(place == width - 2, jnp.logical_not(has_left))
+    return [jnp.where(before, a, jnp.where(after, turn(a, -2), 0.0)) for a in strips[0]]
+
+
+def strips_of(early, own, beside, has_left):
+    if len(beside) == 2:
+        return [jnp.where(early, beside[0], own), jnp.where(early, own, beside[1])]
+    return [jnp.where(early == has_left, beside[0], own)]
 
 
 def join_kernel(
@@ -196,6 +205,7 @@
     lane = lanes_of((levels, cols))
     early = lax.rem(lane, 2 * wide) < wide
     quarter = 2 * wide * wide
+    sides = beside_ref.shape[0] // (fields + 1)
 
     for r in range(wide):
         for f in range(fields):
@@ -205,43 +215,48 @@
             end = 2 * wide - 1 - r
             start_ref[end * fields + f] = pt_ref[(rows - 1 - r) * fields + f] + high
 
-    def ends_of(a, b):
-        return jnp.where(
-            lane < quarter,
-            a,
+    def ends_of(strips, up):
+        if sides == 1:
+            packed = None
+            for f in range(fields):
+                moved = turn(strips[f][0], jnp.where(up, quarter, 0) + f * quarter)
+                packed = moved if f == 0 else jnp.where(lane < f * quarter, packed, moved)
+            return [packed, strips[fields][0]]
+        return [
             jnp.where(
-                lane < 2 * quarter,
-                turn(b, quarter),
-                jnp.where(lane < cols - quarter, turn(b, -quarter), a),
-            ),
-        )
-
-    ends = []
-    far = 0 if n_sides == 1 else 1
+                lane < quarter,
+                a,
+                jnp.where(
+                    lane < 2 * quarter,
+                    turn(b, quarter),
+                    jnp.where(lane < cols - quarter, turn(b, -quarter), a),
+                ),
+            )
+            for a, b in strips
+        ]
+
+    strips = []
     for f in range(fields + 1):
+        beside = []
+        for side in range(sides):
+            if f < fields:
+                k = side * fields + f
+                value = near[side][fields + f] + (edge_ref[k] + other_ref[wide * fields + k])
+            else:
+                value = near[side][2 * fields]
+            if sides == 2:
+                value = jnp.where((has_left, has_right)[side], value, 0.0 if f < fields else OUTSIDE)
+            beside.append(value)
+            beside_ref[side * (fields + 1) + f] = value
         if f < fields:
-            own_rows = {}
-            for r in range(wide):
-                own_rows[r] = start_ref[r * fields + f]
-                own_rows[rows - 1 - r] = start_ref[(2 * wide - 1 - r) * fields + f]
             own = None
-            for x in sorted(own_rows):
-                moved = turn(own_rows[x], 2 * wide * x + wide)
+            for k in range(2 * wide):
+                x = k if k < wide else rows - 2 * wide + k
+                moved = turn(start_ref[k * fields + f], 2 * wide * x + wide)
                 own = moved if own is None else jnp.where(lane < 2 * wide * x, own, moved)
-            sums = []
-            for side in (0, far):
-                k = side * fields + f
-                total = edge_ref[k] + other_ref[wide * fields + k]
-                sums.append(near[side][fields + f] + total)
-            before = jnp.where(has_left, sums[0], 0.0)
-            after = jnp.where(has_right, sums[1], 0.0)
         else:
             own = side_ref[2 * fields]
-            before = jnp.where(has_left, near[0][2 * fields], OUTSIDE)
-            after = jnp.where(has_right, near[far][2 * fields], OUTSIDE)
-        beside_ref[f] = before
-        beside_ref[fields + 1 + f] = after
-        ends.append(ends_of(jnp.where(early, before, own), jnp.where(early, own, after)))
+        strips.append(strips_of(early, own, beside, has_left))
     scale, ground = metric_ref[pl.ds(0, rows), :], metric_ref[pl.ds(rows, rows), :]
     tops = jnp.concatenate([scale[rows - wide :], ground[rows - wide :]], axis=0)
     bottoms = jnp.concatenate([scale[:wide], ground[:wide]], axis=0)
@@ -249,13 +264,13 @@
         base = jnp.where(up, wide, 0) * fields
         for k in range(wide * fields):
             message[k] = start_ref[base + k]
-        for k, end in enumerate(ends):
-            message[wide * fields + k] = end
-        message[wide * fields + fields + 1] = jnp.where(up, tops, bottoms)
+        message[wide * fields] = jnp.where(up, tops, bottoms)
+        for k, end in enumerate(ends_of(strips, up)):
+            message[wide * fields + 1 + k] = end
 
 
 def middle_kernel(
-    pt_ref, outer_ref, mine_ref, other_ref, metric_ref, side_ref, beside_ref,
+    sizes, pt_ref, outer_ref, mine_ref, other_ref, metric_ref, side_ref, beside_ref,
     strip_ref, saved_ref, done_ref, a_ref, b_ref,
 ):
     rows, cols = metric_ref.shape[0] // 2, metric_ref.shape[1]
@@ -280,25 +295,27 @@
             a_ref[r * fields + f] = pt_ref[r * fields + f] + low
             mirrored = (rows - 1 - r) * fields + f
             a_ref[mirrored] = pt_ref[mirrored] + high
-    left, right = [], []
+    has_left, _ = has_neighbours("dy", sizes[2])
+    sides = beside_ref.shape[0] // (fields + 1)
+    strips = [[] for _ in range(sides)]
     for f in range(fields + 1):
         if f < fields:
             own = edges_of([a_ref[x * fields + f] for x in range(rows)], wide)
         else:
             own = side_ref[2 * fields]
-        left.append(jnp.where(early, beside_ref[f], own))
-        right.append(jnp.where(early, own, beside_ref[fields + 1 + f]))
-        strip_ref[f] = left[f]
-        strip_ref[fields + 1 + f] = right[f]
-    strip_coefs = [coefficients(level, side[fields][0:1], side[fields][1:2]) for side in (left, right)]
-    left, right = left[:fields], right[:fields]
+        beside = [beside_ref[side * (fields + 1) + f] for side in range(sides)]
+        for side, strip in enumerate(strips_of(early, own, beside, has_left)):
+            strips[side].append(strip)
+            strip_ref[side * (fields + 1) + f] = strip
+    strip_coefs = [coefficients(level, side[fields][0:1], side[fields][1:2]) for side in strips]
+    strips = [side[:fields] for side in strips]
     coefs = [
         coefficients(level, metric_ref[pl.ds(x, 1), :], metric_ref[pl.ds(rows + x, 1), :])
         for x in range(rows)
     ]
     for number in range(STEPS):
         source, sink = (a_ref, b_ref) if number % 2 == 0 else (b_ref, a_ref)
-        beyond = outside_columns(lane, wide, left, right)
+        beyond = outside_columns(lane, wide, strips, has_left)
         bottom, top = number + 1, rows - 1 - number
         row = lambda x: [source[x * fields + f] for f in range(fields)]
         before, cur = row(bottom - 1), row(bottom)
@@ -317,15 +334,8 @@
                         saved_ref[(4 * number + edge) * fields + f] = new[f]
             before, cur = cur, after
         if number < STEPS - 1:
-            left, right = [
-                strip_step(
-                    level,
-                    strip_coefs[side],
-                    tiles,
-                    [turn(tile, -group) for tile in tiles],
-                    [turn(tile, group) for tile in tiles],
-                )
-                for side, tiles in enumerate((left, right))
+            strips = [
+                strip_step(level, coef, tiles, group) for coef, tiles in zip(strip_coefs, strips)
             ]
 
 
@@ -351,55 +361,30 @@
     def high(k, empty=0.0):
         return jnp.where(has_high, jnp.where(even, second_ref[k], first_ref[k]), empty)
 
-    def stretched(k, empty):
-        mine_a = turn(strip_ref[k], quarter)
-        mine_b = turn(strip_ref[fields + 1 + k], quarter)
-        under, over = low(wide * fields + k, empty), high(wide * fields + k, empty)
-
-        def end(own, other):
-            return jnp.where(lane < quarter, own, jnp.where(lane < 2 * quarter, other, empty))
-
-        return (
-            (
-                jnp.where(lane < quarter, turn(under, quarter), mine_a),
-                end(mine_a, turn(over, quarter)),
-            ),
-            (
-                jnp.where(lane < quarter, turn(under, 2 * quarter), mine_b),
-                end(mine_b, over),
-            ),
-        )
-
-    by_field = [stretched(f, 0.0) for f in range(fields)]
-    strips = [[[by_field[f][side][v] for f in range(fields)] for v in range(2)] for side in range(2)]
-    strip_coefs = [
-        [coefficients(level, tile[0:1], tile[1:2]) for tile in side]
-        for side in stretched(fields, OUTSIDE)
-    ]
-    beyond = []
-    for number in range(STEPS):
-        beyond.append(
-            [outside_columns(lane, wide, strips[0][v], strips[1][v]) for v in range(2)]
-        )
-        if number == STEPS - 1:
-            break
-        new = []
-        for side, (one, two) in enumerate(strips):
-            ahead = [
-                [jnp.where(lane < cols - group, turn(p, -group), turn(q, -group)) for p, q in zip(one, two)],
-                [turn(q, -group) for q in two],
-            ]
-            behind = [
-                [turn(p, group) for p in one],
-                [jnp.where(lane < group, turn(p, group), turn(q, group)) for p, q in zip(one, two)],
-            ]
-            new.append(
-                [
-                    strip_step(level, strip_coefs[side][v], (one, two)[v], ahead[v], behind[v])
-                    for v in range(2)
-                ]
-            )
-        strips = new
+    has_left, _ = has_neighbours("dy", sizes[2])
+    sides = strip_ref.shape[0] // (fields + 1)
+
+    def stretched(is_low, side, f):
+        mine = strip_ref[side * (fields + 1) + f]
+        empty = 0.0 if f < fields else OUTSIDE
+        if sides == 1 and f < fields:
+            k, by = 0, (-f if is_low else -1 - f)
+        else:
+            k, by = min(f, 1) if sides == 1 else f, ((1, 2) if is_low else (-1, 2))[side]
+        theirs = turn((low if is_low else high)(wide * fields + 1 + k, empty), by * quarter)
+        if is_low:
+            return jnp.where(lane < quarter, theirs, turn(mine, quarter))
+        return jnp.where(lane < cols - quarter, turn(mine, -quarter), theirs)
+
+    beyond = {}
+    for is_low in (True, False):
+        strips = [[stretched(is_low, side, f) for f in range(fields + 1)] for side in range(sides)]
+        coefs = [coefficients(level, side[fields][0:1], side[fields][1:2]) for side in strips]
+        strips = [side[:fields] for side in strips]
+        for number in range(STEPS):
+            beyond[is_low, number] = outside_columns(lane, wide, strips, has_left)
+            if number < STEPS - 1:
+                strips = [strip_step(level, c, tiles, group) for c, tiles in zip(coefs, strips)]
 
     for x in range(wide, rows - wide):
         for f in range(fields):
@@ -409,7 +394,7 @@
         return [saved_ref[(4 * (number - 1) + edge) * fields + f] for f in range(fields)]
 
     def finish(is_low):
-        metric = wide * fields + fields + 1
+        metric = wide * fields
         halo = low(metric, OUTSIDE) if is_low else high(metric, OUTSIDE)
         coefs, state = {}, {}
         for r in range(wide):
@@ -433,10 +418,10 @@
             bottom = number + 1 - wide if is_low else rows - 1 - number
             new = {}
             for x in range(bottom, bottom + wide):
-                spot = group * (x + wide) + wide - 1
-                outside = beyond[number][spot // cols]
+                spot = group * (x + (wide if is_low else -wide)) + wide - 1
                 new[x] = row_step(
-                    level, lane, coefs[x], state[x - 1], state[x], state[x + 1], outside, spot % cols
+                    level, lane, coefs[x], state[x - 1], state[x], state[x + 1],
+                    beyond[is_low, number], spot,
                 )
             state = new
         for x, tiles in state.items():
@@ -525,13 +510,13 @@
     edges = jnp.concatenate(edges, axis=0)
     cut = STEPS * fields
     outer = over_chips(keep[:cut] + given[:cut])
-    inner = over_chips(keep[cut:] + given[cut:])
+    inner = over_chips(keep + given)[cut:]
 
     other = over_members(jnp.concatenate([outer, edges], axis=0), 1)
-    count = cut + fields + 2
+    count = cut + (3 if along == 2 else fields + 2)
     start, beside, first, second = pl.pallas_call(
         functools.partial(join_kernel, sizes, len(near)),
-        out_shape=(tiles(2 * cut), tiles(2 * (fields + 1)), tiles(count), tiles(count)),
+        out_shape=(tiles(2 * cut), tiles(len(near) * (fields + 1)), tiles(count), tiles(count)),
         in_specs=[VMEM] * (6 + len(near)),
         out_specs=(VMEM,) * 4,
         compiler_params=MODEST,
@@ -542,9 +527,9 @@
     inner, _ = lax.optimization_barrier((inner, first))
     other = over_members(inner, 1)
     strips, saved, done = pl.pallas_call(
-        middle_kernel,
+        functools.partial(middle_kernel, sizes),
         out_shape=(
-            tiles(2 * (fields + 1)),
+            tiles(len(near) * (fields + 1)),
             tiles(4 * (STEPS - 1) * fields),
             tiles((rows - 2 * STEPS) * fields),
         ),

time: 19.8 us -> 18.9 us (0.955)
  waiting for transfers between devices: 7.5 us -> 6.62 us
  starting transfers between devices: 7.1 us -> 7.49 us
  Pallas kernels: 4.88 us -> 4.49 us
    ppermute x9, waiting for transfers between devices: 7.5 us -> 6.62 us  [send(): return lax.ppermute(value, AXES, pairs)]
    ppermute x9, starting transfers between devices: 7.1 us -> 7.49 us  [send(): return lax.ppermute(value, AXES, pairs)]
    pallas_call x1, Pallas kernels: 1.83 us -> 1.57 us  [on_device(): pl.pallas_call(functools.partial(outer_kernel, sizes), out_shape=jax.Shap...]
where the time goes in v4:
time: 18.9 us; the launch traced here: 18.7 us
  starting transfers between devices  7.49 us (40%)
  waiting for transfers between devices  6.62 us (35%)
  Pallas kernels  4.49 us (24%)
    ppermute x9, starting transfers between devices, send(): return lax.ppermute(value, AXES, pairs)  7.49 us
    ppermute x9, waiting for transfers between devices, send(): return lax.ppermute(value, AXES, pairs)  6.62 us
    pallas_call x1, Pallas kernels, on_device(): pl.pallas_call(functools.partial(outer_kernel, sizes), out_shape=jax.Shap...  1.57 us
    pallas_call x1, Pallas kernels, on_device(): pl.pallas_call(split_kernel, out_shape=(tiles(rows * fields), tiles(half...  1.49 us
    pallas_call x1, Pallas kernels, on_device(): pl.pallas_call(functools.partial(middle_kernel, sizes), out_shape=(tiles(...  1.24 us
  transfers between devices with their start and end apart: 9, of which 6 were waited for; matrix products, arithmetic and copies ran while one was open for 0% of the time, Pallas kernels for 8%

profile of v4, /device:TPU:0, one launch (start us, length us, event | category | flops | bytes accessed | tf_op | source)
XLA Modules:
  0.0 18.7 jit_solution(1191767752295668023)
XLA Ops:
  0.0 1.5 %split.1 = (f32[64,8,128]{2,1,0:T(8,128)S(1)}, f32[32,8,128]{2,1,0:T(8,128)S(1)}, f32[32,8,128]{2,1,0:T(8,128)S(1)}, f32[4,8,128]{2,1,0:T(8,128)S(1)}, f32[9,8,128]{2,1,0:T(8,128)S(1)}, /*index=5*/f32[32,128]{1,0:T(8,128)S(1)}) custom-call(f32[4,128,128]{2,1,0:T(8,128)} %bitcast.3, f32[4,128,128]{2,1,0:T(8,128)} %bitcast.4, s32[4]{0:T(128)} %owner_hbm.1, ...), custom_call_target="tpu_custom_call" | custom-call | tf_op jit(solution)/shard_map/split/pallas_call | solution.py:458
  1.5 0.5 %collective-permute-start = (f32[32,8,128]{2,1,0:T(8,128)S(1)}, f32[32,8,128]{2,1,0:T(8,128)S(1)}, u32[]{:S(2)}, u32[]{:S(2)}) collective-permute-start(f32[32,8,128]{2,1,0:T(8,128)S(1)} %get-tuple-element.21), channel_id=1, source_target_pairs={{0,8},{1,9},{2,10},{3,11},{4,12},{5,13},{6,14},{7,15},{8,0},{9,1},... | collective-permute-start | bytes 393224 | tf_op jit(solution)/shard_map/ppermute | solution.py:35
  2.0 3.5 %collective-permute-start.3 = (f32[4,8,128]{2,1,0:T(8,128)S(1)}, f32[4,8,128]{2,1,0:T(8,128)S(1)}, u32[]{:S(2)}, u32[]{:S(2)}) collective-permute-start(f32[4,8,128]{2,1,0:T(8,128)S(1)} %get-tuple-element.23), channel_id=1, source_target_pairs={{0,17},{1,16},{2,19},{3,18},{4,21},{5,20},{6,23},{7,22},{8,25},{9,... | collective-permute-start | bytes 49160 | tf_op jit(solution)/shard_map/ppermute | solution.py:35
  5.5 0.5 %collective-permute-start.2 = (f32[9,8,128]{2,1,0:T(8,128)S(1)}, f32[9,8,128]{2,1,0:T(8,128)S(1)}, u32[]{:S(2)}, u32[]{:S(2)}) collective-permute-start(f32[9,8,128]{2,1,0:T(8,128)S(1)} %get-tuple-element.22.side_ref), channel_id=1, source_target_pairs={{0,1},{1,0},{2,3},{3,2},{4,5},{5,4},{6,7},{7,6},{8,9},{9,8},{10,11... | collective-permute-start | bytes 110600 | tf_op jit(solution)/shard_map/ppermute | solution.py:35
  6.1 0.0 collective-permute-done
  6.1 0.2 collective-permute-start.1
  6.3 1.0 %collective-permute-done.3 = f32[4,8,128]{2,1,0:T(8,128)S(1)} collective-permute-done((f32[4,8,128]{2,1,0:T(8,128)S(1)}, f32[4,8,128]{2,1,0:T(8,128)S(1)}, u32[]{:S(2)}, u32[]{:S(2)}) %collective-permute-start.3) | collective-permute-done | bytes 16416 | tf_op jit(solution)/shard_map/ppermute | solution.py:35
  7.3 2.2 %collective-permute-done.2.refs_0_ = f32[9,8,128]{2,1,0:T(8,128)S(1)} collective-permute-done((f32[9,8,128]{2,1,0:T(8,128)S(1)}, f32[9,8,128]{2,1,0:T(8,128)S(1)}, u32[]{:S(2)}, u32[]{:S(2)}) %collective-permute-start.2) | collective-permute-done | bytes 36896 | tf_op jit(solution)/shard_map/ppermute | solution.py:35
  9.5 0.6 %collective-permute-start.5 = (f32[32,8,128]{2,1,0:T(8,128)S(1)}, f32[32,8,128]{2,1,0:T(8,128)S(1)}, u32[]{:S(2)}, u32[]{:S(2)}) collective-permute-start(f32[32,8,128]{2,1,0:T(8,128)S(1)} %add.18), channel_id=1, source_target_pairs={{0,16},{1,17},{2,18},{3,19},{4,20},{5,21},{6,22},{7,23},{8,24},{9,... | collective-permute-start | bytes 393224 | tf_op jit(solution)/shard_map/ppermute | solution.py:35
  10.1 0.3 %collective-permute-done.1 = f32[16,8,128]{2,1,0:T(8,128)S(1)} collective-permute-done((f32[16,8,128]{2,1,0:T(8,128)S(1)}, f32[16,8,128]{2,1,0:T(8,128)S(1)}, u32[]{:S(2)}, u32[]{:S(2)}) %collective-permute-start.1) | collective-permute-done | bytes 65568 | tf_op jit(solution)/shard_map/ppermute | solution.py:35
  10.5 0.1 collective-permute-start.4
  10.5 1.3 %collective-permute-done.4.other_ref = f32[20,8,128]{2,1,0:T(8,128)S(1)} collective-permute-done((f32[20,8,128]{2,1,0:T(8,128)S(1)}, f32[20,8,128]{2,1,0:T(8,128)S(1)}, u32[]{:S(2)}, u32[]{:S(2)}) %collective-permute-start.4) | collective-permute-done | bytes 81952 | tf_op jit(solution)/shard_map/ppermute | solution.py:35
  11.8 0.2 join.1
  12.0 0.2 collective-permute-start.8
  12.1 1.9 %collective-permute-start.7 = (f32[19,8,128]{2,1,0:T(8,128)S(1)}, f32[19,8,128]{2,1,0:T(8,128)S(1)}, u32[]{:S(2)}, u32[]{:S(2)}) collective-permute-start(f32[19,8,128]{2,1,0:T(8,128)S(1)} %get-tuple-element.26), channel_id=1, source_target_pairs={{0,2},{1,3},{2,4},{3,5},{4,6},{5,7},{6,14},{7,15},{8,0},{9,1},{10,... | collective-permute-start | bytes 233480 | tf_op jit(solution)/shard_map/ppermute | solution.py:35
  14.0 0.5 %collective-permute-done.5 = f32[32,8,128]{2,1,0:T(8,128)S(1)} collective-permute-done((f32[32,8,128]{2,1,0:T(8,128)S(1)}, f32[32,8,128]{2,1,0:T(8,128)S(1)}, u32[]{:S(2)}, u32[]{:S(2)}) %collective-permute-start.5) | collective-permute-done | bytes 131104 | tf_op jit(solution)/shard_map/ppermute | solution.py:35
  14.6 0.1 collective-permute-start.6
  14.7 1.2 %collective-permute-done.6.other_ref = f32[16,8,128]{2,1,0:T(8,128)S(1)} collective-permute-done((f32[16,8,128]{2,1,0:T(8,128)S(1)}, f32[16,8,128]{2,1,0:T(8,128)S(1)}, u32[]{:S(2)}, u32[]{:S(2)}) %collective-permute-start.6) | collective-permute-done | bytes 65568 | tf_op jit(solution)/shard_map/ppermute | solution.py:35
  15.9 1.2 %middle.1 = (f32[5,8,128]{2,1,0:T(8,128)S(1)}, f32[48,8,128]{2,1,0:T(8,128)S(1)}, f32[32,8,128]{2,1,0:T(8,128)S(1)}) custom-call(f32[64,8,128]{2,1,0:T(8,128)S(1)} %get-tuple-element.19.pt_ref, f32[32,8,128]{2,1,0:T(8,128)S(1)} %get-tuple-element.25.outer_ref, f32[16,8,128]{2,1,0:T(8,128)S(1)} %slice_add_fusion.mine_ref, ...), custom_call_target="tpu_custom_call" | custom-call | flops 7864320 | bytes 1048576 | tf_op jit(solution)/shard_map/middle/pallas_call | solution.py:529
  17.1 0.0 collective-permute-done.8.second_ref
  17.1 0.0 collective-permute-done.7.first_ref
  17.2 1.6 %outer.1 = f32[32,16,128]{2,1,0:T(8,128)} custom-call(f32[32,8,128]{2,1,0:T(8,128)S(1)} %get-tuple-element.25.outer_ref, f32[5,8,128]{2,1,0:T(8,128)S(1)} %get-tuple-element.29.strip_ref, f32[48,8,128]{2,1,0:T(8,128)S(1)} %get-tuple-element.30.saved_ref, f32[32,8,128]{2,1,0:T(8,128)S(1)} %get-tuple-element.31.done_ref, ...), custom_call_target="tpu_custom_call" | custom-call | tf_op jit(solution)/shard_map/outer/pallas_call | solution.py:545
  (6 shorter events, 0.1 us)
Async XLA Ops:
  1.5 4.6 %collective-permute-start = (f32[32,8,128]{2,1,0:T(8,128)S(1)}, f32[32,8,128]{2,1,0:T(8,128)S(1)}, u32[]{:S(2)}, u32[]{:S(2)}) collective-permute-start(f32[32,8,128]{2,1,0:T(8,128)S(1)} %get-tuple-element.21), channel_id=1, source_target_pairs={{0,8},{1,9},{2,10},{3,11},{4,12},{5,13},{6,14},{7,15},{8,0},{9,1},... | collective-permute-start | bytes 393224 | tf_op jit(solution)/shard_map/ppermute | solution.py:35
  2.0 5.2 %collective-permute-start.3 = (f32[4,8,128]{2,1,0:T(8,128)S(1)}, f32[4,8,128]{2,1,0:T(8,128)S(1)}, u32[]{:S(2)}, u32[]{:S(2)}) collective-permute-start(f32[4,8,128]{2,1,0:T(8,128)S(1)} %get-tuple-element.23), channel_id=1, source_target_pairs={{0,17},{1,16},{2,19},{3,18},{4,21},{5,20},{6,23},{7,22},{8,25},{9,... | collective-permute-start | bytes 49160 | tf_op jit(solution)/shard_map/ppermute | solution.py:35
  5.5 4.0 %collective-permute-start.2 = (f32[9,8,128]{2,1,0:T(8,128)S(1)}, f32[9,8,128]{2,1,0:T(8,128)S(1)}, u32[]{:S(2)}, u32[]{:S(2)}) collective-permute-start(f32[9,8,128]{2,1,0:T(8,128)S(1)} %get-tuple-element.22.side_ref), channel_id=1, source_target_pairs={{0,1},{1,0},{2,3},{3,2},{4,5},{5,4},{6,7},{7,6},{8,9},{9,8},{10,11... | collective-permute-start | bytes 110600 | tf_op jit(solution)/shard_map/ppermute | solution.py:35
  6.1 4.3 %collective-permute-start.1 = (f32[16,8,128]{2,1,0:T(8,128)S(1)}, f32[16,8,128]{2,1,0:T(8,128)S(1)}, u32[]{:S(2)}, u32[]{:S(2)}) collective-permute-start(f32[16,8,128]{2,1,0:T(8,128)S(1)} %slice_add_fusion.1), channel_id=1, source_target_pairs={{0,16},{1,17},{2,18},{3,19},{4,20},{5,21},{6,22},{7,23},{8,24},{9,... | collective-permute-start | bytes 196616 | tf_op jit(solution)/shard_map/ppermute | solution.py:35
  9.5 5.0 %collective-permute-start.5 = (f32[32,8,128]{2,1,0:T(8,128)S(1)}, f32[32,8,128]{2,1,0:T(8,128)S(1)}, u32[]{:S(2)}, u32[]{:S(2)}) collective-permute-start(f32[32,8,128]{2,1,0:T(8,128)S(1)} %add.18), channel_id=1, source_target_pairs={{0,16},{1,17},{2,18},{3,19},{4,20},{5,21},{6,22},{7,23},{8,24},{9,... | collective-permute-start | bytes 393224 | tf_op jit(solution)/shard_map/ppermute | solution.py:35
  10.5 1.3 %collective-permute-start.4 = (f32[20,8,128]{2,1,0:T(8,128)S(1)}, f32[20,8,128]{2,1,0:T(8,128)S(1)}, u32[]{:S(2)}, u32[]{:S(2)}) collective-permute-start(f32[20,8,128]{2,1,0:T(8,128)S(1)} %pad_maximum_fusion), channel_id=1, source_target_pairs={{0,8},{1,9},{2,10},{3,11},{4,12},{5,13},{6,14},{7,15},{8,0},{9,1},... | collective-permute-start | bytes 245768 | tf_op jit(solution)/shard_map/ppermute | solution.py:35
  12.0 5.2 %collective-permute-start.8 = (f32[19,8,128]{2,1,0:T(8,128)S(1)}, f32[19,8,128]{2,1,0:T(8,128)S(1)}, u32[]{:S(2)}, u32[]{:S(2)}) collective-permute-start(f32[19,8,128]{2,1,0:T(8,128)S(1)} %get-tuple-element.32), channel_id=1, source_target_pairs={{0,8},{1,9},{2,0},{3,1},{4,2},{5,3},{6,4},{7,5},{8,10},{9,11},{10,... | collective-permute-start | bytes 233480 | tf_op jit(solution)/shard_map/ppermute | solution.py:35
  12.1 5.0 %collective-permute-start.7 = (f32[19,8,128]{2,1,0:T(8,128)S(1)}, f32[19,8,128]{2,1,0:T(8,128)S(1)}, u32[]{:S(2)}, u32[]{:S(2)}) collective-permute-start(f32[19,8,128]{2,1,0:T(8,128)S(1)} %get-tuple-element.26), channel_id=1, source_target_pairs={{0,2},{1,3},{2,4},{3,5},{4,6},{5,7},{6,14},{7,15},{8,0},{9,1},{10,... | collective-permute-start | bytes 233480 | tf_op jit(solution)/shard_map/ppermute | solution.py:35
  14.6 1.3 %collective-permute-start.6 = (f32[16,8,128]{2,1,0:T(8,128)S(1)}, f32[16,8,128]{2,1,0:T(8,128)S(1)}, u32[]{:S(2)}, u32[]{:S(2)}) collective-permute-start(f32[16,8,128]{2,1,0:T(8,128)S(1)} %slice_add_fusion.mine_ref), channel_id=1, source_target_pairs={{0,8},{1,9},{2,10},{3,11},{4,12},{5,13},{6,14},{7,15},{8,0},{9,1},... | collective-permute-start | bytes 196616 | tf_op jit(solution)/shard_map/ppermute | solution.py:35

commit v5 on v4

--- a/solution.py
+++ b/solution.py
@@ -51,7 +51,7 @@
 
 def turn(tile, by, axis=1):
     size = tile.shape[axis]
-    return pltpu.roll(tile, by % size if isinstance(by, int) else lax.rem(by, size), axis)
+    return pltpu.roll(tile, by % size if isinstance(by, int) else lax.rem(by + size, size), axis)
 
 
 def edges_of(tiles, width):
@@ -63,8 +63,28 @@
     return total
 
 
+def pack_of(fields, along):
+    return 2 if along == 2 and fields % 2 == 0 else 1
+
+
+def packed(edges, early, has_left, along):
+    if pack_of(len(edges), along) == 1:
+        return edges
+    by = jnp.where(has_left, -STEPS, STEPS)
+    return [
+        jnp.where(early == has_left, turn(b, by), a) for a, b in zip(edges[::2], edges[1::2])
+    ]
+
+
+def unpacked(tiles, fields, has_left, along):
+    if pack_of(fields, along) == 1:
+        return tiles
+    by = jnp.where(has_left, -STEPS, STEPS)
+    return [part for tile in tiles for part in (tile, turn(tile, by))]
+
+
 def split_kernel(
-    p_hbm, c_hbm, owner_hbm, m_hbm, t_hbm,
+    sizes, p_hbm, c_hbm, owner_hbm, m_hbm, t_hbm,
     pt_ref, keep_ref, send_ref, edge_ref, side_ref, metric_ref,
     p_ref, c_ref, owner_ref, t_ref, sems,
 ):
@@ -94,7 +114,8 @@
         scale = jnp.broadcast_to(metric_ref[pl.ds(x, 1), :], (levels, cols))
         ground = jnp.broadcast_to(metric_ref[pl.ds(rows + x, 1), :], (levels, cols))
         columns.append(jnp.where(level == 0, scale, ground))
-    side_ref[2 * fields] = edges_of(columns, STEPS)
+    side_ref[side_ref.shape[0] - 1] = edges_of(columns, STEPS)
+    part_edges, state_edges = [], []
     weight = jnp.float32(0.0)
     for rank in range(members):
         per_rank = 2.0 * (members - rank) / (members * (members + 1.0))
@@ -112,9 +133,15 @@
         for r in range(half):
             keep_ref[r * fields + f] = jnp.where(first, parts[r], parts[rows - 1 - r])
             send_ref[r * fields + f] = jnp.where(first, parts[rows - 1 - r], parts[r])
-        edge_ref[f] = edges_of(parts, STEPS)
-        side_ref[f] = edge_ref[f]
-        side_ref[fields + f] = edges_of(states, STEPS)
+        part_edges.append(edges_of(parts, STEPS))
+        state_edges.append(edges_of(states, STEPS))
+    early = lax.rem(lanes_of((levels, cols)), 2 * STEPS) < STEPS
+    has_left, _ = has_neighbours("dy", sizes[2])
+    for k, edge in enumerate(packed(part_edges, early, has_left, sizes[2])):
+        edge_ref[k] = edge
+        side_ref[k] = edge
+    for k, edge in enumerate(packed(state_edges, early, has_left, sizes[2])):
+        side_ref[edge_ref.shape[0] + k] = edge
 
 
 def has_neighbours(axis, size):
@@ -235,15 +262,23 @@
             for a, b in strips
         ]
 
+    per_side = edge_ref.shape[0] // sides
+    sums = [
+        unpacked(
+            [
+                near[side][per_side + k]
+                + (edge_ref[side * per_side + k] + other_ref[wide * fields + side * per_side + k])
+                for k in range(per_side)
+            ],
+            fields, has_left, sizes[2],
+        )
+        for side in range(sides)
+    ]
     strips = []
     for f in range(fields + 1):
         beside = []
         for side in range(sides):
-            if f < fields:
-                k = side * fields + f
-                value = near[side][fields + f] + (edge_ref[k] + other_ref[wide * fields + k])
-            else:
-                value = near[side][2 * fields]
+            value = sums[side][f] if f < fields else near[side][2 * per_side]
             if sides == 2:
                 value = jnp.where((has_left, has_right)[side], value, 0.0 if f < fields else OUTSIDE)
             beside.append(value)
@@ -255,7 +290,7 @@
                 moved = turn(start_ref[k * fields + f], 2 * wide * x + wide)
                 own = moved if own is None else jnp.where(lane < 2 * wide * x, own, moved)
         else:
-            own = side_ref[2 * fields]
+            own = side_ref[side_ref.shape[0] - 1]
         strips.append(strips_of(early, own, beside, has_left))
     scale, ground = metric_ref[pl.ds(0, rows), :], metric_ref[pl.ds(rows, rows), :]
     tops = jnp.concatenate([scale[rows - wide :], ground[rows - wide :]], axis=0)
@@ -302,7 +337,7 @@
         if f < fields:
             own = edges_of([a_ref[x * fields + f] for x in range(rows)], wide)
         else:
-            own = side_ref[2 * fields]
+            own = side_ref[side_ref.shape[0] - 1]
         beside = [beside_ref[side * (fields + 1) + f] for side in range(sides)]
         for side, strip in enumerate(strips_of(early, own, beside, has_left)):
             strips[side].append(strip)
@@ -441,11 +476,22 @@
         copy.wait()
 
 
+def pair_kernel(keep_ref, given_ref, outer_ref, inner_ref):
+    count, skip = outer_ref.shape[0], keep_ref.shape[0] - inner_ref.shape[0]
+    for k in range(keep_ref.shape[0]):
+        total = keep_ref[k] + given_ref[k]
+        if k < count:
+            outer_ref[k] = total
+        if k >= skip:
+            inner_ref[k - skip] = total
+
+
 def on_device(perturbed_states, control, owner, map_factor, terrain):
     _, fields, levels, rows, cols = perturbed_states.shape
     sizes = tuple(lax.axis_size(axis) for axis in AXES)
     members, along = sizes[0], sizes[2]
     half = rows // 2
+    n_edges = fields // pack_of(fields, along)
     tile = (levels, cols)
 
     def tiles(count):
@@ -456,13 +502,13 @@
 
     flat = (fields, levels * rows, cols)
     states, keep, give, edge, side, metric = pl.pallas_call(
-        split_kernel,
+        functools.partial(split_kernel, sizes),
         out_shape=(
             tiles(rows * fields),
             tiles(half * fields),
             tiles(half * fields),
-            tiles(fields),
-            tiles(2 * fields + 1),
+            tiles(n_edges),
+            tiles(2 * n_edges + 1),
             jax.ShapeDtypeStruct((2 * rows, cols), jnp.float32),
         ),
         in_specs=[HBM] * 5,
@@ -503,14 +549,22 @@
     near = [from_beside(side, step, 0) for step in steps]
     edges = []
     for step, n in zip(steps, near):
-        total = n[:fields]
+        total = n[:n_edges]
         for bit in range(2, members, 2):
             total = total + from_beside(edge, step, bit)
         edges.append(total)
     edges = jnp.concatenate(edges, axis=0)
     cut = STEPS * fields
-    outer = over_chips(keep[:cut] + given[:cut])
-    inner = over_chips(keep + given)[cut:]
+    outer, inner = pl.pallas_call(
+        pair_kernel,
+        out_shape=(tiles(cut), tiles(half * fields - cut + fields)),
+        in_specs=[VMEM] * 2,
+        out_specs=(VMEM,) * 2,
+        compiler_params=MODEST,
+        name="pair",
+    )(keep, given)
+    outer = over_chips(outer)
+    inner = over_chips(inner)[fields:]
 
     other = over_members(jnp.concatenate([outer, edges], axis=0), 1)
     count = cut + (3 if along == 2 else fields + 2)

time: 18.9 us -> 18.7 us (0.989)
  waiting for transfers between devices: 6.62 us -> 5.62 us
  starting transfers between devices: 7.49 us -> 8.27 us
    ppermute x9, waiting for transfers between devices: 6.62 us -> 5.62 us  [send(): return lax.ppermute(value, AXES, pairs)]
    ppermute x9, starting transfers between devices: 7.49 us -> 8.27 us  [send(): return lax.ppermute(value, AXES, pairs)]
    pallas_call x1 -> x2, Pallas kernels: 1.49 us -> 1.55 us  [the longest x1 1.53 us: on_device(): pl.pallas_call(functools.partial(split_kernel, sizes), out_shape=(tiles(r...]
  transfers between devices with their start and end apart: 9 -> 9, of which waited for: 6 -> 4; matrix products, arithmetic and copies ran while one was open for 0% -> 0% of each run, Pallas kernels for 8% -> 8%
where the time goes in v5:
time: 18.7 us; the launch traced here: 18.5 us
  starting transfers between devices  8.27 us (44%)
  waiting for transfers between devices  5.62 us (30%)
  Pallas kernels  4.54 us (24%)
    ppermute x9, starting transfers between devices, send(): return lax.ppermute(value, AXES, pairs)  8.27 us
    ppermute x9, waiting for transfers between devices, send(): return lax.ppermute(value, AXES, pairs)  5.62 us
    pallas_call x1, Pallas kernels, on_device(): pl.pallas_call(functools.partial(outer_kernel, sizes), out_shape=jax.Shap...  1.57 us
    pallas_call x1, Pallas kernels, on_device(): pl.pallas_call(functools.partial(split_kernel, sizes), out_shape=(tiles(r...  1.53 us
    pallas_call x1, Pallas kernels, on_device(): pl.pallas_call(functools.partial(middle_kernel, sizes), out_shape=(tiles(...  1.24 us
  transfers between devices with their start and end apart: 9, of which 4 were waited for; matrix products, arithmetic and copies ran while one was open for 0% of the time, Pallas kernels for 8%

profile of v5, /device:TPU:0, one launch (start us, length us, event | category | flops | bytes accessed | tf_op | source)
XLA Modules:
  0.0 18.5 jit_solution(808771737017250014)
XLA Ops:
  0.0 1.5 %split.1 = (f32[64,8,128]{2,1,0:T(8,128)S(1)}, f32[32,8,128]{2,1,0:T(8,128)S(1)}, f32[32,8,128]{2,1,0:T(8,128)S(1)}, f32[2,8,128]{2,1,0:T(8,128)S(1)}, f32[5,8,128]{2,1,0:T(8,128)S(1)}, /*index=5*/f32[32,128]{1,0:T(8,128)S(1)}) custom-call(f32[4,128,128]{2,1,0:T(8,128)} %bitcast.3, f32[4,128,128]{2,1,0:T(8,128)} %bitcast.4, s32[4]{0:T(128)} %owner_hbm.1, ...), custom_call_target="tpu_custom_call" | custom-call | tf_op jit(solution)/shard_map/split/pallas_call | solution.py:504
  1.5 0.5 %collective-permute-start = (f32[32,8,128]{2,1,0:T(8,128)S(1)}, f32[32,8,128]{2,1,0:T(8,128)S(1)}, u32[]{:S(2)}, u32[]{:S(2)}) collective-permute-start(f32[32,8,128]{2,1,0:T(8,128)S(1)} %get-tuple-element.23), channel_id=1, source_target_pairs={{0,8},{1,9},{2,10},{3,11},{4,12},{5,13},{6,14},{7,15},{8,0},{9,1},... | collective-permute-start | bytes 393224 | tf_op jit(solution)/shard_map/ppermute | solution.py:35
  2.1 2.6 %collective-permute-start.2 = (f32[5,8,128]{2,1,0:T(8,128)S(1)}, f32[5,8,128]{2,1,0:T(8,128)S(1)}, u32[]{:S(2)}, u32[]{:S(2)}) collective-permute-start(f32[5,8,128]{2,1,0:T(8,128)S(1)} %get-tuple-element.25.side_ref), channel_id=1, source_target_pairs={{0,1},{1,0},{2,3},{3,2},{4,5},{5,4},{6,7},{7,6},{8,9},{9,8},{10,11... | collective-permute-start | bytes 61448 | tf_op jit(solution)/shard_map/ppermute | solution.py:35
  4.6 1.5 %collective-permute-start.3 = (f32[2,8,128]{2,1,0:T(8,128)S(1)}, f32[2,8,128]{2,1,0:T(8,128)S(1)}, u32[]{:S(2)}, u32[]{:S(2)}) collective-permute-start(f32[2,8,128]{2,1,0:T(8,128)S(1)} %get-tuple-element.26), channel_id=1, source_target_pairs={{0,17},{1,16},{2,19},{3,18},{4,21},{5,20},{6,23},{7,22},{8,25},{9,... | collective-permute-start | bytes 24584 | tf_op jit(solution)/shard_map/ppermute | solution.py:35
  6.1 0.0 collective-permute-done.given_ref
  6.1 0.1 collective-permute-start.1
  6.3 3.0 %collective-permute-done.3 = f32[2,8,128]{2,1,0:T(8,128)S(1)} collective-permute-done((f32[2,8,128]{2,1,0:T(8,128)S(1)}, f32[2,8,128]{2,1,0:T(8,128)S(1)}, u32[]{:S(2)}, u32[]{:S(2)}) %collective-permute-start.3) | collective-permute-done | bytes 8224 | tf_op jit(solution)/shard_map/ppermute | solution.py:35
  9.3 0.0 collective-permute-done.2.refs_0_
  9.3 1.4 %collective-permute-start.5 = (f32[20,8,128]{2,1,0:T(8,128)S(1)}, f32[20,8,128]{2,1,0:T(8,128)S(1)}, u32[]{:S(2)}, u32[]{:S(2)}) collective-permute-start(f32[20,8,128]{2,1,0:T(8,128)S(1)} %get-tuple-element.29), channel_id=1, source_target_pairs={{0,16},{1,17},{2,18},{3,19},{4,20},{5,21},{6,22},{7,23},{8,24},{9,... | collective-permute-start | bytes 245768 | tf_op jit(solution)/shard_map/ppermute | solution.py:35
  10.7 0.0 collective-permute-done.1
  10.7 0.1 collective-permute-start.4
  10.8 1.3 %collective-permute-done.4.other_ref = f32[18,8,128]{2,1,0:T(8,128)S(1)} collective-permute-done((f32[18,8,128]{2,1,0:T(8,128)S(1)}, f32[18,8,128]{2,1,0:T(8,128)S(1)}, u32[]{:S(2)}, u32[]{:S(2)}) %collective-permute-start.4) | collective-permute-done | bytes 73760 | tf_op jit(solution)/shard_map/ppermute | solution.py:35
  12.1 0.2 join.1
  12.2 0.2 collective-permute-start.8
  12.4 1.9 %collective-permute-start.7 = (f32[19,8,128]{2,1,0:T(8,128)S(1)}, f32[19,8,128]{2,1,0:T(8,128)S(1)}, u32[]{:S(2)}, u32[]{:S(2)}) collective-permute-start(f32[19,8,128]{2,1,0:T(8,128)S(1)} %get-tuple-element.30), channel_id=1, source_target_pairs={{0,2},{1,3},{2,4},{3,5},{4,6},{5,7},{6,14},{7,15},{8,0},{9,1},{10,... | collective-permute-start | bytes 233480 | tf_op jit(solution)/shard_map/ppermute | solution.py:35
  14.3 0.0 collective-permute-done.5
  14.3 0.1 collective-permute-start.6
  14.4 1.2 %collective-permute-done.6.other_ref = f32[16,8,128]{2,1,0:T(8,128)S(1)} collective-permute-done((f32[16,8,128]{2,1,0:T(8,128)S(1)}, f32[16,8,128]{2,1,0:T(8,128)S(1)}, u32[]{:S(2)}, u32[]{:S(2)}) %collective-permute-start.6) | collective-permute-done | bytes 65568 | tf_op jit(solution)/shard_map/ppermute | solution.py:35
  15.6 1.2 %middle.1 = (f32[5,8,128]{2,1,0:T(8,128)S(1)}, f32[48,8,128]{2,1,0:T(8,128)S(1)}, f32[32,8,128]{2,1,0:T(8,128)S(1)}) custom-call(f32[64,8,128]{2,1,0:T(8,128)S(1)} %get-tuple-element.21.pt_ref, f32[32,8,128]{2,1,0:T(8,128)S(1)} %get-tuple-element.28.outer_ref, f32[16,8,128]{2,1,0:T(8,128)S(1)} %slice_add_fusion.mine_ref, ...), custom_call_target="tpu_custom_call" | custom-call | flops 7864320 | bytes 1048576 | tf_op jit(solution)/shard_map/middle/pallas_call | solution.py:583
  16.9 0.1 collective-permute-done.8.second_ref
  16.9 0.0 collective-permute-done.7.first_ref
  17.0 1.6 %outer.1 = f32[32,16,128]{2,1,0:T(8,128)} custom-call(f32[32,8,128]{2,1,0:T(8,128)S(1)} %get-tuple-element.28.outer_ref, f32[5,8,128]{2,1,0:T(8,128)S(1)} %get-tuple-element.33.strip_ref, f32[48,8,128]{2,1,0:T(8,128)S(1)} %get-tuple-element.34.saved_ref, f32[32,8,128]{2,1,0:T(8,128)S(1)} %get-tuple-element.35.done_ref, ...), custom_call_target="tpu_custom_call" | custom-call | tf_op jit(solution)/shard_map/outer/pallas_call | solution.py:599
  (5 shorter events, 0.1 us)
Async XLA Ops:
  1.5 4.6 %collective-permute-start = (f32[32,8,128]{2,1,0:T(8,128)S(1)}, f32[32,8,128]{2,1,0:T(8,128)S(1)}, u32[]{:S(2)}, u32[]{:S(2)}) collective-permute-start(f32[32,8,128]{2,1,0:T(8,128)S(1)} %get-tuple-element.23), channel_id=1, source_target_pairs={{0,8},{1,9},{2,10},{3,11},{4,12},{5,13},{6,14},{7,15},{8,0},{9,1},... | collective-permute-start | bytes 393224 | tf_op jit(solution)/shard_map/ppermute | solution.py:35
  2.1 7.2 %collective-permute-start.2 = (f32[5,8,128]{2,1,0:T(8,128)S(1)}, f32[5,8,128]{2,1,0:T(8,128)S(1)}, u32[]{:S(2)}, u32[]{:S(2)}) collective-permute-start(f32[5,8,128]{2,1,0:T(8,128)S(1)} %get-tuple-element.25.side_ref), channel_id=1, source_target_pairs={{0,1},{1,0},{2,3},{3,2},{4,5},{5,4},{6,7},{7,6},{8,9},{9,8},{10,11... | collective-permute-start | bytes 61448 | tf_op jit(solution)/shard_map/ppermute | solution.py:35
  4.6 4.7 %collective-permute-start.3 = (f32[2,8,128]{2,1,0:T(8,128)S(1)}, f32[2,8,128]{2,1,0:T(8,128)S(1)}, u32[]{:S(2)}, u32[]{:S(2)}) collective-permute-start(f32[2,8,128]{2,1,0:T(8,128)S(1)} %get-tuple-element.26), channel_id=1, source_target_pairs={{0,17},{1,16},{2,19},{3,18},{4,21},{5,20},{6,23},{7,22},{8,25},{9,... | collective-permute-start | bytes 24584 | tf_op jit(solution)/shard_map/ppermute | solution.py:35
  6.1 4.6 %collective-permute-start.1 = (f32[16,8,128]{2,1,0:T(8,128)S(1)}, f32[16,8,128]{2,1,0:T(8,128)S(1)}, u32[]{:S(2)}, u32[]{:S(2)}) collective-permute-start(f32[16,8,128]{2,1,0:T(8,128)S(1)} %get-tuple-element.24), channel_id=1, source_target_pairs={{0,16},{1,17},{2,18},{3,19},{4,20},{5,21},{6,22},{7,23},{8,24},{9,... | collective-permute-start | bytes 196616 | tf_op jit(solution)/shard_map/ppermute | solution.py:35
  9.3 5.0 %collective-permute-start.5 = (f32[20,8,128]{2,1,0:T(8,128)S(1)}, f32[20,8,128]{2,1,0:T(8,128)S(1)}, u32[]{:S(2)}, u32[]{:S(2)}) collective-permute-start(f32[20,8,128]{2,1,0:T(8,128)S(1)} %get-tuple-element.29), channel_id=1, source_target_pairs={{0,16},{1,17},{2,18},{3,19},{4,20},{5,21},{6,22},{7,23},{8,24},{9,... | collective-permute-start | bytes 245768 | tf_op jit(solution)/shard_map/ppermute | solution.py:35
  10.7 1.3 %collective-permute-start.4 = (f32[18,8,128]{2,1,0:T(8,128)S(1)}, f32[18,8,128]{2,1,0:T(8,128)S(1)}, u32[]{:S(2)}, u32[]{:S(2)}) collective-permute-start(f32[18,8,128]{2,1,0:T(8,128)S(1)} %pad_maximum_fusion), channel_id=1, source_target_pairs={{0,8},{1,9},{2,10},{3,11},{4,12},{5,13},{6,14},{7,15},{8,0},{9,1},... | collective-permute-start | bytes 221192 | tf_op jit(solution)/shard_map/ppermute | solution.py:35
  12.2 4.7 %collective-permute-start.8 = (f32[19,8,128]{2,1,0:T(8,128)S(1)}, f32[19,8,128]{2,1,0:T(8,128)S(1)}, u32[]{:S(2)}, u32[]{:S(2)}) collective-permute-start(f32[19,8,128]{2,1,0:T(8,128)S(1)} %get-tuple-element.36), channel_id=1, source_target_pairs={{0,8},{1,9},{2,0},{3,1},{4,2},{5,3},{6,4},{7,5},{8,10},{9,11},{10,... | collective-permute-start | bytes 233480 | tf_op jit(solution)/shard_map/ppermute | solution.py:35
  12.4 4.5 %collective-permute-start.7 = (f32[19,8,128]{2,1,0:T(8,128)S(1)}, f32[19,8,128]{2,1,0:T(8,128)S(1)}, u32[]{:S(2)}, u32[]{:S(2)}) collective-permute-start(f32[19,8,128]{2,1,0:T(8,128)S(1)} %get-tuple-element.30), channel_id=1, source_target_pairs={{0,2},{1,3},{2,4},{3,5},{4,6},{5,7},{6,14},{7,15},{8,0},{9,1},{10,... | collective-permute-start | bytes 233480 | tf_op jit(solution)/shard_map/ppermute | solution.py:35
  14.3 1.3 %collective-permute-start.6 = (f32[16,8,128]{2,1,0:T(8,128)S(1)}, f32[16,8,128]{2,1,0:T(8,128)S(1)}, u32[]{:S(2)}, u32[]{:S(2)}) collective-permute-start(f32[16,8,128]{2,1,0:T(8,128)S(1)} %slice_add_fusion.mine_ref), channel_id=1, source_target_pairs={{0,8},{1,9},{2,10},{3,11},{4,12},{5,13},{6,14},{7,15},{8,0},{9,1},... | collective-permute-start | bytes 196616 | tf_op jit(solution)/shard_map/ppermute | solution.py:35

commit v6 on v5

--- a/solution.py
+++ b/solution.py
@@ -100,9 +100,11 @@
         pltpu.make_async_copy(m_hbm, metric_ref.at[pl.ds(0, rows), :], sems.at[1]),
         pltpu.make_async_copy(t_hbm, t_ref, sems.at[2]),
     ]
-    for f in range(fields):
-        copies.append(pltpu.make_async_copy(p_hbm.at[f], p_ref.at[f], sems.at[3 + 2 * f]))
-        copies.append(pltpu.make_async_copy(c_hbm.at[f], c_ref.at[f], sems.at[4 + 2 * f]))
+    together = 2 if fields % 2 == 0 else 1
+    for n in range(fields // together):
+        some = pl.ds(n * together, together)
+        copies.append(pltpu.make_async_copy(p_hbm.at[some], p_ref.at[some], sems.at[3 + 2 * n]))
+        copies.append(pltpu.make_async_copy(c_hbm.at[some], c_ref.at[some], sems.at[4 + 2 * n]))
     for copy in copies:
         copy.start()
     for copy in copies[:3]:
@@ -121,8 +123,9 @@
         per_rank = 2.0 * (members - rank) / (members * (members + 1.0))
         weight = weight + jnp.where(owner_ref[rank] == member, per_rank, 0.0)
     for f in range(fields):
-        copies[3 + 2 * f].wait()
-        copies[4 + 2 * f].wait()
+        if f % together == 0:
+            copies[3 + 2 * (f // together)].wait()
+            copies[4 + 2 * (f // together)].wait()
         states, parts = [], []
         for x in range(rows):
             state = p_ref[f, pl.ds(x, levels, stride=rows), :]
@@ -428,7 +431,7 @@
     def saved(number, edge):
         return [saved_ref[(4 * (number - 1) + edge) * fields + f] for f in range(fields)]
 
-    def finish(is_low):
+    def prepare(is_low):
         metric = wide * fields
         halo = low(metric, OUTSIDE) if is_low else high(metric, OUTSIDE)
         coefs, state = {}, {}
@@ -444,28 +447,35 @@
             coefs[x] = coefficients(
                 level, metric_ref[pl.ds(x, 1), :], metric_ref[pl.ds(rows + x, 1), :]
             )
-        for number in range(STEPS):
-            if number > 0:
-                if is_low:
-                    state[number], state[number + 1] = saved(number, 0), saved(number, 1)
-                else:
-                    state[rows - 2 - number], state[rows - 1 - number] = saved(number, 2), saved(number, 3)
-            bottom = number + 1 - wide if is_low else rows - 1 - number
-            new = {}
-            for x in range(bottom, bottom + wide):
-                spot = group * (x + (wide if is_low else -wide)) + wide - 1
-                new[x] = row_step(
-                    level, lane, coefs[x], state[x - 1], state[x], state[x + 1],
-                    beyond[is_low, number], spot,
-                )
-            state = new
+        return state, coefs
+
+    def advanced(is_low, number, state, coefs):
+        if number > 0:
+            if is_low:
+                state[number], state[number + 1] = saved(number, 0), saved(number, 1)
+            else:
+                state[rows - 2 - number], state[rows - 1 - number] = saved(number, 2), saved(number, 3)
+        bottom = number + 1 - wide if is_low else rows - 1 - number
+        new = {}
+        for x in range(bottom, bottom + wide):
+            spot = group * (x + (wide if is_low else -wide)) + wide - 1
+            new[x] = row_step(
+                level, lane, coefs[x], state[x - 1], state[x], state[x + 1],
+                beyond[is_low, number], spot,
+            )
+        return new
+
+    parts = {is_low: prepare(is_low) for is_low in (True, False)}
+    for number in range(STEPS):
+        for is_low, (state, coefs) in parts.items():
+            parts[is_low] = advanced(is_low, number, state, coefs), coefs
+    for state, _ in parts.values():
         for x, tiles in state.items():
             for f in range(fields):
                 out_ref[f, pl.ds(x, levels, stride=rows), :] = tiles[f]
 
     copies = []
     for n, is_low in enumerate((True, False)):
-        finish(is_low)
         part = pl.ds(n * half, half)
         source = out_ref.reshape(fields * levels, rows, cols)
         copies.append(

time: 18.7 us -> 18.5 us (0.989)
  no operation moved by 1% of the time
where the time goes in v6:
time: 18.5 us; the launch traced here: 18.4 us
  starting transfers between devices  8.27 us (45%)
  waiting for transfers between devices  5.62 us (30%)
  Pallas kernels  4.41 us (24%)
    ppermute x9, starting transfers between devices, send(): return lax.ppermute(value, AXES, pairs)  8.27 us
    ppermute x9, waiting for transfers between devices, send(): return lax.ppermute(value, AXES, pairs)  5.62 us
    pallas_call x1, Pallas kernels, on_device(): pl.pallas_call(functools.partial(outer_kernel, sizes), out_shape=jax.Shap...  1.52 us
    pallas_call x1, Pallas kernels, on_device(): pl.pallas_call(functools.partial(split_kernel, sizes), out_shape=(tiles(r...  1.44 us
    pallas_call x1, Pallas kernels, on_device(): pl.pallas_call(functools.partial(middle_kernel, sizes), out_shape=(tiles(...  1.24 us
  transfers between devices with their start and end apart: 9, of which 4 were waited for; matrix products, arithmetic and copies ran while one was open for 0% of the time, Pallas kernels for 8%

profile of v6, /device:TPU:0, one launch (start us, length us, event | category | flops | bytes accessed | tf_op | source)
XLA Modules:
  0.0 18.4 jit_solution(16400807700958596775)
XLA Ops:
  0.0 1.4 %split.1 = (f32[64,8,128]{2,1,0:T(8,128)S(1)}, f32[32,8,128]{2,1,0:T(8,128)S(1)}, f32[32,8,128]{2,1,0:T(8,128)S(1)}, f32[2,8,128]{2,1,0:T(8,128)S(1)}, f32[5,8,128]{2,1,0:T(8,128)S(1)}, /*index=5*/f32[32,128]{1,0:T(8,128)S(1)}) custom-call(f32[4,128,128]{2,1,0:T(8,128)} %bitcast.3, f32[4,128,128]{2,1,0:T(8,128)} %bitcast.4, s32[4]{0:T(128)} %owner_hbm.1, ...), custom_call_target="tpu_custom_call" | custom-call | tf_op jit(solution)/shard_map/split/pallas_call | solution.py:514
  1.5 0.5 %collective-permute-start = (f32[32,8,128]{2,1,0:T(8,128)S(1)}, f32[32,8,128]{2,1,0:T(8,128)S(1)}, u32[]{:S(2)}, u32[]{:S(2)}) collective-permute-start(f32[32,8,128]{2,1,0:T(8,128)S(1)} %get-tuple-element.23), channel_id=1, source_target_pairs={{0,8},{1,9},{2,10},{3,11},{4,12},{5,13},{6,14},{7,15},{8,0},{9,1},... | collective-permute-start | bytes 393224 | tf_op jit(solution)/shard_map/ppermute | solution.py:35
  2.0 2.6 %collective-permute-start.2 = (f32[5,8,128]{2,1,0:T(8,128)S(1)}, f32[5,8,128]{2,1,0:T(8,128)S(1)}, u32[]{:S(2)}, u32[]{:S(2)}) collective-permute-start(f32[5,8,128]{2,1,0:T(8,128)S(1)} %get-tuple-element.25.side_ref), channel_id=1, source_target_pairs={{0,1},{1,0},{2,3},{3,2},{4,5},{5,4},{6,7},{7,6},{8,9},{9,8},{10,11... | collective-permute-start | bytes 61448 | tf_op jit(solution)/shard_map/ppermute | solution.py:35
  4.5 1.5 %collective-permute-start.3 = (f32[2,8,128]{2,1,0:T(8,128)S(1)}, f32[2,8,128]{2,1,0:T(8,128)S(1)}, u32[]{:S(2)}, u32[]{:S(2)}) collective-permute-start(f32[2,8,128]{2,1,0:T(8,128)S(1)} %get-tuple-element.26), channel_id=1, source_target_pairs={{0,17},{1,16},{2,19},{3,18},{4,21},{5,20},{6,23},{7,22},{8,25},{9,... | collective-permute-start | bytes 24584 | tf_op jit(solution)/shard_map/ppermute | solution.py:35
  6.0 0.0 collective-permute-done.given_ref
  6.1 0.1 collective-permute-start.1
  6.2 3.0 %collective-permute-done.3 = f32[2,8,128]{2,1,0:T(8,128)S(1)} collective-permute-done((f32[2,8,128]{2,1,0:T(8,128)S(1)}, f32[2,8,128]{2,1,0:T(8,128)S(1)}, u32[]{:S(2)}, u32[]{:S(2)}) %collective-permute-start.3) | collective-permute-done | bytes 8224 | tf_op jit(solution)/shard_map/ppermute | solution.py:35
  9.2 0.0 collective-permute-done.2.refs_0_
  9.2 1.4 %collective-permute-start.5 = (f32[20,8,128]{2,1,0:T(8,128)S(1)}, f32[20,8,128]{2,1,0:T(8,128)S(1)}, u32[]{:S(2)}, u32[]{:S(2)}) collective-permute-start(f32[20,8,128]{2,1,0:T(8,128)S(1)} %get-tuple-element.29), channel_id=1, source_target_pairs={{0,16},{1,17},{2,18},{3,19},{4,20},{5,21},{6,22},{7,23},{8,24},{9,... | collective-permute-start | bytes 245768 | tf_op jit(solution)/shard_map/ppermute | solution.py:35
  10.6 0.0 collective-permute-done.1
  10.6 0.1 collective-permute-start.4
  10.7 1.3 %collective-permute-done.4.other_ref = f32[18,8,128]{2,1,0:T(8,128)S(1)} collective-permute-done((f32[18,8,128]{2,1,0:T(8,128)S(1)}, f32[18,8,128]{2,1,0:T(8,128)S(1)}, u32[]{:S(2)}, u32[]{:S(2)}) %collective-permute-start.4) | collective-permute-done | bytes 73760 | tf_op jit(solution)/shard_map/ppermute | solution.py:35
  12.0 0.2 join.1
  12.2 0.2 collective-permute-start.8
  12.3 1.9 %collective-permute-start.7 = (f32[19,8,128]{2,1,0:T(8,128)S(1)}, f32[19,8,128]{2,1,0:T(8,128)S(1)}, u32[]{:S(2)}, u32[]{:S(2)}) collective-permute-start(f32[19,8,128]{2,1,0:T(8,128)S(1)} %get-tuple-element.30), channel_id=1, source_target_pairs={{0,2},{1,3},{2,4},{3,5},{4,6},{5,7},{6,14},{7,15},{8,0},{9,1},{10,... | collective-permute-start | bytes 233480 | tf_op jit(solution)/shard_map/ppermute | solution.py:35
  14.2 0.0 collective-permute-done.5
  14.2 0.1 collective-permute-start.6
  14.3 1.2 %collective-permute-done.6.other_ref = f32[16,8,128]{2,1,0:T(8,128)S(1)} collective-permute-done((f32[16,8,128]{2,1,0:T(8,128)S(1)}, f32[16,8,128]{2,1,0:T(8,128)S(1)}, u32[]{:S(2)}, u32[]{:S(2)}) %collective-permute-start.6) | collective-permute-done | bytes 65568 | tf_op jit(solution)/shard_map/ppermute | solution.py:35
  15.5 1.2 %middle.1 = (f32[5,8,128]{2,1,0:T(8,128)S(1)}, f32[48,8,128]{2,1,0:T(8,128)S(1)}, f32[32,8,128]{2,1,0:T(8,128)S(1)}) custom-call(f32[64,8,128]{2,1,0:T(8,128)S(1)} %get-tuple-element.21.pt_ref, f32[32,8,128]{2,1,0:T(8,128)S(1)} %get-tuple-element.28.outer_ref, f32[16,8,128]{2,1,0:T(8,128)S(1)} %slice_add_fusion.mine_ref, ...), custom_call_target="tpu_custom_call" | custom-call | flops 7864320 | bytes 1048576 | tf_op jit(solution)/shard_map/middle/pallas_call | solution.py:593
  16.8 0.1 collective-permute-done.8.second_ref
  16.9 0.0 collective-permute-done.7.first_ref
  16.9 1.5 %outer.1 = f32[32,16,128]{2,1,0:T(8,128)} custom-call(f32[32,8,128]{2,1,0:T(8,128)S(1)} %get-tuple-element.28.outer_ref, f32[5,8,128]{2,1,0:T(8,128)S(1)} %get-tuple-element.33.strip_ref, f32[48,8,128]{2,1,0:T(8,128)S(1)} %get-tuple-element.34.saved_ref, f32[32,8,128]{2,1,0:T(8,128)S(1)} %get-tuple-element.35.done_ref, ...), custom_call_target="tpu_custom_call" | custom-call | tf_op jit(solution)/shard_map/outer/pallas_call | solution.py:609
  (5 shorter events, 0.1 us)
Async XLA Ops:
  1.5 4.6 %collective-permute-start = (f32[32,8,128]{2,1,0:T(8,128)S(1)}, f32[32,8,128]{2,1,0:T(8,128)S(1)}, u32[]{:S(2)}, u32[]{:S(2)}) collective-permute-start(f32[32,8,128]{2,1,0:T(8,128)S(1)} %get-tuple-element.23), channel_id=1, source_target_pairs={{0,8},{1,9},{2,10},{3,11},{4,12},{5,13},{6,14},{7,15},{8,0},{9,1},... | collective-permute-start | bytes 393224 | tf_op jit(solution)/shard_map/ppermute | solution.py:35
  2.0 7.2 %collective-permute-start.2 = (f32[5,8,128]{2,1,0:T(8,128)S(1)}, f32[5,8,128]{2,1,0:T(8,128)S(1)}, u32[]{:S(2)}, u32[]{:S(2)}) collective-permute-start(f32[5,8,128]{2,1,0:T(8,128)S(1)} %get-tuple-element.25.side_ref), channel_id=1, source_target_pairs={{0,1},{1,0},{2,3},{3,2},{4,5},{5,4},{6,7},{7,6},{8,9},{9,8},{10,11... | collective-permute-start | bytes 61448 | tf_op jit(solution)/shard_map/ppermute | solution.py:35
  4.5 4.7 %collective-permute-start.3 = (f32[2,8,128]{2,1,0:T(8,128)S(1)}, f32[2,8,128]{2,1,0:T(8,128)S(1)}, u32[]{:S(2)}, u32[]{:S(2)}) collective-permute-start(f32[2,8,128]{2,1,0:T(8,128)S(1)} %get-tuple-element.26), channel_id=1, source_target_pairs={{0,17},{1,16},{2,19},{3,18},{4,21},{5,20},{6,23},{7,22},{8,25},{9,... | collective-permute-start | bytes 24584 | tf_op jit(solution)/shard_map/ppermute | solution.py:35
  6.1 4.6 %collective-permute-start.1 = (f32[16,8,128]{2,1,0:T(8,128)S(1)}, f32[16,8,128]{2,1,0:T(8,128)S(1)}, u32[]{:S(2)}, u32[]{:S(2)}) collective-permute-start(f32[16,8,128]{2,1,0:T(8,128)S(1)} %get-tuple-element.24), channel_id=1, source_target_pairs={{0,16},{1,17},{2,18},{3,19},{4,20},{5,21},{6,22},{7,23},{8,24},{9,... | collective-permute-start | bytes 196616 | tf_op jit(solution)/shard_map/ppermute | solution.py:35
  9.2 5.0 %collective-permute-start.5 = (f32[20,8,128]{2,1,0:T(8,128)S(1)}, f32[20,8,128]{2,1,0:T(8,128)S(1)}, u32[]{:S(2)}, u32[]{:S(2)}) collective-permute-start(f32[20,8,128]{2,1,0:T(8,128)S(1)} %get-tuple-element.29), channel_id=1, source_target_pairs={{0,16},{1,17},{2,18},{3,19},{4,20},{5,21},{6,22},{7,23},{8,24},{9,... | collective-permute-start | bytes 245768 | tf_op jit(solution)/shard_map/ppermute | solution.py:35
  10.6 1.3 %collective-permute-start.4 = (f32[18,8,128]{2,1,0:T(8,128)S(1)}, f32[18,8,128]{2,1,0:T(8,128)S(1)}, u32[]{:S(2)}, u32[]{:S(2)}) collective-permute-start(f32[18,8,128]{2,1,0:T(8,128)S(1)} %pad_maximum_fusion), channel_id=1, source_target_pairs={{0,8},{1,9},{2,10},{3,11},{4,12},{5,13},{6,14},{7,15},{8,0},{9,1},... | collective-permute-start | bytes 221192 | tf_op jit(solution)/shard_map/ppermute | solution.py:35
  12.2 4.7 %collective-permute-start.8 = (f32[19,8,128]{2,1,0:T(8,128)S(1)}, f32[19,8,128]{2,1,0:T(8,128)S(1)}, u32[]{:S(2)}, u32[]{:S(2)}) collective-permute-start(f32[19,8,128]{2,1,0:T(8,128)S(1)} %get-tuple-element.36), channel_id=1, source_target_pairs={{0,8},{1,9},{2,0},{3,1},{4,2},{5,3},{6,4},{7,5},{8,10},{9,11},{10,... | collective-permute-start | bytes 233480 | tf_op jit(solution)/shard_map/ppermute | solution.py:35
  12.3 4.5 %collective-permute-start.7 = (f32[19,8,128]{2,1,0:T(8,128)S(1)}, f32[19,8,128]{2,1,0:T(8,128)S(1)}, u32[]{:S(2)}, u32[]{:S(2)}) collective-permute-start(f32[19,8,128]{2,1,0:T(8,128)S(1)} %get-tuple-element.30), channel_id=1, source_target_pairs={{0,2},{1,3},{2,4},{3,5},{4,6},{5,7},{6,14},{7,15},{8,0},{9,1},{10,... | collective-permute-start | bytes 233480 | tf_op jit(solution)/shard_map/ppermute | solution.py:35
  14.2 1.3 %collective-permute-start.6 = (f32[16,8,128]{2,1,0:T(8,128)S(1)}, f32[16,8,128]{2,1,0:T(8,128)S(1)}, u32[]{:S(2)}, u32[]{:S(2)}) collective-permute-start(f32[16,8,128]{2,1,0:T(8,128)S(1)} %slice_add_fusion.mine_ref), channel_id=1, source_target_pairs={{0,8},{1,9},{2,10},{3,11},{4,12},{5,13},{6,14},{7,15},{8,0},{9,1},... | collective-permute-start | bytes 196616 | tf_op jit(solution)/shard_map/ppermute | solution.py:35

commit v7 on v6

--- a/solution.py
+++ b/solution.py
@@ -222,10 +222,90 @@
     return [jnp.where(early == has_left, beside[0], own)]
 
 
+def metric_rows(metric_ref, wide, up):
+    rows = metric_ref.shape[0] // 2
+    scale, ground = metric_ref[pl.ds(0, rows), :], metric_ref[pl.ds(rows, rows), :]
+    tops = jnp.concatenate([scale[rows - wide :], ground[rows - wide :]], axis=0)
+    bottoms = jnp.concatenate([scale[:wide], ground[:wide]], axis=0)
+    return jnp.where(up, tops, bottoms)
+
+
+def besides(sizes, fields, near, edge_ref, other_ref, sides):
+    has_left, has_right = has_neighbours("dy", sizes[2])
+    per_side = edge_ref.shape[0] // sides
+    by_side = []
+    for side in range(sides):
+        own, other = (
+            [ref[side * per_side + k] for k in range(per_side)] for ref in (edge_ref, other_ref)
+        )
+        tiles = [near[side][per_side + k] + (own[k] + other[k]) for k in range(per_side)]
+        tiles = unpacked(tiles, fields, has_left, sizes[2]) + [near[side][2 * per_side]]
+        if sides == 2:
+            here = (has_left, has_right)[side]
+            empty = [0.0] * fields + [OUTSIDE]
+            tiles = [jnp.where(here, tile, e) for tile, e in zip(tiles, empty)]
+        by_side.append(tiles)
+    return [list(pair) for pair in zip(*by_side)]
+
+
+def ends_of(strips, up, quarter):
+    lane = lanes_of(strips[0][0].shape)
+    cols = lane.shape[1]
+    fields = len(strips) - 1
+    if len(strips[0]) == 1:
+        packed = None
+        for f in range(fields):
+            moved = turn(strips[f][0], jnp.where(up, quarter, 0) + f * quarter)
+            packed = moved if f == 0 else jnp.where(lane < f * quarter, packed, moved)
+        return [packed, strips[fields][0]]
+    return [
+        jnp.where(
+            lane < quarter,
+            a,
+            jnp.where(
+                lane < 2 * quarter,
+                turn(b, quarter),
+                jnp.where(lane < cols - quarter, turn(b, -quarter), a),
+            ),
+        )
+        for a, b in strips
+    ]
+
+
+def near_kernel(
+    sizes, n_sides, pt_ref, sum_ref, metric_ref, edge_ref, other_ref, side_ref, *refs
+):
+    near, (message_ref,) = refs[:n_sides], refs[n_sides:]
+    rows = metric_ref.shape[0] // 2
+    fields = pt_ref.shape[0] // rows
+    wide = STEPS
+    even = lax.rem(lax.axis_index("member"), 2) == 0
+    has_left, _ = has_neighbours("dy", sizes[2])
+    lane = lanes_of(pt_ref.shape[1:])
+    early = lax.rem(lane, 2 * wide) < wide
+    values = besides(sizes, fields, near, edge_ref, other_ref, n_sides)
+    strips = []
+    for f in range(fields):
+        own = None
+        for r in range(wide):
+            x = jnp.where(even, r, rows - 1 - r)
+            place = jnp.where(even, r, wide - 1 - r) * fields
+            tile = pt_ref[x * fields + f] + sum_ref[r * fields + f]
+            message_ref[place + f] = tile
+            moved = turn(tile, 2 * wide * x + wide)
+            own = moved if own is None else jnp.where(lane // (2 * wide) == x, moved, own)
+        strips.append(strips_of(early, own, values[f], has_left))
+    strips.append(strips_of(early, side_ref[side_ref.shape[0] - 1], values[fields], has_left))
+    up = jnp.logical_not(even)
+    message_ref[wide * fields] = metric_rows(metric_ref, wide, up)
+    for k, end in enumerate(ends_of(strips, up, 2 * wide * wide)):
+        message_ref[wide * fields + 1 + k] = end
+
+
 def join_kernel(
-    sizes, n_sides, pt_ref, mine_ref, edge_ref, other_ref, metric_ref, side_ref, *refs
+    sizes, n_sides, pt_ref, mine_ref, theirs_ref, edge_ref, other_ref, metric_ref, side_ref, *refs
 ):
-    near, (start_ref, beside_ref, first_ref, second_ref) = refs[:n_sides], refs[n_sides:]
+    near, (start_ref, beside_ref, first_ref) = refs[:n_sides], refs[n_sides:]
     rows, cols = metric_ref.shape[0] // 2, metric_ref.shape[1]
     levels = pt_ref.shape[1]
     fields = pt_ref.shape[0] // rows
@@ -239,53 +319,17 @@
 
     for r in range(wide):
         for f in range(fields):
-            mine, other = mine_ref[r * fields + f], other_ref[r * fields + f]
+            mine, other = mine_ref[r * fields + f], theirs_ref[r * fields + f]
             low, high = jnp.where(parity == 0, mine, other), jnp.where(parity == 0, other, mine)
             start_ref[r * fields + f] = pt_ref[r * fields + f] + low
             end = 2 * wide - 1 - r
             start_ref[end * fields + f] = pt_ref[(rows - 1 - r) * fields + f] + high
 
-    def ends_of(strips, up):
-        if sides == 1:
-            packed = None
-            for f in range(fields):
-                moved = turn(strips[f][0], jnp.where(up, quarter, 0) + f * quarter)
-                packed = moved if f == 0 else jnp.where(lane < f * quarter, packed, moved)
-            return [packed, strips[fields][0]]
-        return [
-            jnp.where(
-                lane < quarter,
-                a,
-                jnp.where(
-                    lane < 2 * quarter,
-                    turn(b, quarter),
-                    jnp.where(lane < cols - quarter, turn(b, -quarter), a),
-                ),
-            )
-            for a, b in strips
-        ]
-
-    per_side = edge_ref.shape[0] // sides
-    sums = [
-        unpacked(
-            [
-                near[side][per_side + k]
-                + (edge_ref[side * per_side + k] + other_ref[wide * fields + side * per_side + k])
-                for k in range(per_side)
-            ],
-            fields, has_left, sizes[2],
-        )
-        for side in range(sides)
-    ]
     strips = []
-    for f in range(fields + 1):
-        beside = []
+    values = besides(sizes, fields, near, edge_ref, other_ref, sides)
+    for f, beside in enumerate(values):
         for side in range(sides):
-            value = sums[side][f] if f < fields else near[side][2 * per_side]
-            if sides == 2:
-                value = jnp.where((has_left, has_right)[side], value, 0.0 if f < fields else OUTSIDE)
-            beside.append(value)
-            beside_ref[side * (fields + 1) + f] = value
+            beside_ref[side * (fields + 1) + f] = beside[side]
         if f < fields:
             own = None
             for k in range(2 * wide):
@@ -295,16 +339,13 @@
         else:
             own = side_ref[side_ref.shape[0] - 1]
         strips.append(strips_of(early, own, beside, has_left))
-    scale, ground = metric_ref[pl.ds(0, rows), :], metric_ref[pl.ds(rows, rows), :]
-    tops = jnp.concatenate([scale[rows - wide :], ground[rows - wide :]], axis=0)
-    bottoms = jnp.concatenate([scale[:wide], ground[:wide]], axis=0)
-    for message, up in ((first_ref, parity == 0), (second_ref, parity == 1)):
-        base = jnp.where(up, wide, 0) * fields
-        for k in range(wide * fields):
-            message[k] = start_ref[base + k]
-        message[wide * fields] = jnp.where(up, tops, bottoms)
-        for k, end in enumerate(ends_of(strips, up)):
-            message[wide * fields + 1 + k] = end
+    up = parity == 0
+    base = jnp.where(up, wide, 0) * fields
+    for k in range(wide * fields):
+        first_ref[k] = start_ref[base + k]
+    first_ref[wide * fields] = metric_rows(metric_ref, wide, up)
+    for k, end in enumerate(ends_of(strips, up, quarter)):
+        first_ref[wide * fields + 1 + k] = end
 
 
 def middle_kernel(
@@ -567,27 +608,37 @@
     cut = STEPS * fields
     outer, inner = pl.pallas_call(
         pair_kernel,
-        out_shape=(tiles(cut), tiles(half * fields - cut + fields)),
+        out_shape=(tiles(cut), tiles(half * fields - cut + 1)),
         in_specs=[VMEM] * 2,
         out_specs=(VMEM,) * 2,
         compiler_params=MODEST,
         name="pair",
     )(keep, given)
     outer = over_chips(outer)
-    inner = over_chips(inner)[fields:]
-
-    other = over_members(jnp.concatenate([outer, edges], axis=0), 1)
-    count = cut + (3 if along == 2 else fields + 2)
-    start, beside, first, second = pl.pallas_call(
+    inner = over_chips(inner)[1:]
+
+    other_edges = over_members(edges, 1)
+    outer, other_edges = lax.optimization_barrier((outer, other_edges))
+    n_ends = 2 if along == 2 else fields + 1
+    message = pl.pallas_call(
+        functools.partial(near_kernel, sizes, len(near)),
+        out_shape=tiles(cut + 1 + n_ends),
+        in_specs=[VMEM] * (6 + len(near)),
+        out_specs=VMEM,
+        compiler_params=MODEST,
+        name="near",
+    )(states, outer, metric, edges, other_edges, side, *near)
+    second_in = send(message, loop_target(sizes[1], False))
+    other = over_members(outer, 1)
+    start, beside, first = pl.pallas_call(
         functools.partial(join_kernel, sizes, len(near)),
-        out_shape=(tiles(2 * cut), tiles(len(near) * (fields + 1)), tiles(count), tiles(count)),
-        in_specs=[VMEM] * (6 + len(near)),
-        out_specs=(VMEM,) * 4,
+        out_shape=(tiles(2 * cut), tiles(len(near) * (fields + 1)), tiles(cut + 1 + n_ends)),
+        in_specs=[VMEM] * (7 + len(near)),
+        out_specs=(VMEM,) * 3,
         compiler_params=MODEST,
         name="join",
-    )(states, outer, edges, other, metric, side, *near)
+    )(states, outer, other, edges, other_edges, metric, side, *near)
     first_in = send(first, loop_target(sizes[1], True))
-    second_in = send(second, loop_target(sizes[1], False))
     inner, _ = lax.optimization_barrier((inner, first))
     other = over_members(inner, 1)
     strips, saved, done = pl.pallas_call(

time: 18.5 us -> 18.2 us (0.984)
  waiting for transfers between devices: 5.62 us -> 4.86 us
  starting transfers between devices: 8.27 us -> 8.51 us
    ppermute x9 -> x10, waiting for transfers between devices: 5.62 us -> 4.86 us  [send(): return lax.ppermute(value, AXES, pairs)]
    ppermute x9 -> x10, starting transfers between devices: 8.27 us -> 8.51 us  [send(): return lax.ppermute(value, AXES, pairs)]
  transfers between devices with their start and end apart: 9 -> 10, of which waited for: 4 -> 3; matrix products, arithmetic and copies ran while one was open for 0% -> 0% of each run, Pallas kernels for 8% -> 9%
where the time goes in v7:
time: 18.2 us; the launch traced here: 18 us
  starting transfers between devices  8.51 us (47%)
  waiting for transfers between devices  4.86 us (27%)
  Pallas kernels  4.57 us (25%)
    ppermute x10, starting transfers between devices, send(): return lax.ppermute(value, AXES, pairs)  8.51 us
    ppermute x10, waiting for transfers between devices, send(): return lax.ppermute(value, AXES, pairs)  4.86 us
    pallas_call x1, Pallas kernels, on_device(): pl.pallas_call(functools.partial(outer_kernel, sizes), out_shape=jax.Shap...  1.52 us
    pallas_call x1, Pallas kernels, on_device(): pl.pallas_call(functools.partial(split_kernel, sizes), out_shape=(tiles(r...  1.44 us
    pallas_call x1, Pallas kernels, on_device(): pl.pallas_call(functools.partial(middle_kernel, sizes), out_shape=(tiles(...  1.24 us
  transfers between devices with their start and end apart: 10, of which 3 were waited for; matrix products, arithmetic and copies ran while one was open for 0% of the time, Pallas kernels for 9%

profile of v7, /device:TPU:0, one launch (start us, length us, event | category | flops | bytes accessed | tf_op | source)
XLA Modules:
  0.0 18.0 jit_solution(4298550261123324996)
XLA Ops:
  0.0 1.4 %split.1 = (f32[64,8,128]{2,1,0:T(8,128)S(1)}, f32[32,8,128]{2,1,0:T(8,128)S(1)}, f32[32,8,128]{2,1,0:T(8,128)S(1)}, f32[2,8,128]{2,1,0:T(8,128)S(1)}, f32[5,8,128]{2,1,0:T(8,128)S(1)}, /*index=5*/f32[32,128]{1,0:T(8,128)S(1)}) custom-call(f32[4,128,128]{2,1,0:T(8,128)} %bitcast.3, f32[4,128,128]{2,1,0:T(8,128)} %bitcast.4, s32[4]{0:T(128)} %owner_hbm.1, ...), custom_call_target="tpu_custom_call" | custom-call | tf_op jit(solution)/shard_map/split/pallas_call | solution.py:555
  1.5 0.5 %collective-permute-start = (f32[32,8,128]{2,1,0:T(8,128)S(1)}, f32[32,8,128]{2,1,0:T(8,128)S(1)}, u32[]{:S(2)}, u32[]{:S(2)}) collective-permute-start(f32[32,8,128]{2,1,0:T(8,128)S(1)} %get-tuple-element.24), channel_id=1, source_target_pairs={{0,8},{1,9},{2,10},{3,11},{4,12},{5,13},{6,14},{7,15},{8,0},{9,1},... | collective-permute-start | bytes 393224 | tf_op jit(solution)/shard_map/ppermute | solution.py:35
  2.0 2.6 %collective-permute-start.2 = (f32[5,8,128]{2,1,0:T(8,128)S(1)}, f32[5,8,128]{2,1,0:T(8,128)S(1)}, u32[]{:S(2)}, u32[]{:S(2)}) collective-permute-start(f32[5,8,128]{2,1,0:T(8,128)S(1)} %get-tuple-element.26.side_ref), channel_id=1, source_target_pairs={{0,1},{1,0},{2,3},{3,2},{4,5},{5,4},{6,7},{7,6},{8,9},{9,8},{10,11... | collective-permute-start | bytes 61448 | tf_op jit(solution)/shard_map/ppermute | solution.py:35
  4.5 1.5 %collective-permute-start.3 = (f32[2,8,128]{2,1,0:T(8,128)S(1)}, f32[2,8,128]{2,1,0:T(8,128)S(1)}, u32[]{:S(2)}, u32[]{:S(2)}) collective-permute-start(f32[2,8,128]{2,1,0:T(8,128)S(1)} %get-tuple-element.27), channel_id=1, source_target_pairs={{0,17},{1,16},{2,19},{3,18},{4,21},{5,20},{6,23},{7,22},{8,25},{9,... | collective-permute-start | bytes 24584 | tf_op jit(solution)/shard_map/ppermute | solution.py:35
  6.0 0.0 collective-permute-done.given_ref
  6.1 0.1 collective-permute-start.1
  6.2 3.0 %collective-permute-done.3 = f32[2,8,128]{2,1,0:T(8,128)S(1)} collective-permute-done((f32[2,8,128]{2,1,0:T(8,128)S(1)}, f32[2,8,128]{2,1,0:T(8,128)S(1)}, u32[]{:S(2)}, u32[]{:S(2)}) %collective-permute-start.3) | collective-permute-done | bytes 8224 | tf_op jit(solution)/shard_map/ppermute | solution.py:35
  9.2 0.0 collective-permute-done.2.refs_0_
  9.2 0.0 collective-permute-start.4
  9.2 1.5 %collective-permute-start.6 = (f32[17,8,128]{2,1,0:T(8,128)S(1)}, f32[17,8,128]{2,1,0:T(8,128)S(1)}, u32[]{:S(2)}, u32[]{:S(2)}) collective-permute-start(f32[17,8,128]{2,1,0:T(8,128)S(1)} %get-tuple-element.32), channel_id=1, source_target_pairs={{0,16},{1,17},{2,18},{3,19},{4,20},{5,21},{6,22},{7,23},{8,24},{9,... | collective-permute-start | bytes 208904 | tf_op jit(solution)/shard_map/ppermute | solution.py:35
  10.7 0.0 collective-permute-done.1
  10.7 0.0 collective-permute-done.4.other_ref
  10.7 0.2 %collective-permute-start.5 = (f32[16,8,128]{2,1,0:T(8,128)S(1)}, f32[16,8,128]{2,1,0:T(8,128)S(1)}, u32[]{:S(2)}, u32[]{:S(2)}) collective-permute-start(f32[16,8,128]{2,1,0:T(8,128)S(1)} %add.9.mine_ref.sum_ref), channel_id=1, source_target_pairs={{0,8},{1,9},{2,10},{3,11},{4,12},{5,13},{6,14},{7,15},{8,0},{9,1},... | collective-permute-start | bytes 196616 | tf_op jit(solution)/shard_map/ppermute | solution.py:35
  10.9 0.2 near.1
  11.1 0.4 %collective-permute-start.9 = (f32[19,8,128]{2,1,0:T(8,128)S(1)}, f32[19,8,128]{2,1,0:T(8,128)S(1)}, u32[]{:S(2)}, u32[]{:S(2)}) collective-permute-start(f32[19,8,128]{2,1,0:T(8,128)S(1)} %near.1), channel_id=1, source_target_pairs={{0,8},{1,9},{2,0},{3,1},{4,2},{5,3},{6,4},{7,5},{8,10},{9,11},{10,... | collective-permute-start | bytes 233480 | tf_op jit(solution)/shard_map/ppermute | solution.py:35
  11.5 0.6 %collective-permute-done.5.theirs_ref = f32[16,8,128]{2,1,0:T(8,128)S(1)} collective-permute-done((f32[16,8,128]{2,1,0:T(8,128)S(1)}, f32[16,8,128]{2,1,0:T(8,128)S(1)}, u32[]{:S(2)}, u32[]{:S(2)}) %collective-permute-start.5) | collective-permute-done | bytes 65568 | tf_op jit(solution)/shard_map/ppermute | solution.py:35
  12.0 0.2 %join.1 = (f32[32,8,128]{2,1,0:T(8,128)S(1)}, f32[5,8,128]{2,1,0:T(8,128)S(1)}, f32[19,8,128]{2,1,0:T(8,128)S(1)}) custom-call(f32[64,8,128]{2,1,0:T(8,128)S(1)} %get-tuple-element.22.pt_ref, f32[16,8,128]{2,1,0:T(8,128)S(1)} %add.9.mine_ref.sum_ref, f32[16,8,128]{2,1,0:T(8,128)S(1)} %collective-permute-done.5.theirs_ref, ...), custom_call_target="tpu_custom_call" | custom-call | tf_op jit(solution)/shard_map/join/pallas_call | solution.py:633
  12.2 1.7 %collective-permute-start.8 = (f32[19,8,128]{2,1,0:T(8,128)S(1)}, f32[19,8,128]{2,1,0:T(8,128)S(1)}, u32[]{:S(2)}, u32[]{:S(2)}) collective-permute-start(f32[19,8,128]{2,1,0:T(8,128)S(1)} %get-tuple-element.33), channel_id=1, source_target_pairs={{0,2},{1,3},{2,4},{3,5},{4,6},{5,7},{6,14},{7,15},{8,0},{9,1},{10,... | collective-permute-start | bytes 233480 | tf_op jit(solution)/shard_map/ppermute | solution.py:35
  13.9 0.0 collective-permute-done.6
  13.9 0.1 collective-permute-start.7
  14.0 1.2 %collective-permute-done.7.other_ref = f32[16,8,128]{2,1,0:T(8,128)S(1)} collective-permute-done((f32[16,8,128]{2,1,0:T(8,128)S(1)}, f32[16,8,128]{2,1,0:T(8,128)S(1)}, u32[]{:S(2)}, u32[]{:S(2)}) %collective-permute-start.7) | collective-permute-done | bytes 65568 | tf_op jit(solution)/shard_map/ppermute | solution.py:35
  15.2 1.2 %middle.1 = (f32[5,8,128]{2,1,0:T(8,128)S(1)}, f32[48,8,128]{2,1,0:T(8,128)S(1)}, f32[32,8,128]{2,1,0:T(8,128)S(1)}) custom-call(f32[64,8,128]{2,1,0:T(8,128)S(1)} %get-tuple-element.22.pt_ref, f32[32,8,128]{2,1,0:T(8,128)S(1)} %get-tuple-element.31.outer_ref, f32[16,8,128]{2,1,0:T(8,128)S(1)} %slice_add_fusion.mine_ref, ...), custom_call_target="tpu_custom_call" | custom-call | flops 7864320 | bytes 1048576 | tf_op jit(solution)/shard_map/middle/pallas_call | solution.py:644
  16.5 0.0 collective-permute-done.9.second_ref
  16.5 0.0 collective-permute-done.8.first_ref
  16.5 1.5 %outer.1 = f32[32,16,128]{2,1,0:T(8,128)} custom-call(f32[32,8,128]{2,1,0:T(8,128)S(1)} %get-tuple-element.31.outer_ref, f32[5,8,128]{2,1,0:T(8,128)S(1)} %get-tuple-element.36.strip_ref, f32[48,8,128]{2,1,0:T(8,128)S(1)} %get-tuple-element.37.saved_ref, f32[32,8,128]{2,1,0:T(8,128)S(1)} %get-tuple-element.38.done_ref, ...), custom_call_target="tpu_custom_call" | custom-call | tf_op jit(solution)/shard_map/outer/pallas_call | solution.py:660
  (4 shorter events, 0.0 us)
Async XLA Ops:
  1.5 4.6 %collective-permute-start = (f32[32,8,128]{2,1,0:T(8,128)S(1)}, f32[32,8,128]{2,1,0:T(8,128)S(1)}, u32[]{:S(2)}, u32[]{:S(2)}) collective-permute-start(f32[32,8,128]{2,1,0:T(8,128)S(1)} %get-tuple-element.24), channel_id=1, source_target_pairs={{0,8},{1,9},{2,10},{3,11},{4,12},{5,13},{6,14},{7,15},{8,0},{9,1},... | collective-permute-start | bytes 393224 | tf_op jit(solution)/shard_map/ppermute | solution.py:35
  2.0 7.2 %collective-permute-start.2 = (f32[5,8,128]{2,1,0:T(8,128)S(1)}, f32[5,8,128]{2,1,0:T(8,128)S(1)}, u32[]{:S(2)}, u32[]{:S(2)}) collective-permute-start(f32[5,8,128]{2,1,0:T(8,128)S(1)} %get-tuple-element.26.side_ref), channel_id=1, source_target_pairs={{0,1},{1,0},{2,3},{3,2},{4,5},{5,4},{6,7},{7,6},{8,9},{9,8},{10,11... | collective-permute-start | bytes 61448 | tf_op jit(solution)/shard_map/ppermute | solution.py:35
  4.5 4.7 %collective-permute-start.3 = (f32[2,8,128]{2,1,0:T(8,128)S(1)}, f32[2,8,128]{2,1,0:T(8,128)S(1)}, u32[]{:S(2)}, u32[]{:S(2)}) collective-permute-start(f32[2,8,128]{2,1,0:T(8,128)S(1)} %get-tuple-element.27), channel_id=1, source_target_pairs={{0,17},{1,16},{2,19},{3,18},{4,21},{5,20},{6,23},{7,22},{8,25},{9,... | collective-permute-start | bytes 24584 | tf_op jit(solution)/shard_map/ppermute | solution.py:35
  6.1 4.6 %collective-permute-start.1 = (f32[16,8,128]{2,1,0:T(8,128)S(1)}, f32[16,8,128]{2,1,0:T(8,128)S(1)}, u32[]{:S(2)}, u32[]{:S(2)}) collective-permute-start(f32[16,8,128]{2,1,0:T(8,128)S(1)} %get-tuple-element.25), channel_id=1, source_target_pairs={{0,16},{1,17},{2,18},{3,19},{4,20},{5,21},{6,22},{7,23},{8,24},{9,... | collective-permute-start | bytes 196616 | tf_op jit(solution)/shard_map/ppermute | solution.py:35
  9.2 1.5 %collective-permute-start.4 = (f32[2,8,128]{2,1,0:T(8,128)S(1)}, f32[2,8,128]{2,1,0:T(8,128)S(1)}, u32[]{:S(2)}, u32[]{:S(2)}) collective-permute-start(f32[2,8,128]{2,1,0:T(8,128)S(1)} %slice_add_fusion.1.edge_ref), channel_id=1, source_target_pairs={{0,8},{1,9},{2,10},{3,11},{4,12},{5,13},{6,14},{7,15},{8,0},{9,1},... | collective-permute-start | bytes 24584 | tf_op jit(solution)/shard_map/ppermute | solution.py:35
  9.2 4.7 %collective-permute-start.6 = (f32[17,8,128]{2,1,0:T(8,128)S(1)}, f32[17,8,128]{2,1,0:T(8,128)S(1)}, u32[]{:S(2)}, u32[]{:S(2)}) collective-permute-start(f32[17,8,128]{2,1,0:T(8,128)S(1)} %get-tuple-element.32), channel_id=1, source_target_pairs={{0,16},{1,17},{2,18},{3,19},{4,20},{5,21},{6,22},{7,23},{8,24},{9,... | collective-permute-start | bytes 208904 | tf_op jit(solution)/shard_map/ppermute | solution.py:35
  10.7 1.3 %collective-permute-start.5 = (f32[16,8,128]{2,1,0:T(8,128)S(1)}, f32[16,8,128]{2,1,0:T(8,128)S(1)}, u32[]{:S(2)}, u32[]{:S(2)}) collective-permute-start(f32[16,8,128]{2,1,0:T(8,128)S(1)} %add.9.mine_ref.sum_ref), channel_id=1, source_target_pairs={{0,8},{1,9},{2,10},{3,11},{4,12},{5,13},{6,14},{7,15},{8,0},{9,1},... | collective-permute-start | bytes 196616 | tf_op jit(solution)/shard_map/ppermute | solution.py:35
  11.1 5.4 %collective-permute-start.9 = (f32[19,8,128]{2,1,0:T(8,128)S(1)}, f32[19,8,128]{2,1,0:T(8,128)S(1)}, u32[]{:S(2)}, u32[]{:S(2)}) collective-permute-start(f32[19,8,128]{2,1,0:T(8,128)S(1)} %near.1), channel_id=1, source_target_pairs={{0,8},{1,9},{2,0},{3,1},{4,2},{5,3},{6,4},{7,5},{8,10},{9,11},{10,... | collective-permute-start | bytes 233480 | tf_op jit(solution)/shard_map/ppermute | solution.py:35
  12.2 4.3 %collective-permute-start.8 = (f32[19,8,128]{2,1,0:T(8,128)S(1)}, f32[19,8,128]{2,1,0:T(8,128)S(1)}, u32[]{:S(2)}, u32[]{:S(2)}) collective-permute-start(f32[19,8,128]{2,1,0:T(8,128)S(1)} %get-tuple-element.33), channel_id=1, source_target_pairs={{0,2},{1,3},{2,4},{3,5},{4,6},{5,7},{6,14},{7,15},{8,0},{9,1},{10,... | collective-permute-start | bytes 233480 | tf_op jit(solution)/shard_map/ppermute | solution.py:35
  13.9 1.3 %collective-permute-start.7 = (f32[16,8,128]{2,1,0:T(8,128)S(1)}, f32[16,8,128]{2,1,0:T(8,128)S(1)}, u32[]{:S(2)}, u32[]{:S(2)}) collective-permute-start(f32[16,8,128]{2,1,0:T(8,128)S(1)} %slice_add_fusion.mine_ref), channel_id=1, source_target_pairs={{0,8},{1,9},{2,10},{3,11},{4,12},{5,13},{6,14},{7,15},{8,0},{9,1},... | collective-permute-start | bytes 196616 | tf_op jit(solution)/shard_map/ppermute | solution.py:35

commit v8 on v7

--- a/solution.py
+++ b/solution.py
@@ -639,7 +639,6 @@
         name="join",
     )(states, outer, other, edges, other_edges, metric, side, *near)
     first_in = send(first, loop_target(sizes[1], True))
-    inner, _ = lax.optimization_barrier((inner, first))
     other = over_members(inner, 1)
     strips, saved, done = pl.pallas_call(
         functools.partial(middle_kernel, sizes),

time: 18.2 us -> 18.2 us (level)
  no operation moved by 1% of the time
where the time goes in v8:
time: 18.2 us; the launch traced here: 18 us
  starting transfers between devices  8.51 us (47%)
  waiting for transfers between devices  4.86 us (27%)
  Pallas kernels  4.57 us (25%)
    ppermute x10, starting transfers between devices, send(): return lax.ppermute(value, AXES, pairs)  8.51 us
    ppermute x10, waiting for transfers between devices, send(): return lax.ppermute(value, AXES, pairs)  4.86 us
    pallas_call x1, Pallas kernels, on_device(): pl.pallas_call(functools.partial(outer_kernel, sizes), out_shape=jax.Shap...  1.52 us
    pallas_call x1, Pallas kernels, on_device(): pl.pallas_call(functools.partial(split_kernel, sizes), out_shape=(tiles(r...  1.44 us
    pallas_call x1, Pallas kernels, on_device(): pl.pallas_call(functools.partial(middle_kernel, sizes), out_shape=(tiles(...  1.24 us
  transfers between devices with their start and end apart: 10, of which 3 were waited for; matrix products, arithmetic and copies ran while one was open for 0% of the time, Pallas kernels for 9%

profile of v8, /device:TPU:0, one launch (start us, length us, event | category | flops | bytes accessed | tf_op | source)
XLA Modules:
  0.0 18.0 jit_solution(4298550261123324996)
XLA Ops:
  0.0 1.4 %split.1 = (f32[64,8,128]{2,1,0:T(8,128)S(1)}, f32[32,8,128]{2,1,0:T(8,128)S(1)}, f32[32,8,128]{2,1,0:T(8,128)S(1)}, f32[2,8,128]{2,1,0:T(8,128)S(1)}, f32[5,8,128]{2,1,0:T(8,128)S(1)}, /*index=5*/f32[32,128]{1,0:T(8,128)S(1)}) custom-call(f32[4,128,128]{2,1,0:T(8,128)} %bitcast.3, f32[4,128,128]{2,1,0:T(8,128)} %bitcast.4, s32[4]{0:T(128)} %owner_hbm.1, ...), custom_call_target="tpu_custom_call" | custom-call | tf_op jit(solution)/shard_map/split/pallas_call | solution.py:555
  1.5 0.5 %collective-permute-start = (f32[32,8,128]{2,1,0:T(8,128)S(1)}, f32[32,8,128]{2,1,0:T(8,128)S(1)}, u32[]{:S(2)}, u32[]{:S(2)}) collective-permute-start(f32[32,8,128]{2,1,0:T(8,128)S(1)} %get-tuple-element.23), channel_id=1, source_target_pairs={{0,8},{1,9},{2,10},{3,11},{4,12},{5,13},{6,14},{7,15},{8,0},{9,1},... | collective-permute-start | bytes 393224 | tf_op jit(solution)/shard_map/ppermute | solution.py:35
  2.0 2.6 %collective-permute-start.2 = (f32[5,8,128]{2,1,0:T(8,128)S(1)}, f32[5,8,128]{2,1,0:T(8,128)S(1)}, u32[]{:S(2)}, u32[]{:S(2)}) collective-permute-start(f32[5,8,128]{2,1,0:T(8,128)S(1)} %get-tuple-element.25.side_ref), channel_id=1, source_target_pairs={{0,1},{1,0},{2,3},{3,2},{4,5},{5,4},{6,7},{7,6},{8,9},{9,8},{10,11... | collective-permute-start | bytes 61448 | tf_op jit(solution)/shard_map/ppermute | solution.py:35
  4.5 1.5 %collective-permute-start.3 = (f32[2,8,128]{2,1,0:T(8,128)S(1)}, f32[2,8,128]{2,1,0:T(8,128)S(1)}, u32[]{:S(2)}, u32[]{:S(2)}) collective-permute-start(f32[2,8,128]{2,1,0:T(8,128)S(1)} %get-tuple-element.26), channel_id=1, source_target_pairs={{0,17},{1,16},{2,19},{3,18},{4,21},{5,20},{6,23},{7,22},{8,25},{9,... | collective-permute-start | bytes 24584 | tf_op jit(solution)/shard_map/ppermute | solution.py:35
  6.0 0.0 collective-permute-done.given_ref
  6.1 0.1 collective-permute-start.1
  6.2 3.0 %collective-permute-done.3 = f32[2,8,128]{2,1,0:T(8,128)S(1)} collective-permute-done((f32[2,8,128]{2,1,0:T(8,128)S(1)}, f32[2,8,128]{2,1,0:T(8,128)S(1)}, u32[]{:S(2)}, u32[]{:S(2)}) %collective-permute-start.3) | collective-permute-done | bytes 8224 | tf_op jit(solution)/shard_map/ppermute | solution.py:35
  9.2 0.0 collective-permute-done.2.refs_0_
  9.2 0.0 collective-permute-start.4
  9.2 1.5 %collective-permute-start.6 = (f32[17,8,128]{2,1,0:T(8,128)S(1)}, f32[17,8,128]{2,1,0:T(8,128)S(1)}, u32[]{:S(2)}, u32[]{:S(2)}) collective-permute-start(f32[17,8,128]{2,1,0:T(8,128)S(1)} %get-tuple-element.31), channel_id=1, source_target_pairs={{0,16},{1,17},{2,18},{3,19},{4,20},{5,21},{6,22},{7,23},{8,24},{9,... | collective-permute-start | bytes 208904 | tf_op jit(solution)/shard_map/ppermute | solution.py:35
  10.7 0.0 collective-permute-done.1
  10.7 0.0 collective-permute-done.4.other_ref
  10.7 0.2 %collective-permute-start.5 = (f32[16,8,128]{2,1,0:T(8,128)S(1)}, f32[16,8,128]{2,1,0:T(8,128)S(1)}, u32[]{:S(2)}, u32[]{:S(2)}) collective-permute-start(f32[16,8,128]{2,1,0:T(8,128)S(1)} %add.9.mine_ref.sum_ref), channel_id=1, source_target_pairs={{0,8},{1,9},{2,10},{3,11},{4,12},{5,13},{6,14},{7,15},{8,0},{9,1},... | collective-permute-start | bytes 196616 | tf_op jit(solution)/shard_map/ppermute | solution.py:35
  10.9 0.2 near.1
  11.1 0.4 %collective-permute-start.9 = (f32[19,8,128]{2,1,0:T(8,128)S(1)}, f32[19,8,128]{2,1,0:T(8,128)S(1)}, u32[]{:S(2)}, u32[]{:S(2)}) collective-permute-start(f32[19,8,128]{2,1,0:T(8,128)S(1)} %near.1), channel_id=1, source_target_pairs={{0,8},{1,9},{2,0},{3,1},{4,2},{5,3},{6,4},{7,5},{8,10},{9,11},{10,... | collective-permute-start | bytes 233480 | tf_op jit(solution)/shard_map/ppermute | solution.py:35
  11.5 0.6 %collective-permute-done.5.theirs_ref = f32[16,8,128]{2,1,0:T(8,128)S(1)} collective-permute-done((f32[16,8,128]{2,1,0:T(8,128)S(1)}, f32[16,8,128]{2,1,0:T(8,128)S(1)}, u32[]{:S(2)}, u32[]{:S(2)}) %collective-permute-start.5) | collective-permute-done | bytes 65568 | tf_op jit(solution)/shard_map/ppermute | solution.py:35
  12.0 0.2 %join.1 = (f32[32,8,128]{2,1,0:T(8,128)S(1)}, f32[5,8,128]{2,1,0:T(8,128)S(1)}, f32[19,8,128]{2,1,0:T(8,128)S(1)}) custom-call(f32[64,8,128]{2,1,0:T(8,128)S(1)} %get-tuple-element.21.pt_ref, f32[16,8,128]{2,1,0:T(8,128)S(1)} %add.9.mine_ref.sum_ref, f32[16,8,128]{2,1,0:T(8,128)S(1)} %collective-permute-done.5.theirs_ref, ...), custom_call_target="tpu_custom_call" | custom-call | tf_op jit(solution)/shard_map/join/pallas_call | solution.py:633
  12.2 1.7 %collective-permute-start.8 = (f32[19,8,128]{2,1,0:T(8,128)S(1)}, f32[19,8,128]{2,1,0:T(8,128)S(1)}, u32[]{:S(2)}, u32[]{:S(2)}) collective-permute-start(f32[19,8,128]{2,1,0:T(8,128)S(1)} %get-tuple-element.36), channel_id=1, source_target_pairs={{0,2},{1,3},{2,4},{3,5},{4,6},{5,7},{6,14},{7,15},{8,0},{9,1},{10,... | collective-permute-start | bytes 233480 | tf_op jit(solution)/shard_map/ppermute | solution.py:35
  13.9 0.0 collective-permute-done.6
  13.9 0.1 collective-permute-start.7
  14.0 1.2 %collective-permute-done.7.other_ref = f32[16,8,128]{2,1,0:T(8,128)S(1)} collective-permute-done((f32[16,8,128]{2,1,0:T(8,128)S(1)}, f32[16,8,128]{2,1,0:T(8,128)S(1)}, u32[]{:S(2)}, u32[]{:S(2)}) %collective-permute-start.7) | collective-permute-done | bytes 65568 | tf_op jit(solution)/shard_map/ppermute | solution.py:35
  15.2 1.2 %middle.1 = (f32[5,8,128]{2,1,0:T(8,128)S(1)}, f32[48,8,128]{2,1,0:T(8,128)S(1)}, f32[32,8,128]{2,1,0:T(8,128)S(1)}) custom-call(f32[64,8,128]{2,1,0:T(8,128)S(1)} %get-tuple-element.21.pt_ref, f32[32,8,128]{2,1,0:T(8,128)S(1)} %get-tuple-element.30.outer_ref, f32[16,8,128]{2,1,0:T(8,128)S(1)} %slice_add_fusion.mine_ref, ...), custom_call_target="tpu_custom_call" | custom-call | flops 7864320 | bytes 1048576 | tf_op jit(solution)/shard_map/middle/pallas_call | solution.py:643
  16.5 0.0 collective-permute-done.9.second_ref
  16.5 0.0 collective-permute-done.8.first_ref
  16.5 1.5 %outer.1 = f32[32,16,128]{2,1,0:T(8,128)} custom-call(f32[32,8,128]{2,1,0:T(8,128)S(1)} %get-tuple-element.30.outer_ref, f32[5,8,128]{2,1,0:T(8,128)S(1)} %get-tuple-element.33.strip_ref, f32[48,8,128]{2,1,0:T(8,128)S(1)} %get-tuple-element.34.saved_ref, f32[32,8,128]{2,1,0:T(8,128)S(1)} %get-tuple-element.35.done_ref, ...), custom_call_target="tpu_custom_call" | custom-call | tf_op jit(solution)/shard_map/outer/pallas_call | solution.py:659
  (4 shorter events, 0.0 us)
Async XLA Ops:
  1.5 4.6 %collective-permute-start = (f32[32,8,128]{2,1,0:T(8,128)S(1)}, f32[32,8,128]{2,1,0:T(8,128)S(1)}, u32[]{:S(2)}, u32[]{:S(2)}) collective-permute-start(f32[32,8,128]{2,1,0:T(8,128)S(1)} %get-tuple-element.23), channel_id=1, source_target_pairs={{0,8},{1,9},{2,10},{3,11},{4,12},{5,13},{6,14},{7,15},{8,0},{9,1},... | collective-permute-start | bytes 393224 | tf_op jit(solution)/shard_map/ppermute | solution.py:35
  2.0 7.2 %collective-permute-start.2 = (f32[5,8,128]{2,1,0:T(8,128)S(1)}, f32[5,8,128]{2,1,0:T(8,128)S(1)}, u32[]{:S(2)}, u32[]{:S(2)}) collective-permute-start(f32[5,8,128]{2,1,0:T(8,128)S(1)} %get-tuple-element.25.side_ref), channel_id=1, source_target_pairs={{0,1},{1,0},{2,3},{3,2},{4,5},{5,4},{6,7},{7,6},{8,9},{9,8},{10,11... | collective-permute-start | bytes 61448 | tf_op jit(solution)/shard_map/ppermute | solution.py:35
  4.5 4.7 %collective-permute-start.3 = (f32[2,8,128]{2,1,0:T(8,128)S(1)}, f32[2,8,128]{2,1,0:T(8,128)S(1)}, u32[]{:S(2)}, u32[]{:S(2)}) collective-permute-start(f32[2,8,128]{2,1,0:T(8,128)S(1)} %get-tuple-element.26), channel_id=1, source_target_pairs={{0,17},{1,16},{2,19},{3,18},{4,21},{5,20},{6,23},{7,22},{8,25},{9,... | collective-permute-start | bytes 24584 | tf_op jit(solution)/shard_map/ppermute | solution.py:35
  6.1 4.6 %collective-permute-start.1 = (f32[16,8,128]{2,1,0:T(8,128)S(1)}, f32[16,8,128]{2,1,0:T(8,128)S(1)}, u32[]{:S(2)}, u32[]{:S(2)}) collective-permute-start(f32[16,8,128]{2,1,0:T(8,128)S(1)} %get-tuple-element.24), channel_id=1, source_target_pairs={{0,16},{1,17},{2,18},{3,19},{4,20},{5,21},{6,22},{7,23},{8,24},{9,... | collective-permute-start | bytes 196616 | tf_op jit(solution)/shard_map/ppermute | solution.py:35
  9.2 1.5 %collective-permute-start.4 = (f32[2,8,128]{2,1,0:T(8,128)S(1)}, f32[2,8,128]{2,1,0:T(8,128)S(1)}, u32[]{:S(2)}, u32[]{:S(2)}) collective-permute-start(f32[2,8,128]{2,1,0:T(8,128)S(1)} %slice_add_fusion.1.edge_ref), channel_id=1, source_target_pairs={{0,8},{1,9},{2,10},{3,11},{4,12},{5,13},{6,14},{7,15},{8,0},{9,1},... | collective-permute-start | bytes 24584 | tf_op jit(solution)/shard_map/ppermute | solution.py:35
  9.2 4.7 %collective-permute-start.6 = (f32[17,8,128]{2,1,0:T(8,128)S(1)}, f32[17,8,128]{2,1,0:T(8,128)S(1)}, u32[]{:S(2)}, u32[]{:S(2)}) collective-permute-start(f32[17,8,128]{2,1,0:T(8,128)S(1)} %get-tuple-element.31), channel_id=1, source_target_pairs={{0,16},{1,17},{2,18},{3,19},{4,20},{5,21},{6,22},{7,23},{8,24},{9,... | collective-permute-start | bytes 208904 | tf_op jit(solution)/shard_map/ppermute | solution.py:35
  10.7 1.3 %collective-permute-start.5 = (f32[16,8,128]{2,1,0:T(8,128)S(1)}, f32[16,8,128]{2,1,0:T(8,128)S(1)}, u32[]{:S(2)}, u32[]{:S(2)}) collective-permute-start(f32[16,8,128]{2,1,0:T(8,128)S(1)} %add.9.mine_ref.sum_ref), channel_id=1, source_target_pairs={{0,8},{1,9},{2,10},{3,11},{4,12},{5,13},{6,14},{7,15},{8,0},{9,1},... | collective-permute-start | bytes 196616 | tf_op jit(solution)/shard_map/ppermute | solution.py:35
  11.1 5.4 %collective-permute-start.9 = (f32[19,8,128]{2,1,0:T(8,128)S(1)}, f32[19,8,128]{2,1,0:T(8,128)S(1)}, u32[]{:S(2)}, u32[]{:S(2)}) collective-permute-start(f32[19,8,128]{2,1,0:T(8,128)S(1)} %near.1), channel_id=1, source_target_pairs={{0,8},{1,9},{2,0},{3,1},{4,2},{5,3},{6,4},{7,5},{8,10},{9,11},{10,... | collective-permute-start | bytes 233480 | tf_op jit(solution)/shard_map/ppermute | solution.py:35
  12.2 4.3 %collective-permute-start.8 = (f32[19,8,128]{2,1,0:T(8,128)S(1)}, f32[19,8,128]{2,1,0:T(8,128)S(1)}, u32[]{:S(2)}, u32[]{:S(2)}) collective-permute-start(f32[19,8,128]{2,1,0:T(8,128)S(1)} %get-tuple-element.36), channel_id=1, source_target_pairs={{0,2},{1,3},{2,4},{3,5},{4,6},{5,7},{6,14},{7,15},{8,0},{9,1},{10,... | collective-permute-start | bytes 233480 | tf_op jit(solution)/shard_map/ppermute | solution.py:35
  13.9 1.3 %collective-permute-start.7 = (f32[16,8,128]{2,1,0:T(8,128)S(1)}, f32[16,8,128]{2,1,0:T(8,128)S(1)}, u32[]{:S(2)}, u32[]{:S(2)}) collective-permute-start(f32[16,8,128]{2,1,0:T(8,128)S(1)} %slice_add_fusion.mine_ref), channel_id=1, source_target_pairs={{0,8},{1,9},{2,10},{3,11},{4,12},{5,13},{6,14},{7,15},{8,0},{9,1},... | collective-permute-start | bytes 196616 | tf_op jit(solution)/shard_map/ppermute | solution.py:35

commit v9 on v7

--- a/solution.py
+++ b/solution.py
@@ -608,14 +608,14 @@
     cut = STEPS * fields
     outer, inner = pl.pallas_call(
         pair_kernel,
-        out_shape=(tiles(cut), tiles(half * fields - cut + 1)),
+        out_shape=(tiles(cut), tiles(half * fields - cut + 2)),
         in_specs=[VMEM] * 2,
         out_specs=(VMEM,) * 2,
         compiler_params=MODEST,
         name="pair",
     )(keep, given)
     outer = over_chips(outer)
-    inner = over_chips(inner)[1:]
+    inner = over_chips(inner)[2:]
 
     other_edges = over_members(edges, 1)
     outer, other_edges = lax.optimization_barrier((outer, other_edges))

time: 18.2 us -> 18.2 us (level)
  no operation moved by 1% of the time
where the time goes in v9:
time: 18.2 us; the launch traced here: 18 us
  starting transfers between devices  8.51 us (47%)
  waiting for transfers between devices  4.86 us (27%)
  Pallas kernels  4.57 us (25%)
    ppermute x10, starting transfers between devices, send(): return lax.ppermute(value, AXES, pairs)  8.51 us
    ppermute x10, waiting for transfers between devices, send(): return lax.ppermute(value, AXES, pairs)  4.86 us
    pallas_call x1, Pallas kernels, on_device(): pl.pallas_call(functools.partial(outer_kernel, sizes), out_shape=jax.Shap...  1.52 us
    pallas_call x1, Pallas kernels, on_device(): pl.pallas_call(functools.partial(split_kernel, sizes), out_shape=(tiles(r...  1.44 us
    pallas_call x1, Pallas kernels, on_device(): pl.pallas_call(functools.partial(middle_kernel, sizes), out_shape=(tiles(...  1.24 us
  transfers between devices with their start and end apart: 10, of which 3 were waited for; matrix products, arithmetic and copies ran while one was open for 0% of the time, Pallas kernels for 9%

profile of v9, /device:TPU:0, one launch (start us, length us, event | category | flops | bytes accessed | tf_op | source)
XLA Modules:
  0.0 18.0 jit_solution(15116351413288695396)
XLA Ops:
  0.0 1.4 %split.1 = (f32[64,8,128]{2,1,0:T(8,128)S(1)}, f32[32,8,128]{2,1,0:T(8,128)S(1)}, f32[32,8,128]{2,1,0:T(8,128)S(1)}, f32[2,8,128]{2,1,0:T(8,128)S(1)}, f32[5,8,128]{2,1,0:T(8,128)S(1)}, /*index=5*/f32[32,128]{1,0:T(8,128)S(1)}) custom-call(f32[4,128,128]{2,1,0:T(8,128)} %bitcast.3, f32[4,128,128]{2,1,0:T(8,128)} %bitcast.4, s32[4]{0:T(128)} %owner_hbm.1, ...), custom_call_target="tpu_custom_call" | custom-call | tf_op jit(solution)/shard_map/split/pallas_call | solution.py:555
  1.5 0.5 %collective-permute-start = (f32[32,8,128]{2,1,0:T(8,128)S(1)}, f32[32,8,128]{2,1,0:T(8,128)S(1)}, u32[]{:S(2)}, u32[]{:S(2)}) collective-permute-start(f32[32,8,128]{2,1,0:T(8,128)S(1)} %get-tuple-element.24), channel_id=1, source_target_pairs={{0,8},{1,9},{2,10},{3,11},{4,12},{5,13},{6,14},{7,15},{8,0},{9,1},... | collective-permute-start | bytes 393224 | tf_op jit(solution)/shard_map/ppermute | solution.py:35
  2.0 2.6 %collective-permute-start.2 = (f32[5,8,128]{2,1,0:T(8,128)S(1)}, f32[5,8,128]{2,1,0:T(8,128)S(1)}, u32[]{:S(2)}, u32[]{:S(2)}) collective-permute-start(f32[5,8,128]{2,1,0:T(8,128)S(1)} %get-tuple-element.26.side_ref), channel_id=1, source_target_pairs={{0,1},{1,0},{2,3},{3,2},{4,5},{5,4},{6,7},{7,6},{8,9},{9,8},{10,11... | collective-permute-start | bytes 61448 | tf_op jit(solution)/shard_map/ppermute | solution.py:35
  4.5 1.5 %collective-permute-start.3 = (f32[2,8,128]{2,1,0:T(8,128)S(1)}, f32[2,8,128]{2,1,0:T(8,128)S(1)}, u32[]{:S(2)}, u32[]{:S(2)}) collective-permute-start(f32[2,8,128]{2,1,0:T(8,128)S(1)} %get-tuple-element.27), channel_id=1, source_target_pairs={{0,17},{1,16},{2,19},{3,18},{4,21},{5,20},{6,23},{7,22},{8,25},{9,... | collective-permute-start | bytes 24584 | tf_op jit(solution)/shard_map/ppermute | solution.py:35
  6.0 0.0 collective-permute-done.given_ref
  6.1 0.1 collective-permute-start.1
  6.2 3.0 %collective-permute-done.3 = f32[2,8,128]{2,1,0:T(8,128)S(1)} collective-permute-done((f32[2,8,128]{2,1,0:T(8,128)S(1)}, f32[2,8,128]{2,1,0:T(8,128)S(1)}, u32[]{:S(2)}, u32[]{:S(2)}) %collective-permute-start.3) | collective-permute-done | bytes 8224 | tf_op jit(solution)/shard_map/ppermute | solution.py:35
  9.2 0.0 collective-permute-done.2.refs_0_
  9.2 0.0 collective-permute-start.4
  9.2 1.5 %collective-permute-start.6 = (f32[18,8,128]{2,1,0:T(8,128)S(1)}, f32[18,8,128]{2,1,0:T(8,128)S(1)}, u32[]{:S(2)}, u32[]{:S(2)}) collective-permute-start(f32[18,8,128]{2,1,0:T(8,128)S(1)} %get-tuple-element.32), channel_id=1, source_target_pairs={{0,16},{1,17},{2,18},{3,19},{4,20},{5,21},{6,22},{7,23},{8,24},{9,... | collective-permute-start | bytes 221192 | tf_op jit(solution)/shard_map/ppermute | solution.py:35
  10.7 0.0 collective-permute-done.1
  10.7 0.0 collective-permute-done.4.other_ref
  10.7 0.2 %collective-permute-start.5 = (f32[16,8,128]{2,1,0:T(8,128)S(1)}, f32[16,8,128]{2,1,0:T(8,128)S(1)}, u32[]{:S(2)}, u32[]{:S(2)}) collective-permute-start(f32[16,8,128]{2,1,0:T(8,128)S(1)} %add.9.mine_ref.sum_ref), channel_id=1, source_target_pairs={{0,8},{1,9},{2,10},{3,11},{4,12},{5,13},{6,14},{7,15},{8,0},{9,1},... | collective-permute-start | bytes 196616 | tf_op jit(solution)/shard_map/ppermute | solution.py:35
  10.9 0.2 near.1
  11.1 0.4 %collective-permute-start.9 = (f32[19,8,128]{2,1,0:T(8,128)S(1)}, f32[19,8,128]{2,1,0:T(8,128)S(1)}, u32[]{:S(2)}, u32[]{:S(2)}) collective-permute-start(f32[19,8,128]{2,1,0:T(8,128)S(1)} %near.1), channel_id=1, source_target_pairs={{0,8},{1,9},{2,0},{3,1},{4,2},{5,3},{6,4},{7,5},{8,10},{9,11},{10,... | collective-permute-start | bytes 233480 | tf_op jit(solution)/shard_map/ppermute | solution.py:35
  11.5 0.6 %collective-permute-done.5.theirs_ref = f32[16,8,128]{2,1,0:T(8,128)S(1)} collective-permute-done((f32[16,8,128]{2,1,0:T(8,128)S(1)}, f32[16,8,128]{2,1,0:T(8,128)S(1)}, u32[]{:S(2)}, u32[]{:S(2)}) %collective-permute-start.5) | collective-permute-done | bytes 65568 | tf_op jit(solution)/shard_map/ppermute | solution.py:35
  12.0 0.2 %join.1 = (f32[32,8,128]{2,1,0:T(8,128)S(1)}, f32[5,8,128]{2,1,0:T(8,128)S(1)}, f32[19,8,128]{2,1,0:T(8,128)S(1)}) custom-call(f32[64,8,128]{2,1,0:T(8,128)S(1)} %get-tuple-element.22.pt_ref, f32[16,8,128]{2,1,0:T(8,128)S(1)} %add.9.mine_ref.sum_ref, f32[16,8,128]{2,1,0:T(8,128)S(1)} %collective-permute-done.5.theirs_ref, ...), custom_call_target="tpu_custom_call" | custom-call | tf_op jit(solution)/shard_map/join/pallas_call | solution.py:633
  12.2 1.7 %collective-permute-start.8 = (f32[19,8,128]{2,1,0:T(8,128)S(1)}, f32[19,8,128]{2,1,0:T(8,128)S(1)}, u32[]{:S(2)}, u32[]{:S(2)}) collective-permute-start(f32[19,8,128]{2,1,0:T(8,128)S(1)} %get-tuple-element.33), channel_id=1, source_target_pairs={{0,2},{1,3},{2,4},{3,5},{4,6},{5,7},{6,14},{7,15},{8,0},{9,1},{10,... | collective-permute-start | bytes 233480 | tf_op jit(solution)/shard_map/ppermute | solution.py:35
  13.9 0.0 collective-permute-done.6
  13.9 0.1 collective-permute-start.7
  14.0 1.2 %collective-permute-done.7.other_ref = f32[16,8,128]{2,1,0:T(8,128)S(1)} collective-permute-done((f32[16,8,128]{2,1,0:T(8,128)S(1)}, f32[16,8,128]{2,1,0:T(8,128)S(1)}, u32[]{:S(2)}, u32[]{:S(2)}) %collective-permute-start.7) | collective-permute-done | bytes 65568 | tf_op jit(solution)/shard_map/ppermute | solution.py:35
  15.2 1.2 %middle.1 = (f32[5,8,128]{2,1,0:T(8,128)S(1)}, f32[48,8,128]{2,1,0:T(8,128)S(1)}, f32[32,8,128]{2,1,0:T(8,128)S(1)}) custom-call(f32[64,8,128]{2,1,0:T(8,128)S(1)} %get-tuple-element.22.pt_ref, f32[32,8,128]{2,1,0:T(8,128)S(1)} %get-tuple-element.31.outer_ref, f32[16,8,128]{2,1,0:T(8,128)S(1)} %slice_add_fusion.mine_ref, ...), custom_call_target="tpu_custom_call" | custom-call | flops 7864320 | bytes 1048576 | tf_op jit(solution)/shard_map/middle/pallas_call | solution.py:644
  16.5 0.0 collective-permute-done.9.second_ref
  16.5 0.0 collective-permute-done.8.first_ref
  16.5 1.5 %outer.1 = f32[32,16,128]{2,1,0:T(8,128)} custom-call(f32[32,8,128]{2,1,0:T(8,128)S(1)} %get-tuple-element.31.outer_ref, f32[5,8,128]{2,1,0:T(8,128)S(1)} %get-tuple-element.36.strip_ref, f32[48,8,128]{2,1,0:T(8,128)S(1)} %get-tuple-element.37.saved_ref, f32[32,8,128]{2,1,0:T(8,128)S(1)} %get-tuple-element.38.done_ref, ...), custom_call_target="tpu_custom_call" | custom-call | tf_op jit(solution)/shard_map/outer/pallas_call | solution.py:660
  (4 shorter events, 0.0 us)
Async XLA Ops:
  1.5 4.6 %collective-permute-start = (f32[32,8,128]{2,1,0:T(8,128)S(1)}, f32[32,8,128]{2,1,0:T(8,128)S(1)}, u32[]{:S(2)}, u32[]{:S(2)}) collective-permute-start(f32[32,8,128]{2,1,0:T(8,128)S(1)} %get-tuple-element.24), channel_id=1, source_target_pairs={{0,8},{1,9},{2,10},{3,11},{4,12},{5,13},{6,14},{7,15},{8,0},{9,1},... | collective-permute-start | bytes 393224 | tf_op jit(solution)/shard_map/ppermute | solution.py:35
  2.0 7.2 %collective-permute-start.2 = (f32[5,8,128]{2,1,0:T(8,128)S(1)}, f32[5,8,128]{2,1,0:T(8,128)S(1)}, u32[]{:S(2)}, u32[]{:S(2)}) collective-permute-start(f32[5,8,128]{2,1,0:T(8,128)S(1)} %get-tuple-element.26.side_ref), channel_id=1, source_target_pairs={{0,1},{1,0},{2,3},{3,2},{4,5},{5,4},{6,7},{7,6},{8,9},{9,8},{10,11... | collective-permute-start | bytes 61448 | tf_op jit(solution)/shard_map/ppermute | solution.py:35
  4.5 4.7 %collective-permute-start.3 = (f32[2,8,128]{2,1,0:T(8,128)S(1)}, f32[2,8,128]{2,1,0:T(8,128)S(1)}, u32[]{:S(2)}, u32[]{:S(2)}) collective-permute-start(f32[2,8,128]{2,1,0:T(8,128)S(1)} %get-tuple-element.27), channel_id=1, source_target_pairs={{0,17},{1,16},{2,19},{3,18},{4,21},{5,20},{6,23},{7,22},{8,25},{9,... | collective-permute-start | bytes 24584 | tf_op jit(solution)/shard_map/ppermute | solution.py:35
  6.1 4.6 %collective-permute-start.1 = (f32[16,8,128]{2,1,0:T(8,128)S(1)}, f32[16,8,128]{2,1,0:T(8,128)S(1)}, u32[]{:S(2)}, u32[]{:S(2)}) collective-permute-start(f32[16,8,128]{2,1,0:T(8,128)S(1)} %get-tuple-element.25), channel_id=1, source_target_pairs={{0,16},{1,17},{2,18},{3,19},{4,20},{5,21},{6,22},{7,23},{8,24},{9,... | collective-permute-start | bytes 196616 | tf_op jit(solution)/shard_map/ppermute | solution.py:35
  9.2 1.5 %collective-permute-start.4 = (f32[2,8,128]{2,1,0:T(8,128)S(1)}, f32[2,8,128]{2,1,0:T(8,128)S(1)}, u32[]{:S(2)}, u32[]{:S(2)}) collective-permute-start(f32[2,8,128]{2,1,0:T(8,128)S(1)} %slice_add_fusion.1.edge_ref), channel_id=1, source_target_pairs={{0,8},{1,9},{2,10},{3,11},{4,12},{5,13},{6,14},{7,15},{8,0},{9,1},... | collective-permute-start | bytes 24584 | tf_op jit(solution)/shard_map/ppermute | solution.py:35
  9.2 4.7 %collective-permute-start.6 = (f32[18,8,128]{2,1,0:T(8,128)S(1)}, f32[18,8,128]{2,1,0:T(8,128)S(1)}, u32[]{:S(2)}, u32[]{:S(2)}) collective-permute-start(f32[18,8,128]{2,1,0:T(8,128)S(1)} %get-tuple-element.32), channel_id=1, source_target_pairs={{0,16},{1,17},{2,18},{3,19},{4,20},{5,21},{6,22},{7,23},{8,24},{9,... | collective-permute-start | bytes 221192 | tf_op jit(solution)/shard_map/ppermute | solution.py:35
  10.7 1.3 %collective-permute-start.5 = (f32[16,8,128]{2,1,0:T(8,128)S(1)}, f32[16,8,128]{2,1,0:T(8,128)S(1)}, u32[]{:S(2)}, u32[]{:S(2)}) collective-permute-start(f32[16,8,128]{2,1,0:T(8,128)S(1)} %add.9.mine_ref.sum_ref), channel_id=1, source_target_pairs={{0,8},{1,9},{2,10},{3,11},{4,12},{5,13},{6,14},{7,15},{8,0},{9,1},... | collective-permute-start | bytes 196616 | tf_op jit(solution)/shard_map/ppermute | solution.py:35
  11.1 5.4 %collective-permute-start.9 = (f32[19,8,128]{2,1,0:T(8,128)S(1)}, f32[19,8,128]{2,1,0:T(8,128)S(1)}, u32[]{:S(2)}, u32[]{:S(2)}) collective-permute-start(f32[19,8,128]{2,1,0:T(8,128)S(1)} %near.1), channel_id=1, source_target_pairs={{0,8},{1,9},{2,0},{3,1},{4,2},{5,3},{6,4},{7,5},{8,10},{9,11},{10,... | collective-permute-start | bytes 233480 | tf_op jit(solution)/shard_map/ppermute | solution.py:35
  12.2 4.3 %collective-permute-start.8 = (f32[19,8,128]{2,1,0:T(8,128)S(1)}, f32[19,8,128]{2,1,0:T(8,128)S(1)}, u32[]{:S(2)}, u32[]{:S(2)}) collective-permute-start(f32[19,8,128]{2,1,0:T(8,128)S(1)} %get-tuple-element.33), channel_id=1, source_target_pairs={{0,2},{1,3},{2,4},{3,5},{4,6},{5,7},{6,14},{7,15},{8,0},{9,1},{10,... | collective-permute-start | bytes 233480 | tf_op jit(solution)/shard_map/ppermute | solution.py:35
  13.9 1.3 %collective-permute-start.7 = (f32[16,8,128]{2,1,0:T(8,128)S(1)}, f32[16,8,128]{2,1,0:T(8,128)S(1)}, u32[]{:S(2)}, u32[]{:S(2)}) collective-permute-start(f32[16,8,128]{2,1,0:T(8,128)S(1)} %slice_add_fusion.mine_ref), channel_id=1, source_target_pairs={{0,8},{1,9},{2,10},{3,11},{4,12},{5,13},{6,14},{7,15},{8,0},{9,1},... | collective-permute-start | bytes 196616 | tf_op jit(solution)/shard_map/ppermute | solution.py:35
